TPU v7x, 32 devices: a whole 2x2x4 slice. The times are simulated.
32 devices in a mesh: gx: 4 (over y, x), gy: 8 (over z, core).
Axes of the slice: x: 2, y: 2, z: 4, core: 2. Of those that a mesh axis runs over, the one named last changes fastest.
Arguments:
- velocity: float32 [3, 1536, 32, 512], P(None, 'gy', None, 'gx'), may hold values from -6 to 6
- old_advection: float32 [3, 1536, 32, 512], P(None, 'gy', None, 'gx'), may hold values from -12 to 12
- lower_gap: float32 [1536], P('gy'), may hold values from 0.35 to 1.4
- upper_gap: float32 [1536], P('gy'), may hold values from 0.35 to 1.4, as said below
Outputs:
- new_velocity: float32 [3, 1536, 32, 512], P(None, 'gy', None, 'gx')
- advection: float32 [3, 1536, 32, 512], P(None, 'gy', None, 'gx')
Inputs may be any that keep to these rules, and one draw needn't show every extreme that they name: upper_gap of every point equals lower_gap of the next point.
All inputs are finite; a program needn't handle non-finite values.
Results may differ from a plain program's by a relative error of at most 0.0075.
Values sent between devices are 32-bit elements; how exact they have to be, the bound alone decides.
No kernel may reach another device: no remote copies, remote signals or barrier semaphores. Data moves between devices by JAX's collectives and lax.ppermute only.
A program may use at most 256 MiB of HBM per device.

v0:
```python
import jax
import jax.numpy as jnp
from jax import lax
from jax.sharding import PartitionSpec as P

STIFF = 1024


STENCIL = (0.8, -0.2, 4.0 / 105.0, -1.0 / 280.0)
GAMMA = 5.0 / 12.0
ZETA = -17.0 / 60.0


def extended(array, sides, width, wrap):
    for axis, dim in sides:
        size, length = (lax.axis_size(axis), array.shape[dim])
        up = [(i, (i + 1) % size) for i in range(size if wrap else size - 1)]
        down = [(j, i) for i, j in up]
        last = lax.slice_in_dim(array, length - width, length, axis=dim)
        first = lax.slice_in_dim(array, 0, width, axis=dim)
        before = lax.ppermute(last, axis, up)
        after = lax.ppermute(first, axis, down)
        array = jnp.concatenate([before, array, after], axis=dim)
    return array


def prefix(value, axis, join, neutral, backward):
    count, mine = (lax.axis_size(axis), lax.axis_index(axis))
    pieces = jax.tree.map(lambda part: lax.all_gather(part, axis), value)
    if backward:
        pieces = jax.tree.map(lambda part: part[::-1], pieces)
        mine = count - 1 - mine
    total = jax.tree.map(
        lambda part, zero: jnp.full_like(part, 0) + jnp.asarray(zero, part.dtype), value, neutral
    )

    def turn(position, total):
        longer = join(total, jax.tree.map(lambda part: part[position], pieces))
        return jax.tree.map(lambda new, old: jnp.where(position < mine, new, old), longer, total)

    return lax.fori_loop(0, count - 1, turn, total)


def stream_slope(padded, planes):
    summed = STENCIL[0] * (padded[..., 5 : 5 + planes] - padded[..., 3 : 3 + planes])
    for offset in range(2, 5):
        summed = summed + STENCIL[offset - 1] * (
            padded[..., 4 + offset : 4 + offset + planes]
            - padded[..., 4 - offset : 4 - offset + planes]
        )
    return summed


def roll_slope(values, along_axis):
    summed = STENCIL[0] * (jnp.roll(values, -1, along_axis) - jnp.roll(values, 1, along_axis))
    for offset in range(2, 5):
        summed = summed + STENCIL[offset - 1] * (
            jnp.roll(values, -offset, along_axis) - jnp.roll(values, offset, along_axis)
        )
    return summed


def compose(earlier, latter):
    return (latter[0] * earlier[0], latter[1] + latter[0] * earlier[1])


def chain_ratio(earlier, latter):
    product = jnp.dot(latter, earlier, precision=lax.Precision.HIGHEST)
    return product / jnp.max(jnp.abs(product))


def ratio_matrix(cross_term, top_right, bottom_left):
    unit_entry = jnp.ones((), jnp.float32)
    return jnp.stack([jnp.stack([cross_term, top_right]), jnp.stack([bottom_left, unit_entry])])


def shards(velocity, old_advection, lower_gap, upper_gap):
    planes = velocity.shape[3]
    padded = extended(velocity, (("gx", 3),), 4, True)
    stream = stream_slope(padded, planes)
    spanwise = roll_slope(velocity, 2)
    rimmed = extended(velocity, (("gy", 1),), 1, False)
    gap_sum = lower_gap + upper_gap
    normal_slope = (rimmed[:, 2:] - rimmed[:, :-2]) / gap_sum[None, :, None, None]
    advection = -(
        velocity[0][None] * stream + velocity[1][None] * normal_slope + velocity[2][None] * spanwise
    )
    forcing = velocity + GAMMA * advection + ZETA * old_advection
    lower_coef = -2.0 * STIFF / (gap_sum * lower_gap)
    upper_coef = -2.0 * STIFF / (gap_sum * upper_gap)
    diagonal = 1.0 - lower_coef - upper_coef
    below_band = lower_coef.at[0].set(0.0)
    above_band = upper_coef.at[-1].set(0.0)
    rows_here = velocity.shape[1]
    line_values = forcing.reshape(3, rows_here, -1)
    solved = lax.linalg.tridiagonal_solve(
        jnp.stack([below_band] * 3),
        jnp.stack([diagonal] * 3),
        jnp.stack([above_band] * 3),
        line_values,
    )
    columns = jnp.zeros((rows_here, 2), jnp.float32)
    columns = columns.at[0, 0].set(lower_coef[0]).at[rows_here - 1, 1].set(upper_coef[-1])
    spikes = lax.linalg.tridiagonal_solve(below_band, diagonal, above_band, columns)
    left_spike = spikes[:, 0]
    right_spike = spikes[:, 1]
    left_first = left_spike[0]
    left_last = left_spike[-1]
    right_first = right_spike[0]
    right_last = right_spike[-1]
    cross_term = left_last * right_first - right_last * left_first
    unit_matrix = jnp.eye(2, dtype=jnp.float32)
    below_prefix = prefix(
        ratio_matrix(cross_term, right_last, -left_first), "gy", chain_ratio, unit_matrix, False
    )
    below_ratio = below_prefix[0, 1] / below_prefix[1, 1]
    first_solved = solved[:, 0]
    last_solved = solved[:, -1]
    lower_denom = 1.0 - left_first * below_ratio
    lower_step = (
        jnp.reshape(-left_last / lower_denom, (1, 1)),
        last_solved + left_last * below_ratio / lower_denom * first_solved,
    )
    identity_step = (jnp.ones((1, 1), jnp.float32), jnp.zeros_like(first_solved))
    below_offset = prefix(lower_step, "gy", compose, identity_step, False)[1]
    first_base = (first_solved - left_first * below_offset) / lower_denom
    first_slope = right_first / lower_denom
    upper_step = (jnp.reshape(-first_slope, (1, 1)), first_base)
    above_value = prefix(upper_step, "gy", compose, identity_step, True)[1]
    first_value = first_base - first_slope * above_value
    below_value = below_offset - below_ratio * first_value
    finished = (
        solved
        - below_value[:, None, :] * left_spike[None, :, None]
        - above_value[:, None, :] * right_spike[None, :, None]
    )
    return (finished.reshape(velocity.shape), advection)


def solution(mesh):
    return jax.shard_map(
        shards,
        mesh=mesh,
        in_specs=(P(None, "gy", None, "gx"), P(None, "gy", None, "gx"), P("gy"), P("gy")),
        out_specs=(P(None, "gy", None, "gx"), P(None, "gy", None, "gx")),
        check_vma=False,
    )
```

profile of v0, /device:TPU:0, one launch (start us, length us, event | category | flops | bytes accessed | tf_op | source)
XLA Modules:
  0.0 1670.3 jit_solution(17184400324549401815)
XLA Ops:
  0.6 12.3 fusion.902
  12.9 7.0 copy.667
  19.9 3.9 collective-permute-start
  23.8 7.0 copy.668
  32.9 3.4 collective-permute-start.3
  36.4 7.5 slice_bitcast_fusion.3
  43.9 7.7 fusion.904
  51.6 7.6 fusion.906
  59.2 7.6 fusion.908
  66.9 8.0 fusion.910
  91.3 634.3 %while.111 = (s32[]{:T(128)}, f32[]{:T(128)}, f32[2]{0:T(128)}, f32[5,32]{1,0:T(8,128)}, f32[5,32,2]{1,0,2:T(8,128)S(1)}, /*index=5*/f32[5,32]{1,0:T(8,128)}, f3...) while((s32[]{:T(128)}, f32[]{:T(128)}, f32[2]{0:T(128)}, ...), condition=%wide.region_5.6_spmd, body=%wide.region_4.5_spmd.sunk | while | flops 321 | bytes 6401 | solution.py:104
  156.7 21.2 %fusion.957 = (f32[2]{0:T(128)}, f32[2]{0:T(128)}, f32[2]{0:T(128)}, f32[2]{0:T(128)}, f32[2]{0:T(128)}, /*index=5*/f32[2]{0:T(128)}, f32[2]{0:T(128)}, f32[2]{0...) fusion(f32[5,32,2]{2,1,0:T(8,128)S(1)} %get-tuple-element.3039,, ...), kind=kLoop, calls=%fused_computation.618.clone.1 | loop fusion | flops 192 | bytes 904 | tf_op jit(solution)/shard_map/while/body/eval_jaxpr/div | solution.py:104
  283.6 21.2 %fusion.957 = (f32[2]{0:T(128)}, f32[2]{0:T(128)}, f32[2]{0:T(128)}, f32[2]{0:T(128)}, f32[2]{0:T(128)}, /*index=5*/f32[2]{0:T(128)}, f32[2]{0:T(128)}, f32[2]{0...) fusion(f32[5,32,2]{2,1,0:T(8,128)S(1)} %get-tuple-element.3039,, ...), kind=kLoop, calls=%fused_computation.618.clone.1 | loop fusion | flops 192 | bytes 904 | tf_op jit(solution)/shard_map/while/body/eval_jaxpr/div | solution.py:104
  410.4 21.2 %fusion.957 = (f32[2]{0:T(128)}, f32[2]{0:T(128)}, f32[2]{0:T(128)}, f32[2]{0:T(128)}, f32[2]{0:T(128)}, /*index=5*/f32[2]{0:T(128)}, f32[2]{0:T(128)}, f32[2]{0...) fusion(f32[5,32,2]{2,1,0:T(8,128)S(1)} %get-tuple-element.3039,, ...), kind=kLoop, calls=%fused_computation.618.clone.1 | loop fusion | flops 192 | bytes 904 | tf_op jit(solution)/shard_map/while/body/eval_jaxpr/div | solution.py:104
  537.3 21.2 %fusion.957 = (f32[2]{0:T(128)}, f32[2]{0:T(128)}, f32[2]{0:T(128)}, f32[2]{0:T(128)}, f32[2]{0:T(128)}, /*index=5*/f32[2]{0:T(128)}, f32[2]{0:T(128)}, f32[2]{0...) fusion(f32[5,32,2]{2,1,0:T(8,128)S(1)} %get-tuple-element.3039,, ...), kind=kLoop, calls=%fused_computation.618.clone.1 | loop fusion | flops 192 | bytes 904 | tf_op jit(solution)/shard_map/while/body/eval_jaxpr/div | solution.py:104
  664.1 21.2 %fusion.957 = (f32[2]{0:T(128)}, f32[2]{0:T(128)}, f32[2]{0:T(128)}, f32[2]{0:T(128)}, f32[2]{0:T(128)}, /*index=5*/f32[2]{0:T(128)}, f32[2]{0:T(128)}, f32[2]{0...) fusion(f32[5,32,2]{2,1,0:T(8,128)S(1)} %get-tuple-element.3039,, ...), kind=kLoop, calls=%fused_computation.618.clone.1 | loop fusion | flops 192 | bytes 904 | tf_op jit(solution)/shard_map/while/body/eval_jaxpr/div | solution.py:104
  787.5 20.3 %fusion.643 = (f32[2]{0:T(128)}, f32[2]{0:T(128)S(1)}, f32[2]{0:T(128)S(1)}, f32[2]{0:T(128)S(1)}, f32[2]{0:T(128)S(1)}, /*index=5*/f32[2]{0:T(128)S(1)}, f32[2]...) fusion(f32[192,2]{1,0:T(8,128)S(1)} %scatter.9, ...), kind=kLoop, calls=%fused_computation.1266 | loop fusion | flops 186 | bytes 752 | tf_op jit(solution)/shard_map/eval_jaxpr/div | solution.py:104
  817.5 172.5 %while.112 = (s32[]{:T(128)}, f32[2]{0:T(128)}, f32[5,32,2]{1,0,2:T(8,128)S(1)}, f32[5,32,2]{2,1,0:T(8,128)S(1)}, f32[5,32]{1,0:T(8,128)}, /*index=5*/s32[]{:T(1...) while((s32[]{:T(128)}, f32[2]{0:T(128)}, ...), condition=%wide.region_7.8_spmd, body=%wide.region_6.7_spmd.sunk | while | flops 162 | bytes 3565 | solution.py:104
  820.3 20.8 %fusion.960 = (f32[2]{0:T(128)}, f32[2]{0:T(128)S(1)}, f32[2]{0:T(128)S(1)}, f32[2]{0:T(128)S(1)}, f32[2]{0:T(128)S(1)}, /*index=5*/f32[2]{0:T(128)S(1)}, f32[2]...) fusion(f32[5,32,2]{2,1,0:T(8,128)S(1)} %get-tuple-element.3154,, ...), kind=kLoop, calls=%fused_computation.745.clone.1 | loop fusion | flops 128 | bytes 776 | tf_op jit(solution)/shard_map/while/body/eval_jaxpr/sub | solution.py:104
  854.8 20.8 %fusion.960 = (f32[2]{0:T(128)}, f32[2]{0:T(128)S(1)}, f32[2]{0:T(128)S(1)}, f32[2]{0:T(128)S(1)}, f32[2]{0:T(128)S(1)}, /*index=5*/f32[2]{0:T(128)S(1)}, f32[2]...) fusion(f32[5,32,2]{2,1,0:T(8,128)S(1)} %get-tuple-element.3154,, ...), kind=kLoop, calls=%fused_computation.745.clone.1 | loop fusion | flops 128 | bytes 776 | tf_op jit(solution)/shard_map/while/body/eval_jaxpr/sub | solution.py:104
  889.3 20.8 %fusion.960 = (f32[2]{0:T(128)}, f32[2]{0:T(128)S(1)}, f32[2]{0:T(128)S(1)}, f32[2]{0:T(128)S(1)}, f32[2]{0:T(128)S(1)}, /*index=5*/f32[2]{0:T(128)S(1)}, f32[2]...) fusion(f32[5,32,2]{2,1,0:T(8,128)S(1)} %get-tuple-element.3154,, ...), kind=kLoop, calls=%fused_computation.745.clone.1 | loop fusion | flops 128 | bytes 776 | tf_op jit(solution)/shard_map/while/body/eval_jaxpr/sub | solution.py:104
  923.8 20.8 %fusion.960 = (f32[2]{0:T(128)}, f32[2]{0:T(128)S(1)}, f32[2]{0:T(128)S(1)}, f32[2]{0:T(128)S(1)}, f32[2]{0:T(128)S(1)}, /*index=5*/f32[2]{0:T(128)S(1)}, f32[2]...) fusion(f32[5,32,2]{2,1,0:T(8,128)S(1)} %get-tuple-element.3154,, ...), kind=kLoop, calls=%fused_computation.745.clone.1 | loop fusion | flops 128 | bytes 776 | tf_op jit(solution)/shard_map/while/body/eval_jaxpr/sub | solution.py:104
  958.3 20.8 %fusion.960 = (f32[2]{0:T(128)}, f32[2]{0:T(128)S(1)}, f32[2]{0:T(128)S(1)}, f32[2]{0:T(128)S(1)}, f32[2]{0:T(128)S(1)}, /*index=5*/f32[2]{0:T(128)S(1)}, f32[2]...) fusion(f32[5,32,2]{2,1,0:T(8,128)S(1)} %get-tuple-element.3154,, ...), kind=kLoop, calls=%fused_computation.745.clone.1 | loop fusion | flops 128 | bytes 776 | tf_op jit(solution)/shard_map/while/body/eval_jaxpr/sub | solution.py:104
  990.0 2.7 fusion.645
  992.7 2.6 fusion.646
  997.8 2.6 fusion.648
  1000.5 2.6 fusion.649
  1010.8 2.6 fusion.653
  1018.4 2.6 fusion.656
  1021.0 2.6 fusion.657
  1023.6 2.6 fusion.658
  1034.7 12.0 all-gather.3
  1046.7 9.9 while.113
  1066.0 14.8 all-reduce.3
  1081.6 6.4 copy.521
  1088.1 6.4 copy.523
  1094.5 92.0 %multiply_add_fusion = (f32[3,192,32,128]{3,2,1,0:T(8,128)}, f32[3,192,32,128]{3,2,1,0:T(8,128)}) fusion(f32[3,192,32,128]{3,2,1,0:T(8,128)} %param.27, f32[3,192,32,128]{3,2,1,0:T(8,128)} %param.26, f32[3,192,28,128]{3,2,1,0:T(8,128)} %get-tuple-element.1500, f32[3,192,4,128]{3,2,1,0:T(4,128)} %get-tuple-element.1502, ...), kind=kLoop, calls=%fused_computation.873 | loop fusion | flops 122683392 | bytes 123372288 | tf_op jit(solution)/shard_map/add | solution.py:88
  1186.5 11.2 reshape.1250
  1199.4 4.7 slice_bitcast_fusion
  1204.1 3.7 slice.4456
  1210.3 6.5 broadcast.535.clone
  1216.8 89.8 %while.109 = (s32[]{:T(128)}, f32[3]{0:T(128)S(1)}, f32[3,4096]{1,0:T(4,128)S(1)}, f32[5,32,3]{1,0,2:T(8,128)S(1)}, f32[5,32,3,4096]{3,2,1,0:T(4,128)}, /*index=...) while((s32[]{:T(128)}, f32[3]{0:T(128)S(1)}, ...), condition=%wide.region_1.2_spmd, body=%wide.region_0.1_spmd.sunk | while | flops 1769793 | bytes 14488629 | solution.py:96
  1217.6 4.9 constant_dynamic-slice_fusion.238
  1224.4 4.0 constant_dynamic-slice_fusion.237
  1235.6 4.9 constant_dynamic-slice_fusion.238
  1242.4 3.8 constant_dynamic-slice_fusion.237
  1253.4 4.8 constant_dynamic-slice_fusion.238
  1260.0 4.2 constant_dynamic-slice_fusion.237
  1271.3 4.9 constant_dynamic-slice_fusion.238
  1278.0 3.9 constant_dynamic-slice_fusion.237
  1289.2 5.2 constant_dynamic-slice_fusion.238
  1296.3 3.9 constant_dynamic-slice_fusion.237
  1307.5 57.7 %multiply_subtract_fusion.30 = (f32[3]{0:T(128)S(1)}, f32[3]{0:T(128)S(1)}, f32[3]{0:T(128)S(1)}, f32[3]{0:T(128)S(1)}, f32[3]{0:T(128)S(1)}, /*index=5*/f32[3]{...) fusion(f32[]{:T(128)} %bitcast.623, ...), kind=kLoop, calls=%fused_computation.1300 | loop fusion | flops 276 | bytes 1112 | tf_op jit(solution)/shard_map/vmap()/eval_jaxpr/sub | solution.py:96
  1368.5 12.2 constant_dynamic-update-slice_fusion.95
  1430.3 12.1 slice.4550
  1443.7 6.6 broadcast.535
  1450.2 97.5 %while.110 = (s32[]{:T(128)}, f32[3,4096]{1,0:T(4,128)S(1)}, f32[5,32,3,4096]{3,2,1,0:T(4,128)}, f32[5,32,3,4096]{3,2,1,0:T(4,128)}, f32[5,32,3]{2,1,0:T(8,128)S...) while((s32[]{:T(128)}, f32[3,4096]{1,0:T(4,128)S(1)}, ...), condition=%wide.region_3.4_spmd, body=%wide.region_2.3_spmd.sunk | while | flops 1179681 | bytes 11298529 | solution.py:96
  1581.9 12.1 constant_dynamic-update-slice_fusion.96
  1594.1 16.0 reshape.1291
  1611.1 15.0 all-gather.4
  1626.1 9.1 while.114
  1635.9 15.0 all-gather.5
  1651.0 9.1 while.115
  1660.8 9.1 fusion.486
  (1258 shorter events, 617.0 us)
Async XLA Ops:
  19.9 1061.7 %collective-permute-start = (f32[3,192,32,4]{1,2,3,0:T(8,128)}, f32[3,192,32,4]{1,2,3,0:T(8,128)}, u32[]{:S(2)}, u32[]{:S(2)}) collective-permute-start(f32[3,192,32,4]{1,2,3,0:T(8,128)} %copy.667), channel_id=1, source_target_pairs={{8,0},{16,8},{24,16},{0,24},{9,1},{17,9},{25,17},{1,25},{10,2},{18... | collective-permute-start | bytes 884744 | tf_op jit(solution)/shard_map/ppermute | solution.py:22
  30.8 1057.3 %collective-permute-start.1 = (f32[3,192,32,4]{1,2,3,0:T(8,128)}, f32[3,192,32,4]{1,2,3,0:T(8,128)}, u32[]{:S(2)}, u32[]{:S(2)}) collective-permute-start(f32[3,192,32,4]{1,2,3,0:T(8,128)} %copy.668), channel_id=1, source_target_pairs={{0,8},{8,16},{16,24},{24,0},{1,9},{9,17},{17,25},{25,1},{2,10},{10... | collective-permute-start | bytes 884744 | tf_op jit(solution)/shard_map/ppermute | solution.py:21
  31.6 1062.9 %collective-permute-start.2 = (f32[3,1,32,128]{3,2,1,0:T(8,128)S(1)}, f32[3,1,32,128]{3,2,1,0:T(8,128)S(1)}, u32[]{:S(2)}, u32[]{:S(2)}) collective-permute-start(f32[3,1,32,128]{3,2,1,0:T(8,128)S(1)} %get-tuple-element.1485), channel_id=1, source_target_pairs={{1,0},{2,1},{3,2},{4,3},{5,4},{6,5},{7,6},{9,8},{10,9},{11,10},{12... | collective-permute-start | bytes 147464 | tf_op jit(solution)/shard_map/ppermute | solution.py:22
  32.9 11.0 slice-start
  32.9 11.0 slice-start.1
  32.9 11.0 slice-start.2
  32.9 1061.5 %collective-permute-start.3 = (f32[3,1,32,128]{3,2,1,0:T(8,128)S(1)}, f32[3,1,32,128]{3,2,1,0:T(8,128)S(1)}, u32[]{:S(2)}, u32[]{:S(2)}) collective-permute-start(f32[3,1,32,128]{3,2,1,0:T(8,128)S(1)} %get-tuple-element.1486), channel_id=1, source_target_pairs={{0,1},{1,2},{2,3},{3,4},{4,5},{5,6},{6,7},{8,9},{9,10},{10,11},{11... | collective-permute-start | bytes 147464 | tf_op jit(solution)/shard_map/ppermute | solution.py:21
  74.8 6.3 copy-start.1
  74.8 6.3 copy-start.2
  1081.6 12.8 copy-start
  1594.1 32.0 %copy-start.3 = (f32[8]{0:T(128)S(1)}, f32[8]{0:T(128)}, u32[]{:S(2)}) copy-start(f32[8]{0:T(128)} %get-tuple-element.871) | copy-start | bytes 100
where the time goes:
time: 1700 us; the launch traced here: 1670 us
  other arithmetic  629 us (37%)
  local copies, waits for them, and re-layouts  599 us (35%)
  loops' own time  304 us (18%)
  between operations  67.7 us (4%)
  blocking collectives  56.8 us (3%)
    another operation x2, loops' own time, shards(): lax.linalg.tridiagonal_solve(below_band, diagonal, above_band, columns)  302 us
    broadcast_in_dim x383, local copies, waits for them, and re-layouts, shards(): lax.linalg.tridiagonal_solve(below_band, diagonal, above_band, columns)  248 us
    div x7, other arithmetic, shards(): lax.linalg.tridiagonal_solve(below_band, diagonal, above_band, columns)  128 us
    sub x5, other arithmetic, shards(): lax.linalg.tridiagonal_solve(below_band, diagonal, above_band, columns)  104 us
    while x230, other arithmetic  96.9 us
    add x1, other arithmetic, shards(): forcing = velocity + GAMMA * advection + ZETA * old_advection  92 us
    unnamed x51, other arithmetic  74.2 us
    slice x24, local copies, waits for them, and re-layouts, shards(): lax.linalg.tridiagonal_solve(jnp.stack([below_band] * 3), jnp.stack([diag...  65.8 us
  transfers between devices with their start and end apart: 4, of which 0 were waited for; matrix products, arithmetic and copies ran while one was open for 40% of the time, Pallas kernels for 0%

commit v1 on v0

v1 whole, which is shorter than its diff:
```python
import functools
import math

import jax
import jax.numpy as jnp
import numpy as np
from jax import lax
from jax.experimental import pallas as pl
from jax.experimental.pallas import tpu as pltpu
from jax.sharding import PartitionSpec as P

STIFF = 1024
GAMMA = 5.0 / 12.0
ZETA = -17.0 / 60.0
WEIGHTS = (672.0, -168.0, 32.0, -3.0)
UNIT = 1.0 / 840.0
F32 = jnp.float32
BF16 = jnp.bfloat16
MIB = 1 << 20

INV_GAP, FORWARD, BACKWARD, PSI, PHI = range(5)


def shift_matrix(size, periodic):
    m = np.zeros((size, size), np.float32)
    for j in range(size):
        for k, w in enumerate(WEIGHTS, 1):
            for i, s in ((j + k, w), (j - k, -w)):
                if periodic:
                    m[i % size, j] += s
                elif 0 <= i < size:
                    m[i, j] += s
    return m


def edge_matrices():
    left, right = np.zeros((4, 4), np.float32), np.zeros((4, 4), np.float32)
    for l in range(4):
        for m in range(4):
            if m >= l:
                left[m, l] = -WEIGHTS[l + 3 - m]
            if m <= l:
                right[m, l] = WEIGHTS[m + 3 - l]
    return np.kron(np.eye(32), left), np.kron(np.eye(32), right)


def lanes(shape):
    return lax.broadcasted_iota(jnp.int32, shape, len(shape) - 1)


def split(values):
    hi = values.astype(BF16)
    return hi, (values - hi.astype(F32)).astype(BF16)


def pack_kernel(group, v_ref, left_ref, right_ref):
    lane = lanes((8, 128))
    low = (lane & 7) < 4
    slot = lane >> 3
    for c in range(3):
        for g in range(v_ref.shape[1] // group):
            halves = [jnp.zeros((8, 128), F32), jnp.zeros((8, 128), F32)]
            for yl in range(group):
                for zt in range(4):
                    s = zt * 4 + yl // 2
                    tile = v_ref[c, g * group + yl, 8 * zt : 8 * zt + 8, :]
                    turned = pltpu.roll(tile, (8 * s + 4) % 128, 1)
                    halves[yl % 2] = jnp.where(slot == s, turned, halves[yl % 2])
            even, odd = halves
            right_ref[c, g] = jnp.where(low, even, pltpu.roll(odd, 4, 1))
            left_ref[c, g] = jnp.where(low, pltpu.roll(even, 124, 1), odd)


def interleave(left, right):
    low = (lanes((8, 128)) & 7) < 4
    even = jnp.where(low, right, pltpu.roll(left, 4, 1))
    odd = jnp.where(low, pltpu.roll(right, 124, 1), left)
    return even, odd


def pack(velocity, group, block):
    n = velocity.shape[1]
    packed = jax.ShapeDtypeStruct((3, n // group, 8, 128), F32)
    out = pl.BlockSpec((3, block // group, 8, 128), lambda i: (0, i, 0, 0))
    return pl.pallas_call(
        functools.partial(pack_kernel, group),
        grid=(n // block,),
        in_specs=[pl.BlockSpec((3, block, 32, 128), lambda i: (0, i, 0, 0))],
        out_specs=[out, out],
        out_shape=[packed, packed],
        name="pack_edges",
    )(velocity)


def coef_kernel(n, lower_ref, upper_ref, kappa_ref, inv_ref, out_ref):
    def up(i, state):
        phi, flux = state
        out_ref[PHI, i] = phi
        out_ref[FORWARD, i] = phi * kappa_ref[i]
        out_ref[INV_GAP, i] = inv_ref[i]
        flux = flux + kappa_ref[i] * phi
        return phi + upper_ref[i] * flux, flux

    def down(k, state):
        i = n - 1 - k
        psi, flux = state
        out_ref[PSI, i] = psi
        out_ref[BACKWARD, i] = psi * kappa_ref[i]
        flux = flux + kappa_ref[i] * psi
        return psi + lower_ref[i] * flux, flux

    def both(i, state):
        return up(i, state[0]), down(i, state[1])

    start = ((lower_ref[0], jnp.float32(1.0)), (upper_ref[n - 1], jnp.float32(1.0)))
    (wronskian, _), _ = lax.fori_loop(0, n, both, start, unroll=4)
    scale = (1.0 / jnp.full((8, 128), wronskian, F32))[0, 0]

    def norm(i, _):
        out_ref[PHI, i] = out_ref[PHI, i] * scale
        out_ref[PSI, i] = out_ref[PSI, i] * scale
        return 0

    lax.fori_loop(0, n, norm, 0, unroll=4)


def smem():
    return pl.BlockSpec(memory_space=pltpu.SMEM)


def vmem():
    return pl.BlockSpec(memory_space=pltpu.VMEM)


def coefs(lower_gap, upper_gap):
    n = lower_gap.shape[0]
    gap_sum = lower_gap + upper_gap
    return pl.pallas_call(
        functools.partial(coef_kernel, n),
        in_specs=[smem()] * 4,
        out_specs=smem(),
        out_shape=jax.ShapeDtypeStruct((5, n), F32),
        name="coefficients",
    )(lower_gap, upper_gap, gap_sum * (0.5 / STIFF), 1.0 / gap_sum)


def main_kernel(n, block, group, co, v_ref, before_ref, after_ref, below_ref, above_ref, old_ref,
                dx_ref, dz_ref, adv_ref, u_ref, a_ref, b_ref, f_ref):
    step = pl.program_id(0)
    steps = pl.num_programs(0)

    @pl.when(step == 0)
    def _():
        a_ref[...] = jnp.zeros_like(a_ref)

    rows = group * 32

    def chunk(k, _):
        y0 = k * group
        first = jnp.logical_and(step == 0, k == 0)
        last = jnp.logical_and(step == steps - 1, k == block // group - 1)
        inner = pl.ds(y0, group)
        vel = [v_ref[c, inner].reshape(rows, 128) for c in range(3)]
        for c in range(3):
            f = vel[c]
            pair = jnp.concatenate(split(f), axis=1)
            along_x = jnp.dot(pair, dx_ref[...], preferred_element_type=F32)
            both = jnp.dot(dz_ref[...], pair, preferred_element_type=F32)
            along_z = both[:, :128] + both[:, 128:]
            below = jnp.where(k == 0, before_ref[c, 0], v_ref[c, jnp.maximum(y0 - 1, 0)])
            below = jnp.where(first, below_ref[c, 0], below)
            above = jnp.where(k == block // group - 1, after_ref[c, 0],
                              v_ref[c, jnp.minimum(y0 + group, block - 1)])
            above = jnp.where(last, above_ref[c, 0], above)
            acc = a_ref[c]
            for y in range(group):
                here = slice(32 * y, 32 * y + 32)
                i = step * block + y0 + y
                under = below if y == 0 else f[32 * y - 32 : 32 * y]
                over = above if y == group - 1 else f[32 * y + 32 : 32 * y + 64]
                flat = (vel[0][here] * along_x[here] + vel[2][here] * along_z[here]) * (-UNIT)
                adv = flat - vel[1][here] * ((over - under) * co[INV_GAP, i])
                force = f[here] + GAMMA * adv + ZETA * old_ref[c, y0 + y]
                acc = acc + co[FORWARD, i] * force
                adv_ref[c, i] = adv
                f_ref[c, i] = force
                u_ref[c, i] = co[PSI, i] * acc
            a_ref[c] = acc
        return 0

    lax.fori_loop(0, block // group, chunk, 0)

    @pl.when(step == steps - 1)
    def _():
        b_ref[...] = jnp.zeros_like(b_ref)

        def back(k, _):
            for c in range(3):
                acc = b_ref[c]
                for y in range(group):
                    i = n - 1 - k * group - y
                    u_ref[c, i] = u_ref[c, i] + co[PHI, i] * acc
                    acc = acc + co[BACKWARD, i] * f_ref[c, i]
                b_ref[c] = acc
            return 0

        lax.fori_loop(0, n // group, back, 0)


def main_part(velocity, below, above, old, table, group, block):
    n = velocity.shape[1]
    dx = shift_matrix(128, False)
    dx = jnp.asarray(np.concatenate([dx, dx]), BF16)
    dz = jnp.asarray(np.kron(np.eye(group), shift_matrix(32, True).T), BF16)
    tile = pl.BlockSpec((3, block, 32, 128), lambda i: (0, i, 0, 0))
    kernel = functools.partial(main_kernel, n, block, group)

    def body(v, before, after, lo, hi, old, co, dx, dz, *rest):
        kernel(co, v, before, after, lo, hi, old, dx, dz, *rest)

    return pl.pallas_call(
        body,
        grid=(n // block,),
        in_specs=[
            tile,
            pl.BlockSpec((3, 1, 32, 128), lambda i: (0, jnp.maximum(i * block - 1, 0), 0, 0)),
            pl.BlockSpec((3, 1, 32, 128), lambda i: (0, jnp.minimum(i * block + block, n - 1), 0, 0)),
            pl.BlockSpec((3, 1, 32, 128), lambda i: (0, 0, 0, 0)),
            pl.BlockSpec((3, 1, 32, 128), lambda i: (0, 0, 0, 0)),
            tile,
            smem(),
            pl.BlockSpec(dx.shape, lambda i: (0, 0)),
            pl.BlockSpec(dz.shape, lambda i: (0, 0)),
        ],
        out_specs=[vmem()] * 4,
        out_shape=[
            pltpu.VMEM((3, n, 32, 128), F32),
            pltpu.VMEM((3, n, 32, 128), F32),
            pltpu.VMEM((3, 32, 128), F32),
            pltpu.VMEM((3, 32, 128), F32),
        ],
        scratch_shapes=[pltpu.VMEM((3, n, 32, 128), F32)],
        compiler_params=pltpu.CompilerParams(vmem_limit_bytes=24 * MIB),
        name="inner_part",
    )(velocity, velocity, velocity, below, above, old, table, dx, dz)


def edge_kernel(groups, group, co, from_left, from_right, left_ref, right_ref, a_ref, b_ref,
                ml_ref, mr_ref, adv_l, adv_r, u_l, u_r, load_ref, table_ref):
    n = groups * group
    lane = lanes((8, 128))
    place = (lane & 31) >> 2

    def weights(g, _):
        for t, row in enumerate((FORWARD, BACKWARD, PSI, PHI)):
            value = jnp.zeros((8, 128), F32)
            for yl in range(group):
                value = jnp.where(place == yl, co[row, g * group + yl], value)
            table_ref[t, g] = value
        return 0

    lax.fori_loop(0, groups, weights, 0)

    sides = (
        (from_left, ml_ref, left_ref, adv_l, u_l),
        (from_right, mr_ref, right_ref, adv_r, u_r),
    )
    totals = []
    for halo, matrix, own, adv, u in sides:
        for c in range(3):
            hi, lo = split(halo[c].reshape(groups * 8, 128))
            slope = jnp.dot(hi, matrix[...], preferred_element_type=F32)
            slope = slope + jnp.dot(lo, matrix[...], preferred_element_type=F32)
            adv[c] = (own[0].reshape(groups * 8, 128) * slope * (-UNIT)).reshape(groups, 8, 128)

            def forward(g, carry):
                part = table_ref[0, g] * (GAMMA * adv[c, g])
                for s in (1, 2, 4):
                    part = part + jnp.where(place >= s, pltpu.roll(part, 4 * s, 1), 0.0)
                u[c, g] = table_ref[2, g] * (part + carry)
                total = jnp.where(place == 7, part, 0.0)
                for s in (1, 2, 4):
                    total = total + pltpu.roll(total, 128 - 4 * s, 1)
                return carry + total

            def backward(k, carry):
                g = groups - 1 - k
                own_part = table_ref[1, g] * (GAMMA * adv[c, g])
                part = own_part
                for s in (1, 2, 4):
                    part = part + jnp.where(place < 8 - s, pltpu.roll(part, 128 - 4 * s, 1), 0.0)
                u[c, g] = u[c, g] + table_ref[3, g] * (part - own_part + carry)
                total = jnp.where(place == 0, part, 0.0)
                for s in (1, 2, 4):
                    total = total + pltpu.roll(total, 4 * s, 1)
                return carry + total

            zero = jnp.zeros((8, 128), F32)
            totals.append(
                (lax.fori_loop(0, groups, forward, zero), lax.fori_loop(0, groups, backward, zero))
            )

    for c in range(3):
        for t, (main, row, i) in enumerate(((b_ref, PHI, 0), (a_ref, PSI, n - 1))):
            at_left, at_right = totals[c][1 - t], totals[3 + c][1 - t]
            for zt in range(4):
                value = main[c, 8 * zt : 8 * zt + 8, :]
                value = value + jnp.where(lane < 4, pltpu.roll(at_left, (128 - 32 * zt) % 128, 1), 0.0)
                value = value + jnp.where(lane >= 124, pltpu.roll(at_right, 96 - 32 * zt, 1), 0.0)
                load_ref[pl.ds(t * 96 + c * 32 + zt * 8, 8), :] = value * co[row, i]
    row = lax.broadcasted_iota(jnp.int32, (8, 128), 0)
    ends = jnp.where(row == 0, co[PSI, 0], co[PSI, n - 1])
    ends = jnp.where(row == 2, co[PHI, 0], ends)
    load_ref[192:200, :] = jnp.where(row == 3, co[PHI, n - 1], ends)


def edge_part(from_left, from_right, left, right, a_sum, b_sum, table, group):
    groups = left.shape[1]
    ml, mr = edge_matrices()
    packed = pltpu.VMEM(left.shape, F32)

    def body(fl, fr, lo, hi, a, b, co, ml, mr, *rest):
        edge_kernel(groups, group, co, fl, fr, lo, hi, a, b, ml, mr, *rest)

    return pl.pallas_call(
        body,
        in_specs=[vmem()] * 6 + [smem()] + [vmem()] * 2,
        out_specs=[vmem()] * 5,
        out_shape=[packed] * 4 + [jax.ShapeDtypeStruct((200, 128), F32)],
        scratch_shapes=[pltpu.VMEM((4, groups, 8, 128), F32)],
        name="edge_part",
    )(from_left, from_right, left, right, a_sum, b_sum, table, jnp.asarray(ml, BF16), jnp.asarray(mr, BF16))


def couple(parts, mine, loads, below_ref, above_ref):
    def read(i):
        first, last = loads[i, 0:96, :], loads[i, 96:192, :]
        return (first, last) + tuple(loads[i, 192 + t : 193 + t, :] for t in range(4))

    def up(i, state):
        a, r = state
        first, last, psi_f, psi_l, phi_f, phi_l = read(i)
        share = psi_l * r / (1.0 - psi_f * r)
        return last + psi_l * a + share * (first + psi_f * a), phi_l + share * phi_f

    def down(k, state):
        b, q = state
        first, last, psi_f, psi_l, phi_f, phi_l = read(parts - 1 - k)
        share = phi_f * q / (1.0 - phi_l * q)
        return first + phi_f * b + share * (last + phi_l * b), psi_f + share * psi_l

    zero = (jnp.zeros((96, 128), F32), jnp.zeros((1, 128), F32))
    a, r = lax.fori_loop(0, mine, up, zero)
    b, q = lax.fori_loop(0, parts - 1 - mine, down, zero)
    first, last, psi_f, psi_l, phi_f, phi_l = read(mine)
    a_next, r_next = up(mine, (a, r))
    above = (b + q * a_next) / (1.0 - q * r_next)
    u_first = (first + psi_f * a + phi_f * above) / (1.0 - psi_f * r)
    above_ref[...] = above
    below_ref[...] = a + r * u_first


def final_kernel(parts, block, group, me, co, loads, adv_part, u_part, adv_l, adv_r, u_l, u_r,
                 u_ref, adv_ref, below_ref, above_ref):
    step = pl.program_id(0)

    @pl.when(step == 0)
    def _():
        couple(parts, me[0], loads, below_ref, above_ref)

    lane = lanes((8, 128))
    rim = jnp.logical_or(lane < 4, lane >= 124)
    for c in range(3):
        for k in range(block // group):
            g = step * (block // group) + k
            u_halves = interleave(u_l[c, g], u_r[c, g])
            adv_halves = interleave(adv_l[c, g], adv_r[c, g])
            for yl in range(group):
                i = g * group + yl
                psi, phi = co[PSI, i], co[PHI, i]
                for zt in range(4):
                    s = zt * 4 + yl // 2
                    turn = (124 - 8 * s) % 128
                    z = slice(8 * zt, 8 * zt + 8)
                    lines = slice(c * 32 + 8 * zt, c * 32 + 8 * zt + 8)
                    value = u_part[c, i, z, :] + psi * below_ref[lines, :] + phi * above_ref[lines, :]
                    extra = jnp.where(rim, pltpu.roll(u_halves[yl % 2], turn, 1), 0.0)
                    u_ref[c, k * group + yl, z, :] = value + extra
                    extra = jnp.where(rim, pltpu.roll(adv_halves[yl % 2], turn, 1), 0.0)
                    adv_ref[c, k * group + yl, z, :] = adv_part[c, i, z, :] + extra


def final_part(loads, me, table, adv_part, u_part, edges, group, block):
    parts = loads.shape[0]
    n = adv_part.shape[1]
    whole = jax.ShapeDtypeStruct((3, n, 32, 128), F32)
    tile = pl.BlockSpec((3, block, 32, 128), lambda i: (0, i, 0, 0))
    return pl.pallas_call(
        functools.partial(final_kernel, parts, block, group),
        grid=(n // block,),
        in_specs=[smem(), smem()] + [vmem()] * 7,
        out_specs=[tile, tile],
        out_shape=[whole, whole],
        scratch_shapes=[pltpu.VMEM((96, 128), F32), pltpu.VMEM((96, 128), F32)],
        compiler_params=pltpu.CompilerParams(vmem_limit_bytes=24 * MIB),
        name="final_part",
    )(me, table, loads, adv_part, u_part, *edges)


def shards(velocity, old_advection, lower_gap, upper_gap):
    n = velocity.shape[1]
    group = math.gcd(n, 8)
    block = 2 * group if n % (2 * group) == 0 else group
    wide = 3 * group if n % (3 * group) == 0 else group
    nx, ny = lax.axis_size("gx"), lax.axis_size("gy")
    ring = [(i, (i + 1) % nx) for i in range(nx)]
    line = [(i, i + 1) for i in range(ny - 1)]

    left, right = pack(velocity, group, block)
    from_left = lax.ppermute(right, "gx", ring)
    from_right = lax.ppermute(left, "gx", [(j, i) for i, j in ring])
    below = lax.ppermute(velocity[:, n - 1 :], "gy", line)
    above = lax.ppermute(velocity[:, :1], "gy", [(j, i) for i, j in line])
    table = coefs(lower_gap, upper_gap)
    adv_part, u_part, a_sum, b_sum = main_part(velocity, below, above, old_advection, table, group, wide)
    *edges, load = edge_part(from_left, from_right, left, right, a_sum, b_sum, table, group)
    loads = lax.all_gather(load, "gy")
    me = lax.axis_index("gy").astype(jnp.int32).reshape(1)
    u, adv = final_part(loads, me, table, adv_part, u_part, edges, group, block)
    return u, adv


def solution(mesh):
    spec = P(None, "gy", None, "gx")
    return jax.shard_map(
        shards,
        mesh=mesh,
        in_specs=(spec, spec, P("gy"), P("gy")),
        out_specs=(spec, spec),
        check_vma=False,
    )
```

time: 1700 us -> 219 us (0.13); the launches traced: 1670 us -> 219 us
  other arithmetic: 629 us -> 0.57 us
  local copies, waits for them, and re-layouts: 599 us -> 22.1 us
  loops' own time: 304 us -> 0 us
  Pallas kernels: 0 us -> 170 us
  between operations: 67.7 us -> 0.78 us
  blocking collectives: 56.8 us -> 17 us
    another operation x7 -> x0, loops' own time: 304 us -> none  [the longest x2 302 us: shards(): lax.linalg.tridiagonal_solve(below_band, diagonal, above_band, columns)]
    broadcast_in_dim x574 -> x0, local copies, waits for them, and re-layouts: 266 us -> none  [the longest x383 248 us: shards(): lax.linalg.tridiagonal_solve(below_band, diagonal, above_band, columns)]
    sub x13 -> x0, other arithmetic: 176 us -> none  [the longest x5 104 us: shards(): lax.linalg.tridiagonal_solve(below_band, diagonal, above_band, columns)]
    pallas_call x0 -> x5, Pallas kernels: none -> 170 us  [the longest x1 124 us: edge_part(): pl.pallas_call(body, in_specs=[vmem()] * 6 + [smem()] + [vmem()] * 2, out...]
    slice x87 -> x1, local copies, waits for them, and re-layouts: 152 us -> 0.83 us  [shards(): above = lax.ppermute(velocity[:, :1], 'gy', [(j, i) for i, j in line])]
    div x19 -> x1, other arithmetic: 134 us -> 0.57 us  [coefs(): 1.0 / gap_sum]
    while x230 -> x0, other arithmetic: 96.9 us -> none
    add x1 -> x0, other arithmetic: 92 us -> none  [shards(): forcing = velocity + GAMMA * advection + ZETA * old_advection]
  transfers between devices with their start and end apart: 4 -> 4, of which waited for: 0 -> 0; matrix products, arithmetic and copies ran while one was open for 40% -> 1% of each run, Pallas kernels for 0% -> 9%
where the time goes in v1:
time: 219 us
  Pallas kernels  170 us (78%)
  local copies, waits for them, and re-layouts  22.1 us (10%)
  blocking collectives  17 us (8%)
  starting transfers between devices  8.21 us (4%)
    pallas_call x1, Pallas kernels, edge_part(): pl.pallas_call(body, in_specs=[vmem()] * 6 + [smem()] + [vmem()] * 2, out...  124 us
    unnamed x30, local copies, waits for them, and re-layouts  21.3 us
    all_gather x1, blocking collectives, shards(): loads = lax.all_gather(load, 'gy')  17 us
    pallas_call x1, Pallas kernels, main_part(): pl.pallas_call(body, grid=(n // block,), in_specs=[tile, pl.BlockSpec((3,...  14.9 us
    pallas_call x1, Pallas kernels, final_part(): pl.pallas_call(functools.partial(final_kernel, parts, block, group), grid...  13.9 us
    pallas_call x1, Pallas kernels, pack(): pl.pallas_call(functools.partial(pack_kernel, group), grid=(n // block,),...  11.3 us
    pallas_call x1, Pallas kernels, coefs(): pl.pallas_call(functools.partial(coef_kernel, n), in_specs=[smem()] * 4,...  5.43 us
  transfers between devices with their start and end apart: 4, of which 0 were waited for; matrix products, arithmetic and copies ran while one was open for 1% of the time, Pallas kernels for 9%

profile of v1, /device:TPU:0, one launch (start us, length us, event | category | flops | bytes accessed | tf_op | source)
XLA Modules:
  0.0 218.7 jit_solution(14140333017835299478)
XLA Ops:
  0.6 0.0 copy-start.5
  0.6 0.0 copy-start.8
  0.7 0.0 copy-start.14
  0.7 0.0 copy-start.13
  0.7 11.3 %pack_edges.1 = (f32[3,24,8,128]{3,2,1,0:T(8,128)}, f32[3,24,8,128]{3,2,1,0:T(8,128)}) custom-call(f32[3,192,32,128]{3,2,1,0:T(8,128)} %after.1), custom_call_target="tpu_custom_call" | custom-call | tf_op jit(solution)/shard_map/pack_edges/pallas_call | solution.py:85
  12.0 2.9 %collective-permute-start = (f32[3,24,8,128]{3,2,1,0:T(8,128)}, f32[3,24,8,128]{3,2,1,0:T(8,128)S(1)}, u32[]{:S(2)}, u32[]{:S(2)}) collective-permute-start(f32[3,24,8,128]{3,2,1,0:T(8,128)} %get-tuple-element.13.hi), channel_id=1, source_target_pairs={{0,8},{8,16},{16,24},{24,0},{1,9},{9,17},{17,25},{25,1},{2,10},{10... | collective-permute-start | bytes 884744 | tf_op jit(solution)/shard_map/ppermute | solution.py:420
  14.9 1.0 collective-permute-start.1
  15.9 0.8 fusion
  16.7 1.3 collective-permute-start.3
  18.0 3.0 %collective-permute-start.2 = (f32[3,1,32,128]{3,2,1,0:T(8,128)S(1)}, f32[3,1,32,128]{3,2,1,0:T(8,128)S(1)}, u32[]{:S(2)}, u32[]{:S(2)}) collective-permute-start(f32[3,1,32,128]{3,2,1,0:T(8,128)S(1)} %get-tuple-element.25), channel_id=1, source_target_pairs={{0,1},{1,2},{2,3},{3,4},{4,5},{5,6},{6,7},{8,9},{9,10},{10,11},{11... | collective-permute-start | bytes 147464 | tf_op jit(solution)/shard_map/ppermute | solution.py:422
  21.1 0.0 copy-done.14
  21.1 0.0 copy-done.13
  21.1 0.6 broadcast_divide_fusion
  21.7 5.4 %coefficients.1.co = f32[5,192]{1,0:T(8,128)} custom-call(f32[192]{0:T(256)} %lower_ref.1, f32[192]{0:T(256)} %upper_ref.1, f32[192]{0:T(256)} %get-tuple-element.27.kappa_ref, f32[192]{0:T(256)} %get-tuple-element.26.inv_ref), custom_call_target="tpu_custom_call" | custom-call | tf_op jit(solution)/shard_map/coefficients/pallas_call | solution.py:138
  27.1 0.0 collective-permute-done.3.hi
  27.1 0.0 collective-permute-done.2.lo
  27.1 0.0 copy-done.5
  27.1 0.0 copy-done.8
  27.1 0.0 copy-start
  27.1 3.7 %copy-done = f32[3,192,32,128]{3,2,1,0:T(8,128)S(1)} copy-done((f32[3,192,32,128]{3,2,1,0:T(8,128)S(1)}, f32[3,192,32,128]{3,2,1,0:T(8,128)}, u32[]{:S(2)}) %copy-start) | copy-done | bytes 9437208
  30.8 0.0 copy-start.6
  30.8 0.7 copy-done.6
  31.5 0.0 copy-start.7
  31.5 14.9 %inner_part.1 = (f32[3,192,32,128]{3,2,1,0:T(8,128)S(1)}, f32[3,192,32,128]{3,2,1,0:T(8,128)S(1)}, f32[3,32,128]{2,1,0:T(8,128)S(1)}, f32[3,32,128]{2,1,0:T(8,128)S(1)}) custom-call(f32[3,192,32,128]{3,2,1,0:T(8,128)S(1)} %copy-done, f32[3,192,32,128]{3,2,1,0:T(8,128)S(1)} %copy-done, f32[3,192,32,128]{3,2,1,0:T(8,128)S(1)} %copy-done, ...), custom_call_target="tpu_custom_call" | custom-call | tf_op jit(solution)/shard_map/inner_part/pallas_call | solution.py:221
  46.4 0.0 copy-start.1
  46.4 3.7 %copy-done.1 = f32[3,192,32,128]{3,2,1,0:T(8,128)} copy-done((f32[3,192,32,128]{3,2,1,0:T(8,128)}, f32[3,192,32,128]{3,2,1,0:T(8,128)S(1)}, u32[]{:S(2)}) %copy-start.1) | copy-done | bytes 9437208
  50.2 0.0 copy-start.3
  50.2 3.7 %copy-done.3 = f32[3,192,32,128]{3,2,1,0:T(8,128)} copy-done((f32[3,192,32,128]{3,2,1,0:T(8,128)}, f32[3,192,32,128]{3,2,1,0:T(8,128)S(1)}, u32[]{:S(2)}) %copy-start.3) | copy-done | bytes 9437208
  53.9 0.0 copy-start.9
  53.9 0.6 copy-done.9
  54.5 0.0 copy-start.10
  54.5 0.6 copy-done.10
  55.1 0.0 collective-permute-done.fl
  55.2 0.0 copy-start.11
  55.2 0.0 collective-permute-done.1.fr
  55.2 0.0 copy-start.12
  55.2 0.7 copy-done.11
  55.9 0.1 copy-done.12
  56.0 124.5 %edge_part.1 = (f32[3,24,8,128]{3,2,1,0:T(8,128)S(1)}, f32[3,24,8,128]{3,2,1,0:T(8,128)S(1)}, f32[3,24,8,128]{3,2,1,0:T(8,128)S(1)}, f32[3,24,8,128]{3,2,1,0:T(8,128)S(1)}, f32[200,128]{1,0:T(8,128)}) custom-call(f32[3,24,8,128]{3,2,1,0:T(8,128)} %copy-done.11, f32[3,24,8,128]{3,2,1,0:T(8,128)} %copy-done.12, f32[3,24,8,128]{3,2,1,0:T(8,128)} %get-tuple-element.14.lo, ...), custom_call_target="tpu_custom_call" | custom-call | tf_op jit(solution)/shard_map/edge_part/pallas_call | solution.py:325
  180.5 17.0 %all-gather = f32[1600,128]{1,0:T(8,128)S(1)} all-gather(f32[200,128]{1,0:T(8,128)} %get-tuple-element.17), channel_id=2, replica_groups=mesh['gx'=4,'gy'=8] {'gy'}, dimensions={0}, use_global_device_ids=true | all-gather | bytes 921600 | tf_op jit(solution)/shard_map/all_gather | solution.py:427
  197.4 0.0 copy-done.7
  197.4 0.0 copy-start.2
  197.4 3.7 %copy-done.2 = f32[3,192,32,128]{3,2,1,0:T(8,128)S(1)} copy-done((f32[3,192,32,128]{3,2,1,0:T(8,128)S(1)}, f32[3,192,32,128]{3,2,1,0:T(8,128)}, u32[]{:S(2)}) %copy-start.2) | copy-done | bytes 9437208
  201.1 0.0 copy-start.4
  201.1 3.7 %copy-done.4 = f32[3,192,32,128]{3,2,1,0:T(8,128)S(1)} copy-done((f32[3,192,32,128]{3,2,1,0:T(8,128)S(1)}, f32[3,192,32,128]{3,2,1,0:T(8,128)}, u32[]{:S(2)}) %copy-start.4) | copy-done | bytes 9437208
  204.8 13.9 %final_part.1 = (f32[3,192,32,128]{3,2,1,0:T(8,128)}, f32[3,192,32,128]{3,2,1,0:T(8,128)}) custom-call(s32[1]{0:T(128)} %bitcast.me, f32[5,192]{1,0:T(8,128)S(1)} %copy-done.7, f32[8,200,128]{2,1,0:T(8,128)S(1)} %bitcast.2, f32[3,192,32,128]{3,2,1,0:T(8,128)S(1)} %copy-done.2, f32[3,192,32,128]{3,2,1,0:T(8,128)S(1)} %copy-done.4, ...), custom_call_target="tpu_custom_call" | custom-call | tf_op jit(solution)/shard_map/final_part/pallas_call | solution.py:398
Async XLA Ops:
  0.6 26.5 %copy-start.5 = (bf16[256,256]{1,0:T(8,128)(2,1)S(1)}, bf16[256,256]{1,0:T(8,128)(2,1)}, u32[]{:S(2)}) copy-start(bf16[256,256]{1,0:T(8,128)(2,1)} %constant.17.clone.dz) | copy-start | bytes 393220
  0.6 26.5 %copy-start.8 = (bf16[256,128]{1,0:T(8,128)(2,1)S(1)}, bf16[256,128]{1,0:T(8,128)(2,1)}, u32[]{:S(2)}) copy-start(bf16[256,128]{1,0:T(8,128)(2,1)} %constant.16.clone.dx) | copy-start | bytes 196612
  0.7 20.4 %copy-start.14 = (f32[192]{0:T(256)S(1)}, f32[192]{0:T(256)}, u32[]{:S(2)}) copy-start(f32[192]{0:T(256)} %upper_ref.1) | copy-start | bytes 2308
  0.7 20.4 %copy-start.13 = (f32[192]{0:T(256)S(1)}, f32[192]{0:T(256)}, u32[]{:S(2)}) copy-start(f32[192]{0:T(256)} %lower_ref.1) | copy-start | bytes 2308
  12.0 43.2 %collective-permute-start = (f32[3,24,8,128]{3,2,1,0:T(8,128)}, f32[3,24,8,128]{3,2,1,0:T(8,128)S(1)}, u32[]{:S(2)}, u32[]{:S(2)}) collective-permute-start(f32[3,24,8,128]{3,2,1,0:T(8,128)} %get-tuple-element.13.hi), channel_id=1, source_target_pairs={{0,8},{8,16},{16,24},{24,0},{1,9},{9,17},{17,25},{25,1},{2,10},{10... | collective-permute-start | bytes 884744 | tf_op jit(solution)/shard_map/ppermute | solution.py:420
  14.9 40.2 %collective-permute-start.1 = (f32[3,24,8,128]{3,2,1,0:T(8,128)}, f32[3,24,8,128]{3,2,1,0:T(8,128)S(1)}, u32[]{:S(2)}, u32[]{:S(2)}) collective-permute-start(f32[3,24,8,128]{3,2,1,0:T(8,128)} %get-tuple-element.14.lo), channel_id=1, source_target_pairs={{8,0},{16,8},{24,16},{0,24},{9,1},{17,9},{25,17},{1,25},{10,2},{18... | collective-permute-start | bytes 884744 | tf_op jit(solution)/shard_map/ppermute | solution.py:421
  16.7 10.4 %collective-permute-start.3 = (f32[3,1,32,128]{3,2,1,0:T(8,128)S(1)}, f32[3,1,32,128]{3,2,1,0:T(8,128)S(1)}, u32[]{:S(2)}, u32[]{:S(2)}) collective-permute-start(f32[3,1,32,128]{3,2,1,0:T(8,128)S(1)} %get-tuple-element.24), channel_id=1, source_target_pairs={{1,0},{2,1},{3,2},{4,3},{5,4},{6,5},{7,6},{9,8},{10,9},{11,10},{12... | collective-permute-start | bytes 147464 | tf_op jit(solution)/shard_map/ppermute | solution.py:423
  18.0 9.1 %collective-permute-start.2 = (f32[3,1,32,128]{3,2,1,0:T(8,128)S(1)}, f32[3,1,32,128]{3,2,1,0:T(8,128)S(1)}, u32[]{:S(2)}, u32[]{:S(2)}) collective-permute-start(f32[3,1,32,128]{3,2,1,0:T(8,128)S(1)} %get-tuple-element.25), channel_id=1, source_target_pairs={{0,1},{1,2},{2,3},{3,4},{4,5},{5,6},{6,7},{8,9},{9,10},{10,11},{11... | collective-permute-start | bytes 147464 | tf_op jit(solution)/shard_map/ppermute | solution.py:422
  27.1 3.7 %copy-start = (f32[3,192,32,128]{3,2,1,0:T(8,128)S(1)}, f32[3,192,32,128]{3,2,1,0:T(8,128)}, u32[]{:S(2)}) copy-start(f32[3,192,32,128]{3,2,1,0:T(8,128)} %after.1) | copy-start | bytes 28311556
  30.8 0.7 copy-start.6
  31.5 165.9 %copy-start.7 = (f32[5,192]{1,0:T(8,128)S(1)}, f32[5,192]{1,0:T(8,128)}, u32[]{:S(2)}) copy-start(f32[5,192]{1,0:T(8,128)} %coefficients.1.co) | copy-start | bytes 11524
  46.4 3.7 %copy-start.1 = (f32[3,192,32,128]{3,2,1,0:T(8,128)}, f32[3,192,32,128]{3,2,1,0:T(8,128)S(1)}, u32[]{:S(2)}) copy-start(f32[3,192,32,128]{3,2,1,0:T(8,128)S(1)} %get-tuple-element.18.adv_part) | copy-start | bytes 28311556
  50.2 3.7 %copy-start.3 = (f32[3,192,32,128]{3,2,1,0:T(8,128)}, f32[3,192,32,128]{3,2,1,0:T(8,128)S(1)}, u32[]{:S(2)}) copy-start(f32[3,192,32,128]{3,2,1,0:T(8,128)S(1)} %get-tuple-element.19.u_part) | copy-start | bytes 28311556
  53.9 0.6 copy-start.9
  54.5 0.6 copy-start.10
  55.2 0.7 copy-start.11
  55.2 0.8 copy-start.12
  197.4 3.7 %copy-start.2 = (f32[3,192,32,128]{3,2,1,0:T(8,128)S(1)}, f32[3,192,32,128]{3,2,1,0:T(8,128)}, u32[]{:S(2)}) copy-start(f32[3,192,32,128]{3,2,1,0:T(8,128)} %copy-done.1) | copy-start | bytes 28311556
  201.1 3.7 %copy-start.4 = (f32[3,192,32,128]{3,2,1,0:T(8,128)S(1)}, f32[3,192,32,128]{3,2,1,0:T(8,128)}, u32[]{:S(2)}) copy-start(f32[3,192,32,128]{3,2,1,0:T(8,128)} %copy-done.3) | copy-start | bytes 28311556

commit v2 on v1

v2 whole, which is shorter than its diff:
```python
import functools

import jax
import jax.numpy as jnp
import numpy as np
from jax import lax
from jax.experimental import pallas as pl
from jax.experimental.pallas import tpu as pltpu
from jax.sharding import PartitionSpec as P

STIFF = 1024
GAMMA = 5.0 / 12.0
ZETA = -17.0 / 60.0
WEIGHTS = (672.0, -168.0, 32.0, -3.0)
UNIT = 1.0 / 840.0
F32 = jnp.float32
BF16 = jnp.bfloat16
MIB = 1 << 20

INV_GAP, FORWARD, BACKWARD, PSI, PHI = range(5)


def shift_matrix(size, periodic):
    m = np.zeros((size, size), np.float32)
    for j in range(size):
        for k, w in enumerate(WEIGHTS, 1):
            for i, s in ((j + k, w), (j - k, -w)):
                if periodic:
                    m[i % size, j] += s
                elif 0 <= i < size:
                    m[i, j] += s
    return m


def split(values):
    hi = values.astype(BF16)
    return hi, (values - hi.astype(F32)).astype(BF16)


def sublanes(shape):
    return lax.broadcasted_iota(jnp.int32, shape, len(shape) - 2)


def smem():
    return pl.BlockSpec(memory_space=pltpu.SMEM)


def vmem():
    return pl.BlockSpec(memory_space=pltpu.VMEM)


def limit(mib):
    return pltpu.CompilerParams(vmem_limit_bytes=mib * MIB)


def held(shape):
    return pltpu.VMEM(shape, F32)


def pack_kernel(group, v_hbm, pick_ref, vel, left_ref, right_ref, bottom_ref, top_ref, sems):
    n = vel.shape[1]
    pairs = n // (2 * group)

    def copy(p):
        rows = pl.ds(p * 2 * group, 2 * group)
        return pltpu.make_async_copy(v_hbm.at[:, rows], vel.at[:, rows], sems.at[p])

    for p in range(pairs):
        copy(p).start()
    rows = group * 32
    low = sublanes((8, rows)) < 4
    for p in range(pairs):
        copy(p).wait()
        for c in range(3):
            picked = []
            for h in range(2):
                f = vel[c, pl.ds((2 * p + h) * group, group)].reshape(rows, 128)
                pair = jnp.concatenate(split(f), axis=1)
                picked.append(
                    lax.dot_general(pick_ref[...], pair, (((1,), (1,)), ((), ())),
                                    preferred_element_type=F32)
                )
            one, two = picked
            right_ref[c, p] = jnp.where(low, one[:8], two[8:])
            left_ref[c, p] = jnp.where(low, one[8:], two[:8])
    for c in range(3):
        bottom_ref[c, 0] = vel[c, 0]
        top_ref[c, 0] = vel[c, n - 1]


def pack(velocity, group):
    n = velocity.shape[1]
    pick = np.zeros((16, 256), np.float32)
    edge = [124, 125, 126, 127, 0, 1, 2, 3]
    for r, lane in enumerate(edge + edge[4:] + edge[:4]):
        pick[r, lane] = pick[r, 128 + lane] = 1.0
    pairs = n // (2 * group)
    packed = jax.ShapeDtypeStruct((3, pairs, 8, group * 32), F32)
    row = jax.ShapeDtypeStruct((3, 1, 32, 128), F32)
    return pl.pallas_call(
        functools.partial(pack_kernel, group),
        in_specs=[pl.BlockSpec(memory_space=pltpu.HBM), vmem()],
        out_specs=[vmem()] * 5,
        out_shape=[held(velocity.shape), packed, packed, row, row],
        scratch_shapes=[pltpu.SemaphoreType.DMA((pairs,))],
        compiler_params=limit(8),
        name="pack_edges",
    )(pltpu.with_memory_space_constraint(velocity, pltpu.HBM), jnp.asarray(pick, BF16))


def coef_kernel(n, group, lower_ref, upper_ref, kappa_ref, inv_ref, out_ref, wide_ref):
    def up(i, state):
        phi, flux = state
        out_ref[PHI, i] = phi
        out_ref[FORWARD, i] = phi * kappa_ref[i]
        out_ref[INV_GAP, i] = inv_ref[i]
        flux = flux + kappa_ref[i] * phi
        return phi + upper_ref[i] * flux, flux

    def down(k, state):
        i = n - 1 - k
        psi, flux = state
        out_ref[PSI, i] = psi
        out_ref[BACKWARD, i] = psi * kappa_ref[i]
        flux = flux + kappa_ref[i] * psi
        return psi + lower_ref[i] * flux, flux

    def both(i, state):
        return up(i, state[0]), down(i, state[1])

    start = ((lower_ref[0], jnp.float32(1.0)), (upper_ref[n - 1], jnp.float32(1.0)))
    (wronskian, _), _ = lax.fori_loop(0, n, both, start, unroll=4)
    scale = (1.0 / jnp.full((8, 128), wronskian, F32))[0, 0]

    def norm(i, _):
        out_ref[PHI, i] = out_ref[PHI, i] * scale
        out_ref[PSI, i] = out_ref[PSI, i] * scale
        return 0

    lax.fori_loop(0, n, norm, 0, unroll=4)

    shape = (8, group * 32)
    place = lax.broadcasted_iota(jnp.int32, shape, 1) // 32
    low = sublanes(shape) < 4

    def widen(p, _):
        for t, row in enumerate((FORWARD, BACKWARD, PSI, PHI)):
            halves = []
            for h in range(2):
                value = jnp.zeros(shape, F32)
                for y in range(group):
                    value = jnp.where(place == y, out_ref[row, (2 * p + h) * group + y], value)
                halves.append(value)
            wide_ref[t, p] = jnp.where(low, *halves)
        return 0

    lax.fori_loop(0, n // (2 * group), widen, 0)


def coefs(lower_gap, upper_gap, group):
    n = lower_gap.shape[0]
    gap_sum = lower_gap + upper_gap
    return pl.pallas_call(
        functools.partial(coef_kernel, n, group),
        in_specs=[smem()] * 4,
        out_specs=[smem(), vmem()],
        out_shape=[jax.ShapeDtypeStruct((5, n), F32), held((4, n // (2 * group), 8, group * 32))],
        compiler_params=limit(2),
        name="coefficients",
    )(lower_gap, upper_gap, gap_sum * (0.5 / STIFF), 1.0 / gap_sum)


def main_kernel(n, block, group, co, vel_ref, below_ref, above_ref, old_ref, dx_ref, dz_ref,
                adv_ref, u_ref, a_ref, b_ref, f_ref):
    step = pl.program_id(0)
    steps = pl.num_programs(0)

    @pl.when(step == 0)
    def _():
        a_ref[...] = jnp.zeros_like(a_ref)

    rows = group * 32

    def chunk(k, _):
        y0 = k * group
        i0 = step * block + y0
        vel = [vel_ref[c, pl.ds(i0, group)].reshape(rows, 128) for c in range(3)]
        for c in range(3):
            f = vel[c]
            pair = jnp.concatenate(split(f), axis=1)
            along_x = jnp.dot(pair, dx_ref[...], preferred_element_type=F32)
            both = jnp.dot(dz_ref[...], pair, preferred_element_type=F32)
            along_z = both[:, :128] + both[:, 128:]
            below = jnp.where(i0 == 0, below_ref[c, 0], vel_ref[c, jnp.maximum(i0 - 1, 0)])
            above = jnp.where(i0 == n - group, above_ref[c, 0], vel_ref[c, jnp.minimum(i0 + group, n - 1)])
            acc = a_ref[c]
            for y in range(group):
                here = slice(32 * y, 32 * y + 32)
                i = i0 + y
                under = below if y == 0 else f[32 * y - 32 : 32 * y]
                over = above if y == group - 1 else f[32 * y + 32 : 32 * y + 64]
                flat = (vel[0][here] * along_x[here] + vel[2][here] * along_z[here]) * (-UNIT)
                adv = flat - vel[1][here] * ((over - under) * co[INV_GAP, i])
                force = f[here] + GAMMA * adv + ZETA * old_ref[c, y0 + y]
                acc = acc + co[FORWARD, i] * force
                adv_ref[c, i] = adv
                f_ref[c, i] = force
                u_ref[c, i] = co[PSI, i] * acc
            a_ref[c] = acc
        return 0

    lax.fori_loop(0, block // group, chunk, 0)

    @pl.when(step == steps - 1)
    def _():
        b_ref[...] = jnp.zeros_like(b_ref)

        def back(k, _):
            for c in range(3):
                acc = b_ref[c]
                for y in range(group):
                    i = n - 1 - k * group - y
                    u_ref[c, i] = u_ref[c, i] + co[PHI, i] * acc
                    acc = acc + co[BACKWARD, i] * f_ref[c, i]
                b_ref[c] = acc
            return 0

        lax.fori_loop(0, n // group, back, 0)


def main_part(vel, below, above, old, table, group, block):
    n = vel.shape[1]
    dx = shift_matrix(128, False)
    dx = jnp.asarray(np.concatenate([dx, dx]), BF16)
    dz = jnp.asarray(np.kron(np.eye(group), shift_matrix(32, True).T), BF16)
    return pl.pallas_call(
        functools.partial(main_kernel, n, block, group),
        grid=(n // block,),
        in_specs=[smem(), vmem(), vmem(), vmem(),
                  pl.BlockSpec((3, block, 32, 128), lambda i: (0, i, 0, 0)), vmem(), vmem()],
        out_specs=[vmem()] * 4,
        out_shape=[held(vel.shape), held(vel.shape), held((3, 32, 128)), held((3, 32, 128))],
        scratch_shapes=[held(vel.shape)],
        compiler_params=limit(18),
        name="inner_part",
    )(table, vel, below, above, pltpu.with_memory_space_constraint(old, pltpu.HBM), dx, dz)


def edge_kernel(pairs, group, co, from_left, from_right, left_ref, right_ref, a_ref, b_ref, wide_ref,
                sums_ref, place_ref, extra_ref, load_ref):
    n = 2 * pairs * group
    rows = group * 32
    shape = (pairs, 8, rows)
    sub = sublanes((1, 8, rows))
    low = sub < 4
    quarter = sub & 3

    def swap(x):
        return pltpu.roll(x, 4, x.ndim - 2)

    adv, u, a_total, b_total = {}, {}, {}, {}
    for side, halo, own in ((0, from_left, left_ref), (1, from_right, right_ref)):
        for c in range(3):
            h = halo[c]
            slope = jnp.zeros(shape, F32)
            for d in range(4):
                w = WEIGHTS[3 - d] * UNIT
                if side == 0:
                    weight = jnp.where(quarter + d < 4, -w, 0.0)
                    turned = pltpu.roll(h, 8 - d, 1) if d else h
                else:
                    weight = jnp.where(quarter >= d, w, 0.0)
                    turned = pltpu.roll(h, d, 1) if d else h
                slope = slope + weight * turned
            adv[side, c] = -own[0] * slope
            force = GAMMA * adv[side, c]

            def sums(weighted, which):
                hi, lo = split(weighted.reshape(pairs * 8, rows))
                both = []
                for m in (sums_ref[which], sums_ref[2]):
                    both.append(
                        (jnp.dot(hi, m, preferred_element_type=F32)
                         + jnp.dot(lo, m, preferred_element_type=F32)).reshape(shape)
                    )
                return both

            part, total = sums(wide_ref[0] * force, 0)
            carry = jnp.zeros((8, rows), F32)
            first = []
            for p in range(pairs):
                other = swap(total[p])
                first.append(part[p] + carry + jnp.where(low[0], 0.0, other))
                carry = carry + total[p] + other
            a_total[side, c] = carry
            part, total = sums(wide_ref[1] * force, 1)
            carry = jnp.zeros((8, rows), F32)
            values = [None] * pairs
            for p in reversed(range(pairs)):
                other = swap(total[p])
                second = part[p] + carry + jnp.where(low[0], other, 0.0)
                values[p] = wide_ref[2, p] * first[p] + wide_ref[3, p] * second
                carry = carry + total[p] + other
            b_total[side, c] = carry
            u[side, c] = values

    low = low[0]
    for c in range(3):
        for p in range(pairs):
            for t, (l, r) in enumerate(((u[0, c][p], u[1, c][p]), (adv[0, c][p], adv[1, c][p]))):
                for h, value in ((0, jnp.where(low, l, swap(r))), (1, jnp.where(low, swap(l), r))):
                    extra_ref[c, 2 * p + h, pl.ds(16 * t, 16)] = jnp.concatenate(split(value), axis=0)
        for t, (main, extra, row, i) in enumerate(
            ((b_ref, b_total, PHI, 0), (a_ref, a_total, PSI, n - 1))
        ):
            value = jnp.where(low, extra[0, c], extra[1, c])[:, :32]
            value = jnp.concatenate(split(value), axis=0)
            spread = lax.dot_general(value, place_ref[...], (((0,), (0,)), ((), ())),
                                     preferred_element_type=F32)
            load_ref[pl.ds(t * 96 + c * 32, 32), :] = (main[c] + spread) * co[row, i]
    row = sublanes((8, 128))
    ends = jnp.where(row == 0, co[PSI, 0], co[PSI, n - 1])
    ends = jnp.where(row == 2, co[PHI, 0], ends)
    load_ref[192:200, :] = jnp.where(row == 3, co[PHI, n - 1], ends)


def place_matrix():
    m = np.zeros((16, 128), np.float32)
    for r, lane in enumerate([0, 1, 2, 3, 124, 125, 126, 127]):
        m[r, lane] = m[r + 8, lane] = 1.0
    return m


def edge_part(from_left, from_right, left, right, a_sum, b_sum, table, wide, group):
    pairs = left.shape[1]
    each = np.eye(32)
    ones = np.ones((group, group))
    sums = np.stack([np.kron(np.triu(ones), each), np.kron(np.tril(ones, -1), each), np.kron(ones, each)])
    return pl.pallas_call(
        functools.partial(edge_kernel, pairs, group),
        in_specs=[smem()] + [vmem()] * 9,
        out_specs=[vmem()] * 2,
        out_shape=[pltpu.VMEM((3, 2 * pairs, 32, group * 32), BF16), jax.ShapeDtypeStruct((200, 128), F32)],
        compiler_params=limit(12),
        name="edge_part",
    )(table, from_left, from_right, left, right, a_sum, b_sum, wide, jnp.asarray(sums, BF16),
      jnp.asarray(place_matrix(), BF16))


def couple(parts, mine, loads, below_ref, above_ref):
    def read(i):
        first, last = loads[i, 0:96, :], loads[i, 96:192, :]
        return (first, last) + tuple(loads[i, 192 + t : 193 + t, :] for t in range(4))

    def up(i, state):
        a, r = state
        first, last, psi_f, psi_l, phi_f, phi_l = read(i)
        share = psi_l * r / (1.0 - psi_f * r)
        return last + psi_l * a + share * (first + psi_f * a), phi_l + share * phi_f

    def down(k, state):
        b, q = state
        first, last, psi_f, psi_l, phi_f, phi_l = read(parts - 1 - k)
        share = phi_f * q / (1.0 - phi_l * q)
        return first + phi_f * b + share * (last + phi_l * b), psi_f + share * psi_l

    zero = (jnp.zeros((96, 128), F32), jnp.zeros((1, 128), F32))
    a, r = lax.fori_loop(0, mine, up, zero)
    b, q = lax.fori_loop(0, parts - 1 - mine, down, zero)
    first, last, psi_f, psi_l, phi_f, phi_l = read(mine)
    a_next, r_next = up(mine, (a, r))
    above = (b + q * a_next) / (1.0 - q * r_next)
    u_first = (first + psi_f * a + phi_f * above) / (1.0 - psi_f * r)
    above_ref[...] = above
    below_ref[...] = a + r * u_first


def final_kernel(parts, block, group, me, co, loads, adv_part, u_part, extra_ref, place_ref,
                 u_ref, adv_ref, below_ref, above_ref):
    step = pl.program_id(0)

    @pl.when(step == 0)
    def _():
        couple(parts, me[0], loads, below_ref, above_ref)

    for c in range(3):
        below = below_ref[32 * c : 32 * c + 32, :]
        above = above_ref[32 * c : 32 * c + 32, :]
        for k in range(block // group):
            g = step * (block // group) + k
            spread = lax.dot_general(extra_ref[c, g], place_ref[...], (((0,), (0,)), ((), ())),
                                     preferred_element_type=F32)
            for y in range(group):
                i = g * group + y
                here = slice(32 * y, 32 * y + 32)
                value = u_part[c, i] + co[PSI, i] * below + co[PHI, i] * above
                u_ref[c, k * group + y] = value + spread[here, :128]
                adv_ref[c, k * group + y] = adv_part[c, i] + spread[here, 128:]


def final_part(loads, me, table, adv_part, u_part, extra, group, block):
    parts = loads.shape[0]
    n = adv_part.shape[1]
    whole = jax.ShapeDtypeStruct((3, n, 32, 128), F32)
    tile = pl.BlockSpec((3, block, 32, 128), lambda i: (0, i, 0, 0))
    place = jnp.asarray(np.kron(np.eye(2), place_matrix()), BF16)
    return pl.pallas_call(
        functools.partial(final_kernel, parts, block, group),
        grid=(n // block,),
        in_specs=[smem(), smem()] + [vmem()] * 5,
        out_specs=[tile, tile],
        out_shape=[whole, whole],
        scratch_shapes=[held((96, 128)), held((96, 128))],
        compiler_params=limit(12),
        name="final_part",
    )(me, table, loads, adv_part, u_part, extra, place)


def shards(velocity, old_advection, lower_gap, upper_gap):
    n = velocity.shape[1]
    group = max(d for d in range(1, 9) if n % (2 * d) == 0)
    nx, ny = lax.axis_size("gx"), lax.axis_size("gy")
    ring = [(i, (i + 1) % nx) for i in range(nx)]
    line = [(i, i + 1) for i in range(ny - 1)]

    vel, left, right, bottom, top = pack(velocity, group)
    from_left = lax.ppermute(right, "gx", ring)
    from_right = lax.ppermute(left, "gx", [(j, i) for i, j in ring])
    below = lax.ppermute(top, "gy", line)
    above = lax.ppermute(bottom, "gy", [(j, i) for i, j in line])
    table, wide = coefs(lower_gap, upper_gap, group)
    adv_part, u_part, a_sum, b_sum = main_part(vel, below, above, old_advection, table, group, 2 * group)
    extra, load = edge_part(from_left, from_right, left, right, a_sum, b_sum, table, wide, group)
    loads = lax.all_gather(load, "gy")
    me = lax.axis_index("gy").astype(jnp.int32).reshape(1)
    return final_part(loads, me, table, adv_part, u_part, extra, group, 2 * group)


def solution(mesh):
    spec = P(None, "gy", None, "gx")
    return jax.shard_map(
        shards,
        mesh=mesh,
        in_specs=(spec, spec, P("gy"), P("gy")),
        out_specs=(spec, spec),
        check_vma=False,
    )
```

time: 219 us -> 76.4 us (0.35)
  Pallas kernels: 170 us -> 40.9 us
  local copies, waits for them, and re-layouts: 22.1 us -> 8.17 us
  blocking collectives: 17 us -> 19.5 us
    pallas_call x4, Pallas kernels: 156 us -> 30.3 us  [the longest x1 16.1 us: main_part(): pl.pallas_call(functools.partial(main_kernel, n, block, group), grid=(n /...]
    unnamed x30 -> x20, local copies, waits for them, and re-layouts: 21.3 us -> 8.17 us
    pallas_call x1, Pallas kernels: 13.9 us -> 10.6 us  [final_part(): pl.pallas_call(functools.partial(final_kernel, parts, block, group), grid...]
    all_gather x1, blocking collectives: 17 us -> 19.5 us  [shards(): loads = lax.all_gather(load, 'gy')]
  transfers between devices with their start and end apart: 4 -> 4, of which waited for: 0 -> 0; matrix products, arithmetic and copies ran while one was open for 1% -> 0% of each run, Pallas kernels for 9% -> 30%
where the time goes in v2:
time: 76.4 us; the launch traced here: 76 us
  Pallas kernels  40.9 us (54%)
  blocking collectives  19.5 us (26%)
  local copies, waits for them, and re-layouts  8.17 us (11%)
  starting transfers between devices  6.64 us (9%)
  between operations  0.81 us (1%)
    all_gather x1, blocking collectives, shards(): loads = lax.all_gather(load, 'gy')  19.5 us
    pallas_call x1, Pallas kernels, main_part(): pl.pallas_call(functools.partial(main_kernel, n, block, group), grid=(n /...  16.1 us
    pallas_call x1, Pallas kernels, final_part(): pl.pallas_call(functools.partial(final_kernel, parts, block, group), grid...  10.6 us
    unnamed x20, local copies, waits for them, and re-layouts  8.17 us
    pallas_call x1, Pallas kernels, coefs(): pl.pallas_call(functools.partial(coef_kernel, n, group), in_specs=[smem()...  6.59 us
    pallas_call x1, Pallas kernels, pack(): pl.pallas_call(functools.partial(pack_kernel, group), in_specs=[pl.BlockS...  5.18 us
    ppermute x1, starting transfers between devices, shards(): from_left = lax.ppermute(right, 'gx', ring)  2.94 us
    pallas_call x1, Pallas kernels, edge_part(): pl.pallas_call(functools.partial(edge_kernel, pairs, group), in_specs=[sm...  2.42 us
  transfers between devices with their start and end apart: 4, of which 0 were waited for; matrix products, arithmetic and copies ran while one was open for 0% of the time, Pallas kernels for 30%

profile of v2, /device:TPU:0, one launch (start us, length us, event | category | flops | bytes accessed | tf_op | source)
XLA Modules:
  0.0 76.0 jit_solution(17661894507852716611)
XLA Ops:
  0.6 0.0 copy-start.3
  0.6 0.0 copy-start.4
  0.7 0.0 copy-start.6
  0.7 0.7 copy-done.6
  1.4 0.0 copy-start.8
  1.4 0.0 copy-start.9
  1.4 5.2 %pack_edges.1 = (f32[3,192,32,128]{3,2,1,0:T(8,128)S(1)}, f32[3,12,8,256]{3,2,1,0:T(8,128)S(1)}, f32[3,12,8,256]{3,2,1,0:T(8,128)S(1)}, f32[3,1,32,128]{3,2,1,0:T(8,128)S(1)}, f32[3,1,32,128]{3,2,1,0:T(8,128)S(1)}) custom-call(f32[3,192,32,128]{3,2,1,0:T(8,128)} %v_hbm.1, bf16[16,256]{1,0:T(8,128)(2,1)S(1)} %copy-done.6), custom_call_target="tpu_custom_call" | custom-call | tf_op jit(solution)/shard_map/pack_edges/pallas_call | solution.py:100
  6.6 0.0 copy-start
  6.6 3.7 %copy-done = f32[3,192,32,128]{3,2,1,0:T(8,128)} copy-done((f32[3,192,32,128]{3,2,1,0:T(8,128)}, f32[3,192,32,128]{3,2,1,0:T(8,128)S(1)}, u32[]{:S(2)}) %copy-start) | copy-done | bytes 9437208
  10.3 2.9 %collective-permute-start = (f32[3,12,8,256]{3,2,1,0:T(8,128)S(1)}, f32[3,12,8,256]{3,2,1,0:T(8,128)S(1)}, u32[]{:S(2)}, u32[]{:S(2)}) collective-permute-start(f32[3,12,8,256]{3,2,1,0:T(8,128)S(1)} %get-tuple-element.16.right_ref), channel_id=1, source_target_pairs={{0,8},{8,16},{16,24},{24,0},{1,9},{9,17},{17,25},{25,1},{2,10},{10... | collective-permute-start | bytes 884744 | tf_op jit(solution)/shard_map/ppermute | solution.py:427
  13.3 1.0 %collective-permute-start.1 = (f32[3,12,8,256]{3,2,1,0:T(8,128)S(1)}, f32[3,12,8,256]{3,2,1,0:T(8,128)S(1)}, u32[]{:S(2)}, u32[]{:S(2)}) collective-permute-start(f32[3,12,8,256]{3,2,1,0:T(8,128)S(1)} %get-tuple-element.17.left_ref), channel_id=1, source_target_pairs={{8,0},{16,8},{24,16},{0,24},{9,1},{17,9},{25,17},{1,25},{10,2},{18... | collective-permute-start | bytes 884744 | tf_op jit(solution)/shard_map/ppermute | solution.py:428
  14.2 1.4 %collective-permute-start.2 = (f32[3,1,32,128]{3,2,1,0:T(8,128)S(1)}, f32[3,1,32,128]{3,2,1,0:T(8,128)S(1)}, u32[]{:S(2)}, u32[]{:S(2)}) collective-permute-start(f32[3,1,32,128]{3,2,1,0:T(8,128)S(1)} %get-tuple-element.19), channel_id=1, source_target_pairs={{0,1},{1,2},{2,3},{3,4},{4,5},{5,6},{6,7},{8,9},{9,10},{10,11},{11... | collective-permute-start | bytes 147464 | tf_op jit(solution)/shard_map/ppermute | solution.py:429
  15.7 1.3 %collective-permute-start.3 = (f32[3,1,32,128]{3,2,1,0:T(8,128)S(1)}, f32[3,1,32,128]{3,2,1,0:T(8,128)S(1)}, u32[]{:S(2)}, u32[]{:S(2)}) collective-permute-start(f32[3,1,32,128]{3,2,1,0:T(8,128)S(1)} %get-tuple-element.20), channel_id=1, source_target_pairs={{1,0},{2,1},{3,2},{4,3},{5,4},{6,5},{7,6},{9,8},{10,9},{11,10},{12... | collective-permute-start | bytes 147464 | tf_op jit(solution)/shard_map/ppermute | solution.py:430
  17.0 0.0 copy-done.8
  17.0 0.0 copy-done.9
  17.0 6.6 %coefficients.1 = (f32[5,192]{1,0:T(8,128)S(1)}, f32[4,12,8,256]{3,2,1,0:T(8,128)S(1)}) custom-call(f32[192]{0:T(256)S(1)} %copy-done.8, f32[192]{0:T(256)S(1)} %copy-done.9, f32[192]{0:T(256)S(1)} %get-tuple-element.29.kappa_ref, f32[192]{0:T(256)S(1)} %get-tuple-element.28.inv_ref), custom_call_target="tpu_custom_call" | custom-call | tf_op jit(solution)/shard_map/coefficients/pallas_call | solution.py:163
  23.6 0.0 collective-permute-done.2.below_ref
  23.6 0.0 collective-permute-done.3.above_ref
  23.6 0.0 copy-done.3
  23.7 0.0 copy-done.4
  23.7 0.0 copy-start.1
  23.7 3.7 %copy-done.1 = f32[3,192,32,128]{3,2,1,0:T(8,128)S(1)} copy-done((f32[3,192,32,128]{3,2,1,0:T(8,128)S(1)}, f32[3,192,32,128]{3,2,1,0:T(8,128)}, u32[]{:S(2)}) %copy-start.1) | copy-done | bytes 9437208
  27.4 0.0 copy-start.2
  27.4 0.0 copy-start.7
  27.4 0.0 copy-start.5
  27.4 16.1 %inner_part.1 = (f32[3,192,32,128]{3,2,1,0:T(8,128)S(1)}, f32[3,192,32,128]{3,2,1,0:T(8,128)S(1)}, f32[3,32,128]{2,1,0:T(8,128)S(1)}, f32[3,32,128]{2,1,0:T(8,128)S(1)}) custom-call(f32[5,192]{1,0:T(8,128)S(1)} %get-tuple-element.15.co, f32[3,192,32,128]{3,2,1,0:T(8,128)S(1)} %copy-done.1, f32[3,1,32,128]{3,2,1,0:T(8,128)S(1)} %collective-permute-done.2.below_ref, ...), custom_call_target="tpu_custom_call" | custom-call | tf_op jit(solution)/shard_map/inner_part/pallas_call | solution.py:236
  43.5 0.0 collective-permute-done.from_left
  43.5 0.0 collective-permute-done.1.from_right
  43.5 0.0 copy-done.2
  43.5 0.0 copy-done.7
  43.5 2.4 %edge_part.1 = (bf16[3,24,32,256]{3,2,1,0:T(8,128)(2,1)S(1)}, f32[200,128]{1,0:T(8,128)S(1)}) custom-call(f32[5,192]{1,0:T(8,128)S(1)} %get-tuple-element.15.co, f32[3,12,8,256]{3,2,1,0:T(8,128)S(1)} %collective-permute-done.from_left, f32[3,12,8,256]{3,2,1,0:T(8,128)S(1)} %collective-permute-done.1.from_right, ...), custom_call_target="tpu_custom_call" | custom-call | tf_op jit(solution)/shard_map/edge_part/pallas_call | solution.py:339
  45.9 19.5 %all-gather = f32[1600,128]{1,0:T(8,128)S(1)} all-gather(f32[200,128]{1,0:T(8,128)S(1)} %get-tuple-element.24), channel_id=2, replica_groups=mesh['gx'=4,'gy'=8] {'gy'}, dimensions={0}, use_global_device_ids=true | all-gather | bytes 921600 | tf_op jit(solution)/shard_map/all_gather | solution.py:434
  65.4 0.0 copy-done.5
  65.4 10.6 %final_part.1 = (f32[3,192,32,128]{3,2,1,0:T(8,128)}, f32[3,192,32,128]{3,2,1,0:T(8,128)}) custom-call(s32[1]{0:T(128)} %bitcast.me, f32[5,192]{1,0:T(8,128)S(1)} %get-tuple-element.15.co, f32[8,200,128]{2,1,0:T(8,128)S(1)} %bitcast.2, f32[3,192,32,128]{3,2,1,0:T(8,128)S(1)} %get-tuple-element.25.adv_part, f32[3,192,32,128]{3,2,1,0:T(8,128)S(1)} %get-tuple-element.26.u_part, ...), custom_call_target="tpu_custom_call" | custom-call | tf_op jit(solution)/shard_map/final_part/pallas_call | solution.py:407
  (1 shorter events, 0.0 us)
Async XLA Ops:
  0.6 23.0 %copy-start.3 = (bf16[256,256]{1,0:T(8,128)(2,1)S(1)}, bf16[256,256]{1,0:T(8,128)(2,1)}, u32[]{:S(2)}) copy-start(bf16[256,256]{1,0:T(8,128)(2,1)} %constant.22.clone.dz_ref) | copy-start | bytes 393220
  0.6 23.0 %copy-start.4 = (bf16[256,128]{1,0:T(8,128)(2,1)S(1)}, bf16[256,128]{1,0:T(8,128)(2,1)}, u32[]{:S(2)}) copy-start(bf16[256,128]{1,0:T(8,128)(2,1)} %constant.21.clone.dx_ref) | copy-start | bytes 196612
  0.7 0.7 copy-start.6
  1.4 15.6 %copy-start.8 = (f32[192]{0:T(256)S(1)}, f32[192]{0:T(256)}, u32[]{:S(2)}) copy-start(f32[192]{0:T(256)} %lower_ref.1) | copy-start | bytes 2308
  1.4 15.6 %copy-start.9 = (f32[192]{0:T(256)S(1)}, f32[192]{0:T(256)}, u32[]{:S(2)}) copy-start(f32[192]{0:T(256)} %upper_ref.1) | copy-start | bytes 2308
  6.6 3.7 %copy-start = (f32[3,192,32,128]{3,2,1,0:T(8,128)}, f32[3,192,32,128]{3,2,1,0:T(8,128)S(1)}, u32[]{:S(2)}) copy-start(f32[3,192,32,128]{3,2,1,0:T(8,128)S(1)} %get-tuple-element.18.vel_ref) | copy-start | bytes 28311556
  10.3 33.1 %collective-permute-start = (f32[3,12,8,256]{3,2,1,0:T(8,128)S(1)}, f32[3,12,8,256]{3,2,1,0:T(8,128)S(1)}, u32[]{:S(2)}, u32[]{:S(2)}) collective-permute-start(f32[3,12,8,256]{3,2,1,0:T(8,128)S(1)} %get-tuple-element.16.right_ref), channel_id=1, source_target_pairs={{0,8},{8,16},{16,24},{24,0},{1,9},{9,17},{17,25},{25,1},{2,10},{10... | collective-permute-start | bytes 884744 | tf_op jit(solution)/shard_map/ppermute | solution.py:427
  13.3 30.2 %collective-permute-start.1 = (f32[3,12,8,256]{3,2,1,0:T(8,128)S(1)}, f32[3,12,8,256]{3,2,1,0:T(8,128)S(1)}, u32[]{:S(2)}, u32[]{:S(2)}) collective-permute-start(f32[3,12,8,256]{3,2,1,0:T(8,128)S(1)} %get-tuple-element.17.left_ref), channel_id=1, source_target_pairs={{8,0},{16,8},{24,16},{0,24},{9,1},{17,9},{25,17},{1,25},{10,2},{18... | collective-permute-start | bytes 884744 | tf_op jit(solution)/shard_map/ppermute | solution.py:428
  14.2 9.4 %collective-permute-start.2 = (f32[3,1,32,128]{3,2,1,0:T(8,128)S(1)}, f32[3,1,32,128]{3,2,1,0:T(8,128)S(1)}, u32[]{:S(2)}, u32[]{:S(2)}) collective-permute-start(f32[3,1,32,128]{3,2,1,0:T(8,128)S(1)} %get-tuple-element.19), channel_id=1, source_target_pairs={{0,1},{1,2},{2,3},{3,4},{4,5},{5,6},{6,7},{8,9},{9,10},{10,11},{11... | collective-permute-start | bytes 147464 | tf_op jit(solution)/shard_map/ppermute | solution.py:429
  15.7 8.0 %collective-permute-start.3 = (f32[3,1,32,128]{3,2,1,0:T(8,128)S(1)}, f32[3,1,32,128]{3,2,1,0:T(8,128)S(1)}, u32[]{:S(2)}, u32[]{:S(2)}) collective-permute-start(f32[3,1,32,128]{3,2,1,0:T(8,128)S(1)} %get-tuple-element.20), channel_id=1, source_target_pairs={{1,0},{2,1},{3,2},{4,3},{5,4},{6,5},{7,6},{9,8},{10,9},{11,10},{12... | collective-permute-start | bytes 147464 | tf_op jit(solution)/shard_map/ppermute | solution.py:430
  23.7 3.7 %copy-start.1 = (f32[3,192,32,128]{3,2,1,0:T(8,128)S(1)}, f32[3,192,32,128]{3,2,1,0:T(8,128)}, u32[]{:S(2)}) copy-start(f32[3,192,32,128]{3,2,1,0:T(8,128)} %copy-done) | copy-start | bytes 28311556
  27.4 16.1 %copy-start.2 = (bf16[3,256,256]{2,1,0:T(8,128)(2,1)S(1)}, bf16[3,256,256]{2,1,0:T(8,128)(2,1)}, u32[]{:S(2)}) copy-start(bf16[3,256,256]{2,1,0:T(8,128)(2,1)} %constant.23.clone.sums_ref) | copy-start | bytes 1179652
  27.4 16.1 %copy-start.7 = (bf16[16,128]{1,0:T(8,128)(2,1)S(1)}, bf16[16,128]{1,0:T(8,128)(2,1)}, u32[]{:S(2)}) copy-start(bf16[16,128]{1,0:T(8,128)(2,1)} %constant.24.clone.place_ref) | copy-start | bytes 12292
  27.4 38.0 %copy-start.5 = (bf16[32,256]{1,0:T(8,128)(2,1)S(1)}, bf16[32,256]{1,0:T(8,128)(2,1)}, u32[]{:S(2)}) copy-start(bf16[32,256]{1,0:T(8,128)(2,1)} %constant.25.clone.place_ref) | copy-start | bytes 49156

commit v3 on v2

v3 whole, which is shorter than its diff:
```python
import functools

import jax
import jax.numpy as jnp
import numpy as np
from jax import lax
from jax.experimental import pallas as pl
from jax.experimental.pallas import tpu as pltpu
from jax.sharding import PartitionSpec as P

STIFF = 1024
GAMMA = 5.0 / 12.0
ZETA = -17.0 / 60.0
WEIGHTS = (672.0, -168.0, 32.0, -3.0)
UNIT = 1.0 / 840.0
F32 = jnp.float32
BF16 = jnp.bfloat16
MIB = 1 << 20

INV_GAP, FORWARD, BACKWARD, PSI, PHI, OWN, NEXT = range(7)


def shift_matrix(size, periodic):
    m = np.zeros((size, size), np.float32)
    for j in range(size):
        for k, w in enumerate(WEIGHTS, 1):
            for i, s in ((j + k, w), (j - k, -w)):
                if periodic:
                    m[i % size, j] += s
                elif 0 <= i < size:
                    m[i, j] += s
    return m


def split(values):
    hi = values.astype(BF16)
    return hi, (values - hi.astype(F32)).astype(BF16)


def sublanes(shape):
    return lax.broadcasted_iota(jnp.int32, shape, len(shape) - 2)


def smem():
    return pl.BlockSpec(memory_space=pltpu.SMEM)


def vmem():
    return pl.BlockSpec(memory_space=pltpu.VMEM)


def limit(mib):
    return pltpu.CompilerParams(vmem_limit_bytes=mib * MIB)


def cost(flops, moved=0):
    return pl.CostEstimate(flops=int(flops), bytes_accessed=int(moved), transcendentals=0)


def held(shape):
    return pltpu.VMEM(shape, F32)


def pack_kernel(group, v_hbm, vel, left_ref, right_ref, bottom_ref, top_ref, sems):
    n = vel.shape[1]
    pairs = n // (2 * group)

    def copy(p):
        rows = pl.ds(p * 2 * group, 2 * group)
        return pltpu.make_async_copy(v_hbm.at[:, rows], vel.at[:, rows], sems.at[p])

    for p in range(pairs):
        copy(p).start()
    rows = group * 32
    low = sublanes((8, rows)) < 4
    r = lax.broadcasted_iota(jnp.int32, (16, 256), 0)
    lane = lax.broadcasted_iota(jnp.int32, (16, 256), 1) & 127
    inside = jnp.logical_or(r < 4, r >= 12)
    pick = jnp.where(lane == jnp.where(inside, 124, 0) + (r & 3), 1.0, 0.0).astype(BF16)
    for p in range(pairs):
        copy(p).wait()
        for c in range(3):
            picked = []
            for h in range(2):
                f = vel[c, pl.ds((2 * p + h) * group, group)].reshape(rows, 128)
                pair = jnp.concatenate(split(f), axis=1)
                picked.append(
                    lax.dot_general(pick, pair, (((1,), (1,)), ((), ())), preferred_element_type=F32)
                )
            one, two = picked
            right_ref[c, p] = jnp.where(low, one[:8], two[8:])
            left_ref[c, p] = jnp.where(low, one[8:], two[:8])
    for c in range(3):
        bottom_ref[c, 0] = vel[c, 0]
        top_ref[c, 0] = vel[c, n - 1]


def pack(velocity, group):
    n = velocity.shape[1]
    pairs = n // (2 * group)
    packed = jax.ShapeDtypeStruct((3, pairs, 8, group * 32), F32)
    row = jax.ShapeDtypeStruct((3, 1, 32, 128), F32)
    return pl.pallas_call(
        functools.partial(pack_kernel, group),
        in_specs=[pl.BlockSpec(memory_space=pltpu.HBM)],
        out_specs=[vmem()] * 5,
        out_shape=[held(velocity.shape), packed, packed, row, row],
        scratch_shapes=[pltpu.SemaphoreType.DMA((pairs,))],
        compiler_params=limit(8),
        cost_estimate=cost(velocity.size, 4 * velocity.size),
        name="pack_edges",
    )(pltpu.with_memory_space_constraint(velocity, pltpu.HBM))


def coef_kernel(n, group, lower_ref, upper_ref, out_ref, wide_ref, gap_ref):
    width = out_ref.shape[1]
    shape = (8, width)
    lane = lax.broadcasted_iota(jnp.int32, shape, 1)
    gap_ref[...] = jnp.ones_like(gap_ref)
    gap_ref[0:8, 0:n] = jnp.broadcast_to(lower_ref[...].reshape(1, n), (8, n))
    gap_ref[8:16, 0:n] = jnp.broadcast_to(upper_ref[...].reshape(1, n), (8, n))
    lower, upper = gap_ref[0:8, :], gap_ref[8:16, :]
    gap_sum = lower + upper
    kappa = gap_sum * (0.5 / STIFF)
    live = lane < n

    def at(values, place):
        return jnp.sum(jnp.where(lane == place, values, 0.0), axis=1, keepdims=True)

    def sweep(gap, start, backward):
        one, zero = jnp.ones(shape, F32), jnp.zeros(shape, F32)
        m = [jnp.where(live, v, w) for v, w in
             ((1.0 + gap * kappa, one), (gap, zero), (kappa, zero), (one, one))]
        s = 1
        while s < n:
            inside = lane < width - s if backward else lane >= s
            turn = width - s if backward else s
            a, b, c, d = (jnp.where(inside, pltpu.roll(v, turn, 1), w)
                          for v, w in zip(m, (one, zero, zero, one)))
            m = [m[0] * a + m[1] * c, m[0] * b + m[1] * d, m[2] * a + m[3] * c, m[2] * b + m[3] * d]
            s *= 2
        return m[0] * start + m[1]

    first, last = at(lower, 0), at(upper, n - 1)
    phi_next = sweep(upper, first, False)
    psi_next = sweep(lower, last, True)
    phi = jnp.where(lane == 0, first, pltpu.roll(phi_next, 1, 1))
    psi = jnp.where(lane == n - 1, last, pltpu.roll(psi_next, width - 1, 1))
    scale = 1.0 / at(phi_next, n - 1)
    forward, backward = phi * kappa, psi * kappa
    out_ref[...] = jnp.zeros_like(out_ref)
    for row, value in ((INV_GAP, 1.0 / gap_sum), (FORWARD, forward), (BACKWARD, backward),
                       (PSI, psi * scale), (PHI, phi * scale), (OWN, upper / phi_next), (NEXT, phi / phi_next)):
        out_ref[row : row + 1, :] = value[0:1]

    pairs, rows = wide_ref.shape[1], wide_ref.shape[3]
    y = lax.broadcasted_iota(jnp.int32, (pairs * 8, width), 1)
    r = lax.broadcasted_iota(jnp.int32, (pairs * 8, width), 0)
    mine = y // group == (r // 8) * 2 + (r & 7) // 4
    fold = (lax.broadcasted_iota(jnp.int32, (width, rows), 0) % group
            == lax.broadcasted_iota(jnp.int32, (width, rows), 1) // 32)
    fold = jnp.where(fold, 1.0, 0.0).astype(BF16)
    for t, value in enumerate((forward, backward)):
        value = jnp.where(live, value, 0.0)
        hi, lo = split(jnp.where(mine, jnp.broadcast_to(value[0:1], mine.shape), 0.0))
        spread = jnp.dot(hi, fold, preferred_element_type=F32) + jnp.dot(lo, fold, preferred_element_type=F32)
        wide_ref[t] = spread.reshape(pairs, 8, rows)


def coefs(lower_gap, upper_gap, group):
    n = lower_gap.shape[0]
    width = -(-n // 128) * 128
    return pl.pallas_call(
        functools.partial(coef_kernel, n, group),
        in_specs=[vmem(), vmem()],
        out_specs=[vmem(), vmem()],
        out_shape=[jax.ShapeDtypeStruct((8, width), F32), held((2, n // (2 * group), 8, group * 32))],
        scratch_shapes=[held((16, width))],
        compiler_params=limit(8),
        cost_estimate=cost(1e5),
        name="coefficients",
    )(lower_gap, upper_gap)


def main_kernel(n, block, group, co, vel_ref, old_ref, dx_ref, dz_ref, adv_ref, sum_ref, b_ref, a_ref):
    step = pl.program_id(0)

    @pl.when(step == 0)
    def _():
        a_ref[...] = jnp.zeros_like(a_ref)
        b_ref[...] = jnp.zeros_like(b_ref)

    rows = group * 32
    nothing = jnp.zeros((32, 128), F32)

    for k in range(block // group):
        y0 = k * group
        i0 = step * block + y0
        vel = [vel_ref[c, pl.ds(i0, group)].reshape(rows, 128) for c in range(3)]
        for c in range(3):
            f = vel[c]
            pair = jnp.concatenate(split(f), axis=1)
            along_x = jnp.dot(pair, dx_ref[...], preferred_element_type=F32)
            both = jnp.dot(dz_ref[...], pair, preferred_element_type=F32)
            along_z = both[:, :128] + both[:, 128:]
            below = jnp.where(i0 == 0, nothing, vel_ref[c, jnp.maximum(i0 - 1, 0)])
            above = jnp.where(i0 == n - group, nothing, vel_ref[c, jnp.minimum(i0 + group, n - 1)])
            up, down = a_ref[c], b_ref[c]
            for y in range(group):
                here = slice(32 * y, 32 * y + 32)
                i = i0 + y
                under = below if y == 0 else f[32 * y - 32 : 32 * y]
                over = above if y == group - 1 else f[32 * y + 32 : 32 * y + 64]
                flat = (vel[0][here] * along_x[here] + vel[2][here] * along_z[here]) * (-UNIT)
                adv = flat - vel[1][here] * ((over - under) * co[INV_GAP, i])
                force = f[here] + GAMMA * adv + ZETA * old_ref[c, y0 + y]
                up = up + co[FORWARD, i] * force
                down = down + co[BACKWARD, i] * force
                adv_ref[c, i] = adv
                sum_ref[c, i] = up
            a_ref[c] = up
            b_ref[c] = down


def main_part(vel, old, table, group, block):
    n = vel.shape[1]
    dx = shift_matrix(128, False)
    dx = jnp.asarray(np.concatenate([dx, dx]), BF16)
    dz = jnp.asarray(np.kron(np.eye(group), shift_matrix(32, True).T), BF16)
    return pl.pallas_call(
        functools.partial(main_kernel, n, block, group),
        grid=(n // block,),
        in_specs=[smem(), vmem(), pl.BlockSpec((3, block, 32, 128), lambda i: (0, i, 0, 0)), vmem(), vmem()],
        out_specs=[vmem()] * 3,
        out_shape=[held(vel.shape), held(vel.shape), held((3, 32, 128))],
        scratch_shapes=[held((3, 32, 128))],
        compiler_params=limit(8),
        cost_estimate=cost(25 * old.size, 4 * old.size),
        name="inner_part",
    )(table, vel, pltpu.with_memory_space_constraint(old, pltpu.HBM), dx, dz)


def place_matrix():
    r = lax.broadcasted_iota(jnp.int32, (16, 128), 0) & 7
    lane = lax.broadcasted_iota(jnp.int32, (16, 128), 1)
    return jnp.where(lane == jnp.where(r < 4, r, r + 120), 1.0, 0.0).astype(BF16)


def spread_planes(value):
    return lax.dot_general(value, place_matrix(), (((0,), (0,)), ((), ())), preferred_element_type=F32)


def edge_kernel(pairs, group, co, from_left, from_right, left_ref, right_ref, sum_ref, b_ref, wide_ref,
                low_ref, high_ref, vel_ref, extra_ref, rim_ref, load_ref):
    n = 2 * pairs * group
    rows = group * 32
    shape = (pairs, 8, rows)
    sub = sublanes((1, 8, rows))
    low = sub[0] < 4
    quarter = sub & 3

    def swap(x):
        return pltpu.roll(x, 4, 0)

    def total(x):
        t = x[0]
        for p in range(1, pairs):
            t = t + x[p]
        t = t + swap(t)
        parts = t[:, 0:32]
        for y in range(1, group):
            parts = parts + t[:, 32 * y : 32 * y + 32]
        return parts

    for c in range(3):
        rims = (vel_ref[1, 0] * low_ref[c, 0] * co[INV_GAP, 0],
                -vel_ref[1, n - 1] * high_ref[c, 0] * co[INV_GAP, n - 1])
        rim_ref[0, c], rim_ref[1, c] = rims
        adv, totals = [], []
        for side, halo, own in ((0, from_left, left_ref), (1, from_right, right_ref)):
            h = halo[c]
            slope = jnp.zeros(shape, F32)
            for d in range(4):
                w = WEIGHTS[3 - d] * UNIT
                if side == 0:
                    weight = jnp.where(quarter + d < 4, -w, 0.0)
                    turned = pltpu.roll(h, 8 - d, 1) if d else h
                else:
                    weight = jnp.where(quarter >= d, w, 0.0)
                    turned = pltpu.roll(h, d, 1) if d else h
                slope = slope + weight * turned
            adv.append(-own[0] * slope)
            force = GAMMA * adv[side]
            totals.append([total(wide_ref[t] * force) for t in range(2)])
        for p in range(pairs):
            l, r = adv[0][p], adv[1][p]
            for h, value in ((0, jnp.where(low, l, swap(r))), (1, jnp.where(low, swap(l), r))):
                extra_ref[c, 2 * p + h] = jnp.concatenate(split(value), axis=0)
        for t, (main, weight, row, i) in enumerate(
            ((b_ref[c], BACKWARD, PHI, 0), (sum_ref[c, n - 1], FORWARD, PSI, n - 1))
        ):
            main = main + (GAMMA * co[weight, 0]) * rims[0] + (GAMMA * co[weight, n - 1]) * rims[1]
            value = jnp.where(low[:, :32], totals[0][1 - t], totals[1][1 - t])
            spread = spread_planes(jnp.concatenate(split(value), axis=0))
            load_ref[pl.ds(t * 96 + c * 32, 32), :] = (main + spread) * co[row, i]
    row = sublanes((8, 128))
    ends = jnp.where(row == 0, co[PSI, 0], co[PSI, n - 1])
    ends = jnp.where(row == 2, co[PHI, 0], ends)
    load_ref[192:200, :] = jnp.where(row == 3, co[PHI, n - 1], ends)


def edge_part(from_left, from_right, left, right, sums, b_sum, wide, low, high, vel, table, group):
    pairs = left.shape[1]
    return pl.pallas_call(
        functools.partial(edge_kernel, pairs, group),
        in_specs=[smem()] + [vmem()] * 10,
        out_specs=[vmem()] * 3,
        out_shape=[pltpu.VMEM((3, 2 * pairs, 16, group * 32), BF16), held((2, 3, 32, 128)),
                   jax.ShapeDtypeStruct((200, 128), F32)],
        compiler_params=limit(8),
        cost_estimate=cost(40 * left.size),
        name="edge_part",
    )(table, from_left, from_right, left, right, sums, b_sum, wide, low, high, vel)


def read(ref):
    return (ref[0:96, :], ref[96:192, :]) + tuple(ref[192 + t : 193 + t, :] for t in range(4))


def write(ref, run):
    ref[0:96, :] = run[0]
    ref[96:192, :] = run[1]
    for t in range(4):
        ref[192 + t : 193 + t, :] = run[2 + t]
    ref[196:200, :] = jnp.zeros((4, 128), F32)


def join(lower, upper):
    f1, l1, pf1, pl1, qf1, ql1 = lower
    f2, l2, pf2, pl2, qf2, ql2 = upper
    inverse = 1.0 / (1.0 - pf2 * ql1)
    over, under = qf1 * inverse, pl2 * inverse
    return (
        f1 + over * (f2 + pf2 * l1),
        l2 + under * (l1 + ql1 * f2),
        pf1 + over * pf2 * pl1,
        under * pl1,
        over * qf2,
        ql2 + under * ql1 * qf2,
    )


def empty():
    zero, one, none = (jnp.zeros((1, 128), F32), jnp.ones((1, 128), F32), jnp.zeros((96, 128), F32))
    return (none, none, zero, one, one, zero)


def join_kernel(bit, opening, closing, all_ref, other_ref, *refs):
    me = lax.axis_index("gy")
    if opening:
        lower_in = upper_in = None
        all_out, lower_out, upper_out = refs[:3]
    else:
        lower_in, upper_in, all_out, lower_out, upper_out = refs[:5]
    lower = empty() if opening else read(lower_in)
    upper = empty() if opening else read(upper_in)
    whole, other = read(all_ref), read(other_ref)

    def send(run):
        if closing:
            above_me = (me & (2 * bit)) != 0
            all_out[0:96, :] = jnp.where(above_me, run[0], run[1])
            all_out[96:104, :] = jnp.broadcast_to(jnp.where(above_me, run[2], run[5]), (8, 128))
        else:
            write(all_out, run)

    @pl.when((me & bit) != 0)
    def _():
        send(join(other, whole))
        write(lower_out, join(other, lower))
        write(upper_out, upper)

    @pl.when((me & bit) == 0)
    def _():
        send(join(whole, other))
        write(lower_out, lower)
        write(upper_out, join(upper, other))


def join_runs(bit, closing, whole, other, around):
    run = jax.ShapeDtypeStruct((200, 128), F32)
    half = jax.ShapeDtypeStruct((104, 128), F32)
    return pl.pallas_call(
        functools.partial(join_kernel, bit, not around, closing),
        in_specs=[vmem()] * (2 + len(around)),
        out_specs=[vmem()] * 3,
        out_shape=[half if closing else run, run, run],
        compiler_params=limit(8),
        cost_estimate=cost(20 * whole.size),
        name="join_runs",
    )(whole, other, *around)


def couple(bit, me, load, other_ref, lower_ref, upper_ref, below_ref, above_ref):
    lower, upper = read(lower_ref), read(upper_ref)
    vector, scalar = other_ref[0:96, :], other_ref[96:97, :]
    none, zero = jnp.zeros((96, 128), F32), jnp.zeros((1, 128), F32)

    def solve(lower, upper):
        _, a, _, _, _, r = lower
        b, _, q, _, _, _ = upper
        first, last, psi_f, psi_l, phi_f, phi_l = read(load)
        share = 1.0 / (1.0 - psi_f * r)
        a_next = last + psi_l * a + psi_l * r * share * (first + psi_f * a)
        r_next = phi_l + psi_l * r * share * phi_f
        above = (b + q * a_next) / (1.0 - q * r_next)
        above_ref[...] = above
        below_ref[...] = a + r * share * (first + psi_f * a + phi_f * above)

    @pl.when((me & bit) != 0)
    def _():
        solve(join((none, vector, zero, zero, zero, scalar), lower), upper)

    @pl.when((me & bit) == 0)
    def _():
        solve(lower, join(upper, (vector, none, scalar, zero, zero, zero)))


def up_kernel(block, group, token, co, adv_part, sum_part, extra_ref, rim_ref, adv_ref, sum_ref, acc_ref):
    step = pl.program_id(0)
    last = pl.num_programs(0) - 1

    @pl.when(step == 0)
    def _():
        acc_ref[...] = (GAMMA * co[FORWARD, 0]) * rim_ref[0]

    for c in range(3):
        acc = acc_ref[c]
        for k in range(block // group):
            g = step * (block // group) + k
            spread = spread_planes(extra_ref[c, g])
            for y in range(group):
                i = g * group + y
                extra = spread[32 * y : 32 * y + 32]
                adv_ref[c, k * group + y] = adv_part[c, i] + extra
                acc = acc + (GAMMA * co[FORWARD, i]) * extra
                sum_ref[c, i] = sum_part[c, i] + acc
        acc_ref[c] = acc

    @pl.when(step == 0)
    def _():
        adv_ref[:, 0] = adv_ref[:, 0] + rim_ref[0]

    @pl.when(step == last)
    def _():
        adv_ref[:, block - 1] = adv_ref[:, block - 1] + rim_ref[1]
        i = (last + 1) * block - 1
        sum_ref[:, i] = sum_ref[:, i] + (GAMMA * co[FORWARD, i]) * rim_ref[1]


def sweep_up(token, table, adv_part, sums, extra, rims, group, block):
    shape = adv_part.shape
    return pl.pallas_call(
        functools.partial(up_kernel, block, group),
        grid=(shape[1] // block,),
        in_specs=[pl.BlockSpec(memory_space=pl.ANY), smem()] + [vmem()] * 4,
        out_specs=[pl.BlockSpec((3, block, 32, 128), lambda i: (0, i, 0, 0)), vmem()],
        out_shape=[jax.ShapeDtypeStruct(shape, F32), held(shape)],
        scratch_shapes=[held((3, 32, 128))],
        compiler_params=limit(8),
        cost_estimate=cost(8 * adv_part.size, 4 * adv_part.size),
        name="sweep_up",
    )(token, table, adv_part, sums, extra, rims)


def down_kernel(bit, block, co, load, other, lower, upper, sum_ref, u_ref, below_ref, above_ref):
    step = pl.program_id(0)
    start = (pl.num_programs(0) - 1 - step) * block

    @pl.when(step == 0)
    def _():
        couple(bit, lax.axis_index("gy"), load, other, lower, upper, below_ref, above_ref)

    for c in range(3):
        lines = slice(32 * c, 32 * c + 32)
        below, value = below_ref[lines, :], above_ref[lines, :]
        for y in reversed(range(block)):
            i = start + y
            value = co[OWN, i] * (sum_ref[c, i] + below) + co[NEXT, i] * value
            u_ref[c, y] = value
        above_ref[lines, :] = value


def sweep_down(bit, table, load, other, around, sums, block):
    shape = sums.shape
    steps = shape[1] // block
    return pl.pallas_call(
        functools.partial(down_kernel, bit, block),
        grid=(steps,),
        in_specs=[smem()] + [vmem()] * 5,
        out_specs=pl.BlockSpec((3, block, 32, 128), lambda i: (0, steps - 1 - i, 0, 0)),
        out_shape=jax.ShapeDtypeStruct(shape, F32),
        scratch_shapes=[held((96, 128)), held((96, 128))],
        compiler_params=limit(8),
        cost_estimate=cost(4 * sums.size, 4 * sums.size),
        name="sweep_down",
    )(table, load, other, *around, sums)


def shards(velocity, old_advection, lower_gap, upper_gap):
    n = velocity.shape[1]
    group = max(d for d in range(1, 9) if n % (2 * d) == 0)
    block = 2 * group
    nx, ny = lax.axis_size("gx"), lax.axis_size("gy")
    ring = [(i, (i + 1) % nx) for i in range(nx)]
    line = [(i, i + 1) for i in range(ny - 1)]

    vel, left, right, bottom, top = pack(velocity, group)
    from_left = lax.ppermute(right, "gx", ring)
    from_right = lax.ppermute(left, "gx", [(j, i) for i, j in ring])
    below = lax.ppermute(top, "gy", line)
    above = lax.ppermute(bottom, "gy", [(j, i) for i, j in line])
    table, wide = coefs(lower_gap, upper_gap, group)
    adv_part, sums, b_sum = main_part(vel, old_advection, table, group, block)
    extra, rims, load = edge_part(
        from_left, from_right, left, right, sums, b_sum, wide, below, above, vel, table, group
    )
    bits = [1 << t for t in range(ny.bit_length() - 1)]
    whole, around, token = load, [], load
    for bit in bits:
        other = lax.ppermute(whole, "gy", [(i, i ^ bit) for i in range(ny)])
        if bit != bits[-1]:
            whole, *around = join_runs(bit, 2 * bit == bits[-1], whole, other, around)
            token = whole if bit == 1 else token
    adv, sums = sweep_up(token, table, adv_part, sums, extra, rims, group, block)
    return sweep_down(bits[-1], table, load, other, around, sums, block), adv


def solution(mesh):
    spec = P(None, "gy", None, "gx")
    return jax.shard_map(
        shards,
        mesh=mesh,
        in_specs=(spec, spec, P("gy"), P("gy")),
        out_specs=(spec, spec),
        check_vma=False,
    )
```

time: 76.4 us -> 56.5 us (0.74)
  blocking collectives: 19.5 us -> 0 us
  starting transfers between devices: 6.64 us -> 14.8 us
  local copies, waits for them, and re-layouts: 8.17 us -> 0.02 us
  Pallas kernels: 40.9 us -> 36.3 us
  waiting for transfers between devices: 0.01 us -> 4.16 us
    all_gather x1 -> x0, blocking collectives: 19.5 us -> none  [shards(): loads = lax.all_gather(load, 'gy')]
    unnamed x20 -> x8, local copies, waits for them, and re-layouts: 8.17 us -> 0.02 us
    ppermute x0 -> x3, starting transfers between devices: none -> 8.08 us  [shards(): other = lax.ppermute(whole, 'gy', [(i, i ^ bit) for i in range(ny)])]
    ppermute x0 -> x3, waiting for transfers between devices: none -> 4.15 us  [shards(): other = lax.ppermute(whole, 'gy', [(i, i ^ bit) for i in range(ny)])]
    pallas_call x1, Pallas kernels: 16.1 us -> 13.1 us  [main_part(): pl.pallas_call(functools.partial(main_kernel, n, block, group), grid=(n /...]
    pallas_call x1, Pallas kernels: 2.42 us -> 1.47 us  [edge_part(): pl.pallas_call(functools.partial(edge_kernel, pairs, group), in_specs=[sm...]
    pallas_call x2 -> x5, Pallas kernels: 17.2 us -> 16.5 us  [the longest x1 8.38 us: sweep_up(): pl.pallas_call(functools.partial(up_kernel, block, group), grid=(shape[1]...]
  transfers between devices with their start and end apart: 4 -> 7, of which waited for: 0 -> 2; matrix products, arithmetic and copies ran while one was open for 0% -> 0% of each run, Pallas kernels for 30% -> 40%
where the time goes in v3:
time: 56.5 us; the launch traced here: 56.1 us
  Pallas kernels  36.3 us (64%)
  starting transfers between devices  14.8 us (26%)
  waiting for transfers between devices  4.16 us (7%)
  between operations  0.77 us (1%)
    pallas_call x1, Pallas kernels, main_part(): pl.pallas_call(functools.partial(main_kernel, n, block, group), grid=(n /...  13.1 us
    pallas_call x1, Pallas kernels, sweep_up(): pl.pallas_call(functools.partial(up_kernel, block, group), grid=(shape[1]...  8.38 us
    ppermute x3, starting transfers between devices, shards(): other = lax.ppermute(whole, 'gy', [(i, i ^ bit) for i in range(ny)])  8.08 us
    pallas_call x1, Pallas kernels, sweep_down(): pl.pallas_call(functools.partial(down_kernel, bit, block), grid=(steps,),...  7.12 us
    pallas_call x1, Pallas kernels, pack(): pl.pallas_call(functools.partial(pack_kernel, group), in_specs=[pl.BlockS...  5.24 us
    ppermute x3, waiting for transfers between devices, shards(): other = lax.ppermute(whole, 'gy', [(i, i ^ bit) for i in range(ny)])  4.15 us
    ppermute x1, starting transfers between devices, shards(): from_left = lax.ppermute(right, 'gx', ring)  2.99 us
    pallas_call x1, Pallas kernels, edge_part(): pl.pallas_call(functools.partial(edge_kernel, pairs, group), in_specs=[sm...  1.47 us
  transfers between devices with their start and end apart: 7, of which 2 were waited for; matrix products, arithmetic and copies ran while one was open for 0% of the time, Pallas kernels for 40%

profile of v3, /device:TPU:0, one launch (start us, length us, event | category | flops | bytes accessed | tf_op | source)
XLA Modules:
  0.0 56.1 jit_solution(2438399914448362566)
XLA Ops:
  0.6 0.0 copy-start
  0.6 0.0 copy-start.1
  0.7 0.0 copy-start.3
  0.7 0.0 copy-start.2
  0.7 5.2 %pack_edges.1 = (f32[3,192,32,128]{3,2,1,0:T(8,128)S(1)}, f32[3,12,8,256]{3,2,1,0:T(8,128)S(1)}, f32[3,12,8,256]{3,2,1,0:T(8,128)S(1)}, f32[3,1,32,128]{3,2,1,0:T(8,128)S(1)}, f32[3,1,32,128]{3,2,1,0:T(8,128)S(1)}) custom-call(f32[3,192,32,128]{3,2,1,0:T(8,128)} %v_hbm.1), custom_call_target="tpu_custom_call" | custom-call | flops 2359296 | bytes 9437184 | tf_op jit(solution)/shard_map/pack_edges/pallas_call | solution.py:103
  5.9 3.0 %collective-permute-start = (f32[3,12,8,256]{3,2,1,0:T(8,128)S(1)}, f32[3,12,8,256]{3,2,1,0:T(8,128)S(1)}, u32[]{:S(2)}, u32[]{:S(2)}) collective-permute-start(f32[3,12,8,256]{3,2,1,0:T(8,128)S(1)} %get-tuple-element.24.right_ref), channel_id=1, source_target_pairs={{0,8},{8,16},{16,24},{24,0},{1,9},{9,17},{17,25},{25,1},{2,10},{10... | collective-permute-start | bytes 884744 | tf_op jit(solution)/shard_map/ppermute | solution.py:519
  8.9 1.0 %collective-permute-start.1 = (f32[3,12,8,256]{3,2,1,0:T(8,128)S(1)}, f32[3,12,8,256]{3,2,1,0:T(8,128)S(1)}, u32[]{:S(2)}, u32[]{:S(2)}) collective-permute-start(f32[3,12,8,256]{3,2,1,0:T(8,128)S(1)} %get-tuple-element.25.left_ref), channel_id=1, source_target_pairs={{8,0},{16,8},{24,16},{0,24},{9,1},{17,9},{25,17},{1,25},{10,2},{18... | collective-permute-start | bytes 884744 | tf_op jit(solution)/shard_map/ppermute | solution.py:520
  9.9 1.4 %collective-permute-start.2 = (f32[3,1,32,128]{3,2,1,0:T(8,128)S(1)}, f32[3,1,32,128]{3,2,1,0:T(8,128)S(1)}, u32[]{:S(2)}, u32[]{:S(2)}) collective-permute-start(f32[3,1,32,128]{3,2,1,0:T(8,128)S(1)} %get-tuple-element.30), channel_id=1, source_target_pairs={{0,1},{1,2},{2,3},{3,4},{4,5},{5,6},{6,7},{8,9},{9,10},{10,11},{11... | collective-permute-start | bytes 147464 | tf_op jit(solution)/shard_map/ppermute | solution.py:521
  11.4 1.3 %collective-permute-start.3 = (f32[3,1,32,128]{3,2,1,0:T(8,128)S(1)}, f32[3,1,32,128]{3,2,1,0:T(8,128)S(1)}, u32[]{:S(2)}, u32[]{:S(2)}) collective-permute-start(f32[3,1,32,128]{3,2,1,0:T(8,128)S(1)} %get-tuple-element.31), channel_id=1, source_target_pairs={{1,0},{2,1},{3,2},{4,3},{5,4},{6,5},{7,6},{9,8},{10,9},{11,10},{12... | collective-permute-start | bytes 147464 | tf_op jit(solution)/shard_map/ppermute | solution.py:522
  12.7 0.0 copy-done.3
  12.7 0.0 copy-done.2
  12.7 0.9 %coefficients.1 = (f32[8,256]{1,0:T(8,128)S(1)}, f32[2,12,8,256]{3,2,1,0:T(8,128)S(1)}) custom-call(f32[192]{0:T(256)S(1)} %copy-done.2, f32[192]{0:T(256)S(1)} %copy-done.3), custom_call_target="tpu_custom_call" | custom-call | flops 100000 | tf_op jit(solution)/shard_map/coefficients/pallas_call | solution.py:173
  13.6 0.0 copy-done
  13.6 0.0 copy-done.1
  13.6 13.1 %inner_part.1 = (f32[3,192,32,128]{3,2,1,0:T(8,128)S(1)}, f32[3,192,32,128]{3,2,1,0:T(8,128)S(1)}, f32[3,32,128]{2,1,0:T(8,128)S(1)}) custom-call(f32[8,256]{1,0:T(8,128)S(1)} %get-tuple-element.23.co, f32[3,192,32,128]{3,2,1,0:T(8,128)S(1)} %get-tuple-element.26.vel_ref, f32[3,192,32,128]{3,2,1,0:T(8,128)} %old_ref.1, bf16[256,128]{1,0:T(8,128)(2,1)S(1)} %copy-done.1, ...), custom_call_target="tpu_custom_call" | custom-call | flops 58982400 | bytes 9437184 | tf_op jit(solution)/shard_map/inner_part/pallas_call | solution.py:230
  26.8 0.0 collective-permute-done.2.low_ref
  26.8 0.0 collective-permute-done.3.high_ref
  26.8 0.0 collective-permute-done.from_left
  26.8 0.0 collective-permute-done.1.from_right
  26.8 1.5 %edge_part.1 = (bf16[3,24,16,256]{3,2,1,0:T(8,128)(2,1)S(1)}, f32[2,3,32,128]{3,2,1,0:T(8,128)S(1)}, f32[200,128]{1,0:T(8,128)S(1)}) custom-call(f32[8,256]{1,0:T(8,128)S(1)} %get-tuple-element.23.co, f32[3,12,8,256]{3,2,1,0:T(8,128)S(1)} %collective-permute-done.from_left, f32[3,12,8,256]{3,2,1,0:T(8,128)S(1)} %collective-permute-done.1.from_right, ...), custom_call_target="tpu_custom_call" | custom-call | flops 2949120 | tf_op jit(solution)/shard_map/edge_part/pallas_call | solution.py:314
  28.3 3.2 %collective-permute-start.4 = (f32[200,128]{1,0:T(8,128)S(1)}, f32[200,128]{1,0:T(8,128)S(1)}, u32[]{:S(2)}, u32[]{:S(2)}) collective-permute-start(f32[200,128]{1,0:T(8,128)S(1)} %get-tuple-element.32.all_ref.load), channel_id=1, source_target_pairs={{0,1},{1,0},{2,3},{3,2},{4,5},{5,4},{6,7},{7,6},{8,9},{9,8},{10,11... | collective-permute-start | bytes 307208 | tf_op jit(solution)/shard_map/ppermute | solution.py:531
  31.5 0.9 %collective-permute-done.4.other_ref = f32[200,128]{1,0:T(8,128)S(1)} collective-permute-done((f32[200,128]{1,0:T(8,128)S(1)}, f32[200,128]{1,0:T(8,128)S(1)}, u32[]{:S(2)}, u32[]{:S(2)}) %collective-permute-start.4) | collective-permute-done | bytes 102432 | tf_op jit(solution)/shard_map/ppermute | solution.py:531
  32.5 2.0 %collective-permute-start.5 = (f32[200,128]{1,0:T(8,128)S(1)}, f32[200,128]{1,0:T(8,128)S(1)}, u32[]{:S(2)}, u32[]{:S(2)}) collective-permute-start(f32[200,128]{1,0:T(8,128)S(1)} %get-tuple-element.33.all_ref.token), channel_id=1, source_target_pairs={{0,2},{1,3},{2,0},{3,1},{4,6},{5,7},{6,4},{7,5},{8,10},{9,11},{10,... | collective-permute-start | bytes 307208 | tf_op jit(solution)/shard_map/ppermute | solution.py:531
  34.5 3.2 %collective-permute-done.5.other_ref = f32[200,128]{1,0:T(8,128)S(1)} collective-permute-done((f32[200,128]{1,0:T(8,128)S(1)}, f32[200,128]{1,0:T(8,128)S(1)}, u32[]{:S(2)}, u32[]{:S(2)}) %collective-permute-start.5) | collective-permute-done | bytes 102432 | tf_op jit(solution)/shard_map/ppermute | solution.py:531
  37.7 0.1 join_runs.3
  37.8 2.8 %collective-permute-start.6 = (f32[104,128]{1,0:T(8,128)S(1)}, f32[104,128]{1,0:T(8,128)S(1)}, u32[]{:S(2)}, u32[]{:S(2)}) collective-permute-start(f32[104,128]{1,0:T(8,128)S(1)} %get-tuple-element.36), channel_id=1, source_target_pairs={{0,4},{1,5},{2,6},{3,7},{4,0},{5,1},{6,2},{7,3},{8,12},{9,13},{10,... | collective-permute-start | bytes 159752 | tf_op jit(solution)/shard_map/ppermute | solution.py:531
  40.6 8.4 %sweep_up.1 = (f32[3,192,32,128]{3,2,1,0:T(8,128)}, f32[3,192,32,128]{3,2,1,0:T(8,128)S(1)}) custom-call(f32[200,128]{1,0:T(8,128)S(1)} %get-tuple-element.33.all_ref.token, f32[8,256]{1,0:T(8,128)S(1)} %get-tuple-element.23.co, f32[3,192,32,128]{3,2,1,0:T(8,128)S(1)} %get-tuple-element.39.adv_part, ...), custom_call_target="tpu_custom_call" | custom-call | flops 18874368 | bytes 9437184 | tf_op jit(solution)/shard_map/sweep_up/pallas_call | solution.py:463
  49.0 0.0 collective-permute-done.6.other
  49.0 7.1 %sweep_down.1 = f32[3,192,32,128]{3,2,1,0:T(8,128)} custom-call(f32[8,256]{1,0:T(8,128)S(1)} %get-tuple-element.23.co, f32[200,128]{1,0:T(8,128)S(1)} %get-tuple-element.32.all_ref.load, f32[104,128]{1,0:T(8,128)S(1)} %collective-permute-done.6.other, f32[200,128]{1,0:T(8,128)S(1)} %get-tuple-element.37.lower, f32[200,128]{1,0:T(8,128)S(1)} %get-tuple-element.38.upper, ...), custom_call_target="tpu_custom_call" | custom-call | flops 9437184 | bytes 9437184 | tf_op jit(solution)/shard_map/sweep_down/pallas_call | solution.py:497
  (1 shorter events, 0.0 us)
Async XLA Ops:
  0.6 13.0 %copy-start = (bf16[256,256]{1,0:T(8,128)(2,1)S(1)}, bf16[256,256]{1,0:T(8,128)(2,1)}, u32[]{:S(2)}) copy-start(bf16[256,256]{1,0:T(8,128)(2,1)} %constant.5.clone.dz_ref) | copy-start | bytes 393220
  0.6 13.0 %copy-start.1 = (bf16[256,128]{1,0:T(8,128)(2,1)S(1)}, bf16[256,128]{1,0:T(8,128)(2,1)}, u32[]{:S(2)}) copy-start(bf16[256,128]{1,0:T(8,128)(2,1)} %constant.4.clone.dx_ref) | copy-start | bytes 196612
  0.7 12.0 %copy-start.3 = (f32[192]{0:T(256)S(1)}, f32[192]{0:T(256)}, u32[]{:S(2)}) copy-start(f32[192]{0:T(256)} %upper_ref.1) | copy-start | bytes 2308
  0.7 12.0 %copy-start.2 = (f32[192]{0:T(256)S(1)}, f32[192]{0:T(256)}, u32[]{:S(2)}) copy-start(f32[192]{0:T(256)} %lower_ref.1) | copy-start | bytes 2308
  5.9 20.9 %collective-permute-start = (f32[3,12,8,256]{3,2,1,0:T(8,128)S(1)}, f32[3,12,8,256]{3,2,1,0:T(8,128)S(1)}, u32[]{:S(2)}, u32[]{:S(2)}) collective-permute-start(f32[3,12,8,256]{3,2,1,0:T(8,128)S(1)} %get-tuple-element.24.right_ref), channel_id=1, source_target_pairs={{0,8},{8,16},{16,24},{24,0},{1,9},{9,17},{17,25},{25,1},{2,10},{10... | collective-permute-start | bytes 884744 | tf_op jit(solution)/shard_map/ppermute | solution.py:519
  8.9 17.9 %collective-permute-start.1 = (f32[3,12,8,256]{3,2,1,0:T(8,128)S(1)}, f32[3,12,8,256]{3,2,1,0:T(8,128)S(1)}, u32[]{:S(2)}, u32[]{:S(2)}) collective-permute-start(f32[3,12,8,256]{3,2,1,0:T(8,128)S(1)} %get-tuple-element.25.left_ref), channel_id=1, source_target_pairs={{8,0},{16,8},{24,16},{0,24},{9,1},{17,9},{25,17},{1,25},{10,2},{18... | collective-permute-start | bytes 884744 | tf_op jit(solution)/shard_map/ppermute | solution.py:520
  9.9 16.8 %collective-permute-start.2 = (f32[3,1,32,128]{3,2,1,0:T(8,128)S(1)}, f32[3,1,32,128]{3,2,1,0:T(8,128)S(1)}, u32[]{:S(2)}, u32[]{:S(2)}) collective-permute-start(f32[3,1,32,128]{3,2,1,0:T(8,128)S(1)} %get-tuple-element.30), channel_id=1, source_target_pairs={{0,1},{1,2},{2,3},{3,4},{4,5},{5,6},{6,7},{8,9},{9,10},{10,11},{11... | collective-permute-start | bytes 147464 | tf_op jit(solution)/shard_map/ppermute | solution.py:521
  11.4 15.4 %collective-permute-start.3 = (f32[3,1,32,128]{3,2,1,0:T(8,128)S(1)}, f32[3,1,32,128]{3,2,1,0:T(8,128)S(1)}, u32[]{:S(2)}, u32[]{:S(2)}) collective-permute-start(f32[3,1,32,128]{3,2,1,0:T(8,128)S(1)} %get-tuple-element.31), channel_id=1, source_target_pairs={{1,0},{2,1},{3,2},{4,3},{5,4},{6,5},{7,6},{9,8},{10,9},{11,10},{12... | collective-permute-start | bytes 147464 | tf_op jit(solution)/shard_map/ppermute | solution.py:522
  28.3 4.2 %collective-permute-start.4 = (f32[200,128]{1,0:T(8,128)S(1)}, f32[200,128]{1,0:T(8,128)S(1)}, u32[]{:S(2)}, u32[]{:S(2)}) collective-permute-start(f32[200,128]{1,0:T(8,128)S(1)} %get-tuple-element.32.all_ref.load), channel_id=1, source_target_pairs={{0,1},{1,0},{2,3},{3,2},{4,5},{5,4},{6,7},{7,6},{8,9},{9,8},{10,11... | collective-permute-start | bytes 307208 | tf_op jit(solution)/shard_map/ppermute | solution.py:531
  32.5 5.2 %collective-permute-start.5 = (f32[200,128]{1,0:T(8,128)S(1)}, f32[200,128]{1,0:T(8,128)S(1)}, u32[]{:S(2)}, u32[]{:S(2)}) collective-permute-start(f32[200,128]{1,0:T(8,128)S(1)} %get-tuple-element.33.all_ref.token), channel_id=1, source_target_pairs={{0,2},{1,3},{2,0},{3,1},{4,6},{5,7},{6,4},{7,5},{8,10},{9,11},{10,... | collective-permute-start | bytes 307208 | tf_op jit(solution)/shard_map/ppermute | solution.py:531
  37.8 11.2 %collective-permute-start.6 = (f32[104,128]{1,0:T(8,128)S(1)}, f32[104,128]{1,0:T(8,128)S(1)}, u32[]{:S(2)}, u32[]{:S(2)}) collective-permute-start(f32[104,128]{1,0:T(8,128)S(1)} %get-tuple-element.36), channel_id=1, source_target_pairs={{0,4},{1,5},{2,6},{3,7},{4,0},{5,1},{6,2},{7,3},{8,12},{9,13},{10,... | collective-permute-start | bytes 159752 | tf_op jit(solution)/shard_map/ppermute | solution.py:531

commit v4 on v3

--- a/solution.py
+++ b/solution.py
@@ -182,44 +182,51 @@
     )(lower_gap, upper_gap)
 
 
-def main_kernel(n, block, group, co, vel_ref, old_ref, dx_ref, dz_ref, adv_ref, sum_ref, b_ref, a_ref):
-    step = pl.program_id(0)
-
-    @pl.when(step == 0)
-    def _():
-        a_ref[...] = jnp.zeros_like(a_ref)
-        b_ref[...] = jnp.zeros_like(b_ref)
-
+def main_kernel(n, block, group, co, vel_ref, old_hbm, dx_ref, dz_ref, adv_ref, sum_ref, b_ref, old_ref, a_ref, sems):
+    steps = n // block
     rows = group * 32
     nothing = jnp.zeros((32, 128), F32)
 
-    for k in range(block // group):
-        y0 = k * group
-        i0 = step * block + y0
-        vel = [vel_ref[c, pl.ds(i0, group)].reshape(rows, 128) for c in range(3)]
-        for c in range(3):
-            f = vel[c]
-            pair = jnp.concatenate(split(f), axis=1)
-            along_x = jnp.dot(pair, dx_ref[...], preferred_element_type=F32)
-            both = jnp.dot(dz_ref[...], pair, preferred_element_type=F32)
-            along_z = both[:, :128] + both[:, 128:]
-            below = jnp.where(i0 == 0, nothing, vel_ref[c, jnp.maximum(i0 - 1, 0)])
-            above = jnp.where(i0 == n - group, nothing, vel_ref[c, jnp.minimum(i0 + group, n - 1)])
-            up, down = a_ref[c], b_ref[c]
-            for y in range(group):
-                here = slice(32 * y, 32 * y + 32)
-                i = i0 + y
-                under = below if y == 0 else f[32 * y - 32 : 32 * y]
-                over = above if y == group - 1 else f[32 * y + 32 : 32 * y + 64]
-                flat = (vel[0][here] * along_x[here] + vel[2][here] * along_z[here]) * (-UNIT)
-                adv = flat - vel[1][here] * ((over - under) * co[INV_GAP, i])
-                force = f[here] + GAMMA * adv + ZETA * old_ref[c, y0 + y]
-                up = up + co[FORWARD, i] * force
-                down = down + co[BACKWARD, i] * force
-                adv_ref[c, i] = adv
-                sum_ref[c, i] = up
-            a_ref[c] = up
-            b_ref[c] = down
+    def copy(step):
+        here = pl.ds(step * block, block)
+        return pltpu.make_async_copy(old_hbm.at[:, here], old_ref.at[:, here], sems.at[step])
+
+    for step in range(steps):
+        copy(step).start()
+    a_ref[...] = jnp.zeros_like(a_ref)
+    b_ref[...] = jnp.zeros_like(b_ref)
+
+    def part(step, _):
+        copy(step).wait()
+        for k in range(block // group):
+            i0 = step * block + k * group
+            vel = [vel_ref[c, pl.ds(i0, group)].reshape(rows, 128) for c in range(3)]
+            for c in range(3):
+                f = vel[c]
+                pair = jnp.concatenate(split(f), axis=1)
+                along_x = jnp.dot(pair, dx_ref[...], preferred_element_type=F32)
+                both = jnp.dot(dz_ref[...], pair, preferred_element_type=F32)
+                along_z = both[:, :128] + both[:, 128:]
+                below = jnp.where(i0 == 0, nothing, vel_ref[c, jnp.maximum(i0 - 1, 0)])
+                above = jnp.where(i0 == n - group, nothing, vel_ref[c, jnp.minimum(i0 + group, n - 1)])
+                up, down = a_ref[c], b_ref[c]
+                for y in range(group):
+                    here = slice(32 * y, 32 * y + 32)
+                    i = i0 + y
+                    under = below if y == 0 else f[32 * y - 32 : 32 * y]
+                    over = above if y == group - 1 else f[32 * y + 32 : 32 * y + 64]
+                    flat = (vel[0][here] * along_x[here] + vel[2][here] * along_z[here]) * (-UNIT)
+                    adv = flat - vel[1][here] * ((over - under) * co[INV_GAP, i])
+                    force = f[here] + GAMMA * adv + ZETA * old_ref[c, i]
+                    up = up + co[FORWARD, i] * force
+                    down = down + co[BACKWARD, i] * force
+                    adv_ref[c, i] = adv
+                    sum_ref[c, i] = up
+                a_ref[c] = up
+                b_ref[c] = down
+        return 0
+
+    lax.fori_loop(0, steps, part, 0)
 
 
 def main_part(vel, old, table, group, block):
@@ -229,12 +236,11 @@
     dz = jnp.asarray(np.kron(np.eye(group), shift_matrix(32, True).T), BF16)
     return pl.pallas_call(
         functools.partial(main_kernel, n, block, group),
-        grid=(n // block,),
-        in_specs=[smem(), vmem(), pl.BlockSpec((3, block, 32, 128), lambda i: (0, i, 0, 0)), vmem(), vmem()],
+        in_specs=[smem(), vmem(), pl.BlockSpec(memory_space=pltpu.HBM), vmem(), vmem()],
         out_specs=[vmem()] * 3,
         out_shape=[held(vel.shape), held(vel.shape), held((3, 32, 128))],
-        scratch_shapes=[held((3, 32, 128))],
-        compiler_params=limit(8),
+        scratch_shapes=[held(vel.shape), held((3, 32, 128)), pltpu.SemaphoreType.DMA((n // block,))],
+        compiler_params=limit(12),
         cost_estimate=cost(25 * old.size, 4 * old.size),
         name="inner_part",
     )(table, vel, pltpu.with_memory_space_constraint(old, pltpu.HBM), dx, dz)
@@ -355,7 +361,7 @@
     return (none, none, zero, one, one, zero)
 
 
-def join_kernel(bit, opening, closing, all_ref, other_ref, *refs):
+def join_kernel(bit, opening, closing, token, all_ref, other_ref, *refs):
     me = lax.axis_index("gy")
     if opening:
         lower_in = upper_in = None
@@ -387,18 +393,18 @@
         write(upper_out, join(upper, other))
 
 
-def join_runs(bit, closing, whole, other, around):
+def join_runs(bit, closing, token, whole, other, around):
     run = jax.ShapeDtypeStruct((200, 128), F32)
     half = jax.ShapeDtypeStruct((104, 128), F32)
     return pl.pallas_call(
         functools.partial(join_kernel, bit, not around, closing),
-        in_specs=[vmem()] * (2 + len(around)),
+        in_specs=[pl.BlockSpec(memory_space=pl.ANY)] + [vmem()] * (2 + len(around)),
         out_specs=[vmem()] * 3,
         out_shape=[half if closing else run, run, run],
         compiler_params=limit(8),
         cost_estimate=cost(20 * whole.size),
         name="join_runs",
-    )(whole, other, *around)
+    )(token, whole, other, *around)
 
 
 def couple(bit, me, load, other_ref, lower_ref, upper_ref, below_ref, above_ref):
@@ -426,85 +432,122 @@
         solve(lower, join(upper, (vector, none, scalar, zero, zero, zero)))
 
 
-def up_kernel(block, group, token, co, adv_part, sum_part, extra_ref, rim_ref, adv_ref, sum_ref, acc_ref):
-    step = pl.program_id(0)
-    last = pl.num_programs(0) - 1
-
-    @pl.when(step == 0)
-    def _():
-        acc_ref[...] = (GAMMA * co[FORWARD, 0]) * rim_ref[0]
-
-    for c in range(3):
-        acc = acc_ref[c]
-        for k in range(block // group):
-            g = step * (block // group) + k
-            spread = spread_planes(extra_ref[c, g])
-            for y in range(group):
-                i = g * group + y
-                extra = spread[32 * y : 32 * y + 32]
-                adv_ref[c, k * group + y] = adv_part[c, i] + extra
-                acc = acc + (GAMMA * co[FORWARD, i]) * extra
-                sum_ref[c, i] = sum_part[c, i] + acc
-        acc_ref[c] = acc
-
-    @pl.when(step == 0)
-    def _():
-        adv_ref[:, 0] = adv_ref[:, 0] + rim_ref[0]
-
-    @pl.when(step == last)
-    def _():
-        adv_ref[:, block - 1] = adv_ref[:, block - 1] + rim_ref[1]
-        i = (last + 1) * block - 1
-        sum_ref[:, i] = sum_ref[:, i] + (GAMMA * co[FORWARD, i]) * rim_ref[1]
-
-
-def sweep_up(token, table, adv_part, sums, extra, rims, group, block):
+def up_kernel(start, count, block, group, token, co, adv_part, sum_part, extra_ref, rim_ref, *refs):
+    n = adv_part.shape[1]
+    if start:
+        _, before_ref, adv_hbm, sum_ref, end_ref, adv_ref, sems = refs
+        end_ref[...] = before_ref[...]
+    else:
+        adv_hbm, sum_ref, end_ref, adv_ref, sems = refs
+        end_ref[...] = (GAMMA * co[FORWARD, 0]) * rim_ref[0]
+    steps = count // block
+
+    def copy(step):
+        here = pl.ds(step * block, block)
+        there = pl.ds(start + step * block, block)
+        return pltpu.make_async_copy(adv_ref.at[:, here], adv_hbm.at[:, there], sems.at[step])
+
+    def part(step, _):
+        for c in range(3):
+            acc = end_ref[c]
+            for k in range(block // group):
+                here = step * block + k * group
+                spread = spread_planes(extra_ref[c, start // group + step * (block // group) + k])
+                for y in range(group):
+                    i = here + y
+                    extra = spread[32 * y : 32 * y + 32]
+                    adv_ref[c, i] = adv_part[c, start + i] + extra
+                    acc = acc + (GAMMA * co[FORWARD, start + i]) * extra
+                    sum_ref[c, i] = sum_part[c, start + i] + acc
+            end_ref[c] = acc
+
+        if start == 0:
+            @pl.when(step == 0)
+            def _():
+                adv_ref[:, 0] = adv_ref[:, 0] + rim_ref[0]
+
+        if start + count == n:
+            @pl.when(step == steps - 1)
+            def _():
+                adv_ref[:, count - 1] = adv_ref[:, count - 1] + rim_ref[1]
+                sum_ref[:, count - 1] = sum_ref[:, count - 1] + (GAMMA * co[FORWARD, n - 1]) * rim_ref[1]
+
+        copy(step).start()
+        return 0
+
+    lax.fori_loop(0, steps, part, 0)
+
+    def finish(step, _):
+        copy(step).wait()
+        return 0
+
+    lax.fori_loop(0, steps, finish, 0)
+
+
+def sweep_up(start, count, token, table, adv_part, sums, extra, rims, group, before=()):
     shape = adv_part.shape
-    return pl.pallas_call(
-        functools.partial(up_kernel, block, group),
-        grid=(shape[1] // block,),
-        in_specs=[pl.BlockSpec(memory_space=pl.ANY), smem()] + [vmem()] * 4,
-        out_specs=[pl.BlockSpec((3, block, 32, 128), lambda i: (0, i, 0, 0)), vmem()],
-        out_shape=[jax.ShapeDtypeStruct(shape, F32), held(shape)],
-        scratch_shapes=[held((3, 32, 128))],
+    block = max(d for d in range(group, 33, group) if count % d == 0)
+    hbm = pl.BlockSpec(memory_space=pltpu.HBM)
+    part = (3, count, 32, 128)
+    return pl.pallas_call(
+        functools.partial(up_kernel, start, count, block, group),
+        in_specs=[pl.BlockSpec(memory_space=pl.ANY), smem()] + [vmem()] * 4 + ([hbm, vmem()] if before else []),
+        out_specs=[hbm, vmem(), vmem()],
+        out_shape=[jax.ShapeDtypeStruct(shape, F32), held(part), held((3, 32, 128))],
+        scratch_shapes=[held(part), pltpu.SemaphoreType.DMA((count // block,))],
+        input_output_aliases={6: 0} if before else {},
         compiler_params=limit(8),
-        cost_estimate=cost(8 * adv_part.size, 4 * adv_part.size),
+        cost_estimate=cost(4 * adv_part.size, 2 * adv_part.size),
         name="sweep_up",
-    )(token, table, adv_part, sums, extra, rims)
-
-
-def down_kernel(bit, block, co, load, other, lower, upper, sum_ref, u_ref, below_ref, above_ref):
-    step = pl.program_id(0)
-    start = (pl.num_programs(0) - 1 - step) * block
-
-    @pl.when(step == 0)
-    def _():
-        couple(bit, lax.axis_index("gy"), load, other, lower, upper, below_ref, above_ref)
-
-    for c in range(3):
-        lines = slice(32 * c, 32 * c + 32)
-        below, value = below_ref[lines, :], above_ref[lines, :]
-        for y in reversed(range(block)):
-            i = start + y
-            value = co[OWN, i] * (sum_ref[c, i] + below) + co[NEXT, i] * value
-            u_ref[c, y] = value
-        above_ref[lines, :] = value
+    )(token, table, adv_part, sums, extra, rims, *before)
+
+
+def down_kernel(bit, n, block, co, load, other, lower, upper, low_ref, high_ref, u_hbm, u_ref, below_ref, above_ref,
+                sems):
+    steps = n // block
+    couple(bit, lax.axis_index("gy"), load, other, lower, upper, below_ref, above_ref)
+    below = below_ref[...].reshape(3, 32, 128)
+
+    def copy(step):
+        here = pl.ds(step * block, block)
+        return pltpu.make_async_copy(u_ref.at[:, here], u_hbm.at[:, here], sems.at[step])
+
+    def part(sum_ref, first):
+        def run(k, value):
+            step = steps // 2 - 1 - k
+            for y in reversed(range(block)):
+                i = step * block + y
+                value = co[OWN, first + i] * (sum_ref[:, i] + below) + co[NEXT, first + i] * value
+                u_ref[:, first + i] = value
+            copy(first // block + step).start()
+            return value
+
+        return run
+
+    value = above_ref[...].reshape(3, 32, 128)
+    value = lax.fori_loop(0, steps // 2, part(high_ref, n // 2), value)
+    lax.fori_loop(0, steps // 2, part(low_ref, 0), value)
+
+    def finish(step, _):
+        copy(step).wait()
+        return 0
+
+    lax.fori_loop(0, steps, finish, 0)
 
 
 def sweep_down(bit, table, load, other, around, sums, block):
-    shape = sums.shape
-    steps = shape[1] // block
-    return pl.pallas_call(
-        functools.partial(down_kernel, bit, block),
-        grid=(steps,),
-        in_specs=[smem()] + [vmem()] * 5,
-        out_specs=pl.BlockSpec((3, block, 32, 128), lambda i: (0, steps - 1 - i, 0, 0)),
+    n = 2 * sums[0].shape[1]
+    shape = (3, n, 32, 128)
+    return pl.pallas_call(
+        functools.partial(down_kernel, bit, n, block),
+        in_specs=[smem()] + [vmem()] * 6,
+        out_specs=pl.BlockSpec(memory_space=pltpu.HBM),
         out_shape=jax.ShapeDtypeStruct(shape, F32),
-        scratch_shapes=[held((96, 128)), held((96, 128))],
-        compiler_params=limit(8),
-        cost_estimate=cost(4 * sums.size, 4 * sums.size),
+        scratch_shapes=[held(shape), held((96, 128)), held((96, 128)), pltpu.SemaphoreType.DMA((n // block,))],
+        compiler_params=limit(12),
+        cost_estimate=cost(12 * sums[0].size, 8 * sums[0].size),
         name="sweep_down",
-    )(table, load, other, *around, sums)
+    )(table, load, other, *around, *sums)
 
 
 def shards(velocity, old_advection, lower_gap, upper_gap):
@@ -526,14 +569,18 @@
         from_left, from_right, left, right, sums, b_sum, wide, below, above, vel, table, group
     )
     bits = [1 << t for t in range(ny.bit_length() - 1)]
+    half = n // 2
     whole, around, token = load, [], load
     for bit in bits:
         other = lax.ppermute(whole, "gy", [(i, i ^ bit) for i in range(ny)])
         if bit != bits[-1]:
-            whole, *around = join_runs(bit, 2 * bit == bits[-1], whole, other, around)
-            token = whole if bit == 1 else token
-    adv, sums = sweep_up(token, table, adv_part, sums, extra, rims, group, block)
-    return sweep_down(bits[-1], table, load, other, around, sums, block), adv
+            whole, *around = join_runs(bit, 2 * bit == bits[-1], token, whole, other, around)
+        if bit == bits[0]:
+            adv, low, end = sweep_up(0, half, whole, table, adv_part, sums, extra, rims, group)
+            token = end
+    adv, high, _ = sweep_up(half, half, whole, table, adv_part, sums, extra, rims, group, (adv, end))
+    down_block = block if half % block == 0 else group
+    return sweep_down(bits[-1], table, load, other, around, (low, high), down_block), adv
 
 
 def solution(mesh):

time: 56.5 us -> 48.2 us (0.85)
  Pallas kernels: 36.3 us -> 31.5 us
  waiting for transfers between devices: 4.16 us -> 0.97 us
    pallas_call x3 -> x4, Pallas kernels: 28.6 us -> 23.8 us  [the longest x1 11.9 us: main_part(): pl.pallas_call(functools.partial(main_kernel, n, block, group), in_specs=...]
    ppermute x3, waiting for transfers between devices: 4.15 us -> 0.95 us  [shards(): other = lax.ppermute(whole, 'gy', [(i, i ^ bit) for i in range(ny)])]
  transfers between devices with their start and end apart: 7 -> 7, of which waited for: 2 -> 1; matrix products, arithmetic and copies ran while one was open for 0% -> 0% of each run, Pallas kernels for 40% -> 42%
where the time goes in v4:
time: 48.2 us; the launch traced here: 48 us
  Pallas kernels  31.5 us (65%)
  starting transfers between devices  14.7 us (30%)
  waiting for transfers between devices  0.97 us (2%)
  between operations  0.81 us (2%)
    pallas_call x1, Pallas kernels, main_part(): pl.pallas_call(functools.partial(main_kernel, n, block, group), in_specs=...  11.9 us
    ppermute x3, starting transfers between devices, shards(): other = lax.ppermute(whole, 'gy', [(i, i ^ bit) for i in range(ny)])  7.92 us
    pallas_call x2, Pallas kernels, sweep_up(): pl.pallas_call(functools.partial(up_kernel, start, count, block, group),...  7.29 us
    pallas_call x1, Pallas kernels, pack(): pl.pallas_call(functools.partial(pack_kernel, group), in_specs=[pl.BlockS...  5.24 us
    pallas_call x1, Pallas kernels, sweep_down(): pl.pallas_call(functools.partial(down_kernel, bit, n, block), in_specs=[s...  4.58 us
    ppermute x1, starting transfers between devices, shards(): from_left = lax.ppermute(right, 'gx', ring)  2.99 us
    pallas_call x1, Pallas kernels, edge_part(): pl.pallas_call(functools.partial(edge_kernel, pairs, group), in_specs=[sm...  1.47 us
    ppermute x1, starting transfers between devices, shards(): below = lax.ppermute(top, 'gy', line)  1.45 us
  transfers between devices with their start and end apart: 7, of which 1 were waited for; matrix products, arithmetic and copies ran while one was open for 0% of the time, Pallas kernels for 42%

profile of v4, /device:TPU:0, one launch (start us, length us, event | category | flops | bytes accessed | tf_op | source)
XLA Modules:
  0.0 48.0 jit_solution(14808036620055266199)
XLA Ops:
  0.6 0.0 copy-start
  0.6 0.0 copy-start.1
  0.7 0.0 copy-start.3
  0.7 0.0 copy-start.2
  0.7 5.2 %pack_edges.1 = (f32[3,192,32,128]{3,2,1,0:T(8,128)S(1)}, f32[3,12,8,256]{3,2,1,0:T(8,128)S(1)}, f32[3,12,8,256]{3,2,1,0:T(8,128)S(1)}, f32[3,1,32,128]{3,2,1,0:T(8,128)S(1)}, f32[3,1,32,128]{3,2,1,0:T(8,128)S(1)}) custom-call(f32[3,192,32,128]{3,2,1,0:T(8,128)} %v_hbm.1), custom_call_target="tpu_custom_call" | custom-call | flops 2359296 | bytes 9437184 | tf_op jit(solution)/shard_map/pack_edges/pallas_call | solution.py:103
  5.9 3.0 %collective-permute-start = (f32[3,12,8,256]{3,2,1,0:T(8,128)S(1)}, f32[3,12,8,256]{3,2,1,0:T(8,128)S(1)}, u32[]{:S(2)}, u32[]{:S(2)}) collective-permute-start(f32[3,12,8,256]{3,2,1,0:T(8,128)S(1)} %get-tuple-element.27.right_ref), channel_id=1, source_target_pairs={{0,8},{8,16},{16,24},{24,0},{1,9},{9,17},{17,25},{25,1},{2,10},{10... | collective-permute-start | bytes 884744 | tf_op jit(solution)/shard_map/ppermute | solution.py:562
  8.9 1.0 %collective-permute-start.1 = (f32[3,12,8,256]{3,2,1,0:T(8,128)S(1)}, f32[3,12,8,256]{3,2,1,0:T(8,128)S(1)}, u32[]{:S(2)}, u32[]{:S(2)}) collective-permute-start(f32[3,12,8,256]{3,2,1,0:T(8,128)S(1)} %get-tuple-element.28.left_ref), channel_id=1, source_target_pairs={{8,0},{16,8},{24,16},{0,24},{9,1},{17,9},{25,17},{1,25},{10,2},{18... | collective-permute-start | bytes 884744 | tf_op jit(solution)/shard_map/ppermute | solution.py:563
  9.9 1.4 %collective-permute-start.2 = (f32[3,1,32,128]{3,2,1,0:T(8,128)S(1)}, f32[3,1,32,128]{3,2,1,0:T(8,128)S(1)}, u32[]{:S(2)}, u32[]{:S(2)}) collective-permute-start(f32[3,1,32,128]{3,2,1,0:T(8,128)S(1)} %get-tuple-element.33), channel_id=1, source_target_pairs={{0,1},{1,2},{2,3},{3,4},{4,5},{5,6},{6,7},{8,9},{9,10},{10,11},{11... | collective-permute-start | bytes 147464 | tf_op jit(solution)/shard_map/ppermute | solution.py:564
  11.4 1.3 %collective-permute-start.3 = (f32[3,1,32,128]{3,2,1,0:T(8,128)S(1)}, f32[3,1,32,128]{3,2,1,0:T(8,128)S(1)}, u32[]{:S(2)}, u32[]{:S(2)}) collective-permute-start(f32[3,1,32,128]{3,2,1,0:T(8,128)S(1)} %get-tuple-element.34), channel_id=1, source_target_pairs={{1,0},{2,1},{3,2},{4,3},{5,4},{6,5},{7,6},{9,8},{10,9},{11,10},{12... | collective-permute-start | bytes 147464 | tf_op jit(solution)/shard_map/ppermute | solution.py:565
  12.7 0.0 copy-done.3
  12.7 0.0 copy-done.2
  12.7 0.9 %coefficients.1 = (f32[8,256]{1,0:T(8,128)S(1)}, f32[2,12,8,256]{3,2,1,0:T(8,128)S(1)}) custom-call(f32[192]{0:T(256)S(1)} %copy-done.2, f32[192]{0:T(256)S(1)} %copy-done.3), custom_call_target="tpu_custom_call" | custom-call | flops 100000 | tf_op jit(solution)/shard_map/coefficients/pallas_call | solution.py:173
  13.6 0.0 copy-done
  13.6 0.0 copy-done.1
  13.6 11.9 %inner_part.1 = (f32[3,192,32,128]{3,2,1,0:T(8,128)S(1)}, f32[3,192,32,128]{3,2,1,0:T(8,128)S(1)}, f32[3,32,128]{2,1,0:T(8,128)S(1)}) custom-call(f32[8,256]{1,0:T(8,128)S(1)} %get-tuple-element.26.co, f32[3,192,32,128]{3,2,1,0:T(8,128)S(1)} %get-tuple-element.29.vel_ref, f32[3,192,32,128]{3,2,1,0:T(8,128)} %old_hbm.1, bf16[256,128]{1,0:T(8,128)(2,1)S(1)} %copy-done.1, ...), custom_call_target="tpu_custom_call" | custom-call | flops 58982400 | bytes 9437184 | tf_op jit(solution)/shard_map/inner_part/pallas_call | solution.py:237
  25.5 0.0 collective-permute-done.2.low_ref
  25.5 0.0 collective-permute-done.3.high_ref
  25.6 0.0 collective-permute-done.from_left
  25.6 0.0 collective-permute-done.1.from_right
  25.6 1.5 %edge_part.1 = (bf16[3,24,16,256]{3,2,1,0:T(8,128)(2,1)S(1)}, f32[2,3,32,128]{3,2,1,0:T(8,128)S(1)}, f32[200,128]{1,0:T(8,128)S(1)}) custom-call(f32[8,256]{1,0:T(8,128)S(1)} %get-tuple-element.26.co, f32[3,12,8,256]{3,2,1,0:T(8,128)S(1)} %collective-permute-done.from_left, f32[3,12,8,256]{3,2,1,0:T(8,128)S(1)} %collective-permute-done.1.from_right, ...), custom_call_target="tpu_custom_call" | custom-call | flops 2949120 | tf_op jit(solution)/shard_map/edge_part/pallas_call | solution.py:320
  27.0 3.2 %collective-permute-start.4 = (f32[200,128]{1,0:T(8,128)S(1)}, f32[200,128]{1,0:T(8,128)S(1)}, u32[]{:S(2)}, u32[]{:S(2)}) collective-permute-start(f32[200,128]{1,0:T(8,128)S(1)} %get-tuple-element.35.token.all_ref.load), channel_id=1, source_target_pairs={{0,1},{1,0},{2,3},{3,2},{4,5},{5,4},{6,7},{7,6},{8,9},{9,8},{10,11... | collective-permute-start | bytes 307208 | tf_op jit(solution)/shard_map/ppermute | solution.py:575
  30.3 0.9 %collective-permute-done.4.other_ref = f32[200,128]{1,0:T(8,128)S(1)} collective-permute-done((f32[200,128]{1,0:T(8,128)S(1)}, f32[200,128]{1,0:T(8,128)S(1)}, u32[]{:S(2)}, u32[]{:S(2)}) %collective-permute-start.4) | collective-permute-done | bytes 102432 | tf_op jit(solution)/shard_map/ppermute | solution.py:575
  31.3 2.0 %collective-permute-start.5 = (f32[200,128]{1,0:T(8,128)S(1)}, f32[200,128]{1,0:T(8,128)S(1)}, u32[]{:S(2)}, u32[]{:S(2)}) collective-permute-start(f32[200,128]{1,0:T(8,128)S(1)} %get-tuple-element.36.token.all_ref), channel_id=1, source_target_pairs={{0,2},{1,3},{2,0},{3,1},{4,6},{5,7},{6,4},{7,5},{8,10},{9,11},{10,... | collective-permute-start | bytes 307208 | tf_op jit(solution)/shard_map/ppermute | solution.py:575
  33.3 3.3 %sweep_up.2 = (f32[3,192,32,128]{3,2,1,0:T(8,128)}, f32[3,96,32,128]{3,2,1,0:T(8,128)S(1)}, f32[3,32,128]{2,1,0:T(8,128)S(1)}) custom-call(f32[200,128]{1,0:T(8,128)S(1)} %get-tuple-element.36.token.all_ref, f32[8,256]{1,0:T(8,128)S(1)} %get-tuple-element.26.co, f32[3,192,32,128]{3,2,1,0:T(8,128)S(1)} %get-tuple-element.37.adv_part, ...), custom_call_target="tpu_custom_call" | custom-call | flops 9437184 | bytes 4718592 | tf_op jit(solution)/shard_map/sweep_up/pallas_call | solution.py:492
  36.7 0.0 collective-permute-done.5.other_ref
  36.7 0.1 join_runs.3
  36.8 2.7 %collective-permute-start.6 = (f32[104,128]{1,0:T(8,128)S(1)}, f32[104,128]{1,0:T(8,128)S(1)}, u32[]{:S(2)}, u32[]{:S(2)}) collective-permute-start(f32[104,128]{1,0:T(8,128)S(1)} %get-tuple-element.43.token), channel_id=1, source_target_pairs={{0,4},{1,5},{2,6},{3,7},{4,0},{5,1},{6,2},{7,3},{8,12},{9,13},{10,... | collective-permute-start | bytes 159752 | tf_op jit(solution)/shard_map/ppermute | solution.py:575
  39.4 4.0 %sweep_up.3 = (f32[3,192,32,128]{3,2,1,0:T(8,128)}, f32[3,96,32,128]{3,2,1,0:T(8,128)S(1)}, f32[3,32,128]{2,1,0:T(8,128)}) custom-call(f32[104,128]{1,0:T(8,128)S(1)} %get-tuple-element.43.token, f32[8,256]{1,0:T(8,128)S(1)} %get-tuple-element.26.co, f32[3,192,32,128]{3,2,1,0:T(8,128)S(1)} %get-tuple-element.37.adv_part, ...), custom_call_target="tpu_custom_call", output_to_operand_aliasing={{0}: (6, {})} | custom-call | flops 9437184 | bytes 4718592 | tf_op jit(solution)/shard_map/sweep_up/pallas_call | solution.py:492
  43.4 0.0 collective-permute-done.6.other
  43.4 4.6 %sweep_down.1 = f32[3,192,32,128]{3,2,1,0:T(8,128)} custom-call(f32[8,256]{1,0:T(8,128)S(1)} %get-tuple-element.26.co, f32[200,128]{1,0:T(8,128)S(1)} %get-tuple-element.35.token.all_ref.load, f32[104,128]{1,0:T(8,128)S(1)} %collective-permute-done.6.other, f32[200,128]{1,0:T(8,128)S(1)} %get-tuple-element.44.lower, f32[200,128]{1,0:T(8,128)S(1)} %get-tuple-element.45.upper, ...), custom_call_target="tpu_custom_call" | custom-call | flops 14155776 | bytes 9437184 | tf_op jit(solution)/shard_map/sweep_down/pallas_call | solution.py:541
  (1 shorter events, 0.0 us)
Async XLA Ops:
  0.6 13.0 %copy-start = (bf16[256,256]{1,0:T(8,128)(2,1)S(1)}, bf16[256,256]{1,0:T(8,128)(2,1)}, u32[]{:S(2)}) copy-start(bf16[256,256]{1,0:T(8,128)(2,1)} %constant.5.clone.dz_ref) | copy-start | bytes 393220
  0.6 13.0 %copy-start.1 = (bf16[256,128]{1,0:T(8,128)(2,1)S(1)}, bf16[256,128]{1,0:T(8,128)(2,1)}, u32[]{:S(2)}) copy-start(bf16[256,128]{1,0:T(8,128)(2,1)} %constant.4.clone.dx_ref) | copy-start | bytes 196612
  0.7 12.0 %copy-start.3 = (f32[192]{0:T(256)S(1)}, f32[192]{0:T(256)}, u32[]{:S(2)}) copy-start(f32[192]{0:T(256)} %upper_ref.1) | copy-start | bytes 2308
  0.7 12.0 %copy-start.2 = (f32[192]{0:T(256)S(1)}, f32[192]{0:T(256)}, u32[]{:S(2)}) copy-start(f32[192]{0:T(256)} %lower_ref.1) | copy-start | bytes 2308
  5.9 19.6 %collective-permute-start = (f32[3,12,8,256]{3,2,1,0:T(8,128)S(1)}, f32[3,12,8,256]{3,2,1,0:T(8,128)S(1)}, u32[]{:S(2)}, u32[]{:S(2)}) collective-permute-start(f32[3,12,8,256]{3,2,1,0:T(8,128)S(1)} %get-tuple-element.27.right_ref), channel_id=1, source_target_pairs={{0,8},{8,16},{16,24},{24,0},{1,9},{9,17},{17,25},{25,1},{2,10},{10... | collective-permute-start | bytes 884744 | tf_op jit(solution)/shard_map/ppermute | solution.py:562
  8.9 16.7 %collective-permute-start.1 = (f32[3,12,8,256]{3,2,1,0:T(8,128)S(1)}, f32[3,12,8,256]{3,2,1,0:T(8,128)S(1)}, u32[]{:S(2)}, u32[]{:S(2)}) collective-permute-start(f32[3,12,8,256]{3,2,1,0:T(8,128)S(1)} %get-tuple-element.28.left_ref), channel_id=1, source_target_pairs={{8,0},{16,8},{24,16},{0,24},{9,1},{17,9},{25,17},{1,25},{10,2},{18... | collective-permute-start | bytes 884744 | tf_op jit(solution)/shard_map/ppermute | solution.py:563
  9.9 15.6 %collective-permute-start.2 = (f32[3,1,32,128]{3,2,1,0:T(8,128)S(1)}, f32[3,1,32,128]{3,2,1,0:T(8,128)S(1)}, u32[]{:S(2)}, u32[]{:S(2)}) collective-permute-start(f32[3,1,32,128]{3,2,1,0:T(8,128)S(1)} %get-tuple-element.33), channel_id=1, source_target_pairs={{0,1},{1,2},{2,3},{3,4},{4,5},{5,6},{6,7},{8,9},{9,10},{10,11},{11... | collective-permute-start | bytes 147464 | tf_op jit(solution)/shard_map/ppermute | solution.py:564
  11.4 14.2 %collective-permute-start.3 = (f32[3,1,32,128]{3,2,1,0:T(8,128)S(1)}, f32[3,1,32,128]{3,2,1,0:T(8,128)S(1)}, u32[]{:S(2)}, u32[]{:S(2)}) collective-permute-start(f32[3,1,32,128]{3,2,1,0:T(8,128)S(1)} %get-tuple-element.34), channel_id=1, source_target_pairs={{1,0},{2,1},{3,2},{4,3},{5,4},{6,5},{7,6},{9,8},{10,9},{11,10},{12... | collective-permute-start | bytes 147464 | tf_op jit(solution)/shard_map/ppermute | solution.py:565
  27.0 4.2 %collective-permute-start.4 = (f32[200,128]{1,0:T(8,128)S(1)}, f32[200,128]{1,0:T(8,128)S(1)}, u32[]{:S(2)}, u32[]{:S(2)}) collective-permute-start(f32[200,128]{1,0:T(8,128)S(1)} %get-tuple-element.35.token.all_ref.load), channel_id=1, source_target_pairs={{0,1},{1,0},{2,3},{3,2},{4,5},{5,4},{6,7},{7,6},{8,9},{9,8},{10,11... | collective-permute-start | bytes 307208 | tf_op jit(solution)/shard_map/ppermute | solution.py:575
  31.3 5.4 %collective-permute-start.5 = (f32[200,128]{1,0:T(8,128)S(1)}, f32[200,128]{1,0:T(8,128)S(1)}, u32[]{:S(2)}, u32[]{:S(2)}) collective-permute-start(f32[200,128]{1,0:T(8,128)S(1)} %get-tuple-element.36.token.all_ref), channel_id=1, source_target_pairs={{0,2},{1,3},{2,0},{3,1},{4,6},{5,7},{6,4},{7,5},{8,10},{9,11},{10,... | collective-permute-start | bytes 307208 | tf_op jit(solution)/shard_map/ppermute | solution.py:575
  36.8 6.6 %collective-permute-start.6 = (f32[104,128]{1,0:T(8,128)S(1)}, f32[104,128]{1,0:T(8,128)S(1)}, u32[]{:S(2)}, u32[]{:S(2)}) collective-permute-start(f32[104,128]{1,0:T(8,128)S(1)} %get-tuple-element.43.token), channel_id=1, source_target_pairs={{0,4},{1,5},{2,6},{3,7},{4,0},{5,1},{6,2},{7,3},{8,12},{9,13},{10,... | collective-permute-start | bytes 159752 | tf_op jit(solution)/shard_map/ppermute | solution.py:575

commit v5 on v4

--- a/solution.py
+++ b/solution.py
@@ -61,7 +61,83 @@
     return pltpu.VMEM(shape, F32)
 
 
-def pack_kernel(group, v_hbm, vel, left_ref, right_ref, bottom_ref, top_ref, sems):
+def coef_kernel(n, group, lower_ref, upper_ref, vel_ref, out_ref, wide_ref, near_ref, far_ref, gap_ref):
+    width = out_ref.shape[1]
+    shape = (8, width)
+    lane = lax.broadcasted_iota(jnp.int32, shape, 1)
+    gap_ref[...] = jnp.ones_like(gap_ref)
+    gap_ref[0:8, 0:n] = jnp.broadcast_to(lower_ref[...].reshape(1, n), (8, n))
+    gap_ref[8:16, 0:n] = jnp.broadcast_to(upper_ref[...].reshape(1, n), (8, n))
+    lower, upper = gap_ref[0:8, :], gap_ref[8:16, :]
+    gap_sum = lower + upper
+    kappa = gap_sum * (0.5 / STIFF)
+    live = lane < n
+
+    def at(values, place):
+        return jnp.sum(jnp.where(lane == place, values, 0.0), axis=1, keepdims=True)
+
+    def sweep(gap, start, backward):
+        one, zero = jnp.ones(shape, F32), jnp.zeros(shape, F32)
+        m = [jnp.where(live, v, w) for v, w in
+             ((1.0 + gap * kappa, one), (gap, zero), (kappa, zero), (one, one))]
+        s = 1
+        while s < n:
+            inside = lane < width - s if backward else lane >= s
+            turn = width - s if backward else s
+            a, b, c, d = (jnp.where(inside, pltpu.roll(v, turn, 1), w)
+                          for v, w in zip(m, (one, zero, zero, one)))
+            m = [m[0] * a + m[1] * c, m[0] * b + m[1] * d, m[2] * a + m[3] * c, m[2] * b + m[3] * d]
+            s *= 2
+        return m[0] * start + m[1]
+
+    first, last = at(lower, 0), at(upper, n - 1)
+    phi_next = sweep(upper, first, False)
+    psi_next = sweep(lower, last, True)
+    phi = jnp.where(lane == 0, first, pltpu.roll(phi_next, 1, 1))
+    psi = jnp.where(lane == n - 1, last, pltpu.roll(psi_next, width - 1, 1))
+    scale = 1.0 / at(phi_next, n - 1)
+    forward, backward = phi * kappa, psi * kappa
+    out_ref[...] = jnp.zeros_like(out_ref)
+    for row, value in ((INV_GAP, (1.0 / UNIT) / gap_sum), (FORWARD, forward), (BACKWARD, backward),
+                       (PSI, psi * scale), (PHI, phi * scale), (OWN, upper / phi_next), (NEXT, phi / phi_next)):
+        out_ref[row : row + 1, :] = value[0:1]
+
+    pairs, rows = wide_ref.shape[1], wide_ref.shape[3]
+    y = lax.broadcasted_iota(jnp.int32, (pairs * 8, width), 1)
+    r = lax.broadcasted_iota(jnp.int32, (pairs * 8, width), 0)
+    mine = y // group == (r // 8) * 2 + (r & 7) // 4
+    fold = (lax.broadcasted_iota(jnp.int32, (width, rows), 0) % group
+            == lax.broadcasted_iota(jnp.int32, (width, rows), 1) // 32)
+    fold = jnp.where(fold, 1.0, 0.0).astype(BF16)
+    for t, value in enumerate((forward, backward)):
+        value = jnp.where(live, value, 0.0)
+        hi, lo = split(jnp.where(mine, jnp.broadcast_to(value[0:1], mine.shape), 0.0))
+        spread = jnp.dot(hi, fold, preferred_element_type=F32) + jnp.dot(lo, fold, preferred_element_type=F32)
+        wide_ref[t] = spread.reshape(pairs, 8, rows)
+
+    even = (lax.axis_index("gy") & 1) == 0
+    for c in range(3):
+        near_ref[c, 0] = jnp.where(even, vel_ref[c, n - 1], vel_ref[c, 0])
+        far_ref[c, 0] = jnp.where(even, vel_ref[c, 0], vel_ref[c, n - 1])
+
+
+def coefs(lower_gap, upper_gap, vel, group):
+    n = lower_gap.shape[0]
+    width = -(-n // 128) * 128
+    row = jax.ShapeDtypeStruct((3, 1, 32, 128), F32)
+    return pl.pallas_call(
+        functools.partial(coef_kernel, n, group),
+        in_specs=[vmem()] * 3,
+        out_specs=[vmem()] * 4,
+        out_shape=[jax.ShapeDtypeStruct((8, width), F32), held((2, n // (2 * group), 8, group * 32)), row, row],
+        scratch_shapes=[held((16, width))],
+        compiler_params=limit(4),
+        cost_estimate=cost(1e5),
+        name="coefficients",
+    )(lower_gap, upper_gap, vel)
+
+
+def pack_kernel(group, v_hbm, vel, pair_ref, left_ref, right_ref, sems):
     n = vel.shape[1]
     pairs = n // (2 * group)
 
@@ -84,27 +160,24 @@
             for h in range(2):
                 f = vel[c, pl.ds((2 * p + h) * group, group)].reshape(rows, 128)
                 pair = jnp.concatenate(split(f), axis=1)
+                pair_ref[c, pl.ds((2 * p + h) * rows, rows), :] = pair
                 picked.append(
                     lax.dot_general(pick, pair, (((1,), (1,)), ((), ())), preferred_element_type=F32)
                 )
             one, two = picked
             right_ref[c, p] = jnp.where(low, one[:8], two[8:])
             left_ref[c, p] = jnp.where(low, one[8:], two[:8])
-    for c in range(3):
-        bottom_ref[c, 0] = vel[c, 0]
-        top_ref[c, 0] = vel[c, n - 1]
 
 
 def pack(velocity, group):
     n = velocity.shape[1]
     pairs = n // (2 * group)
     packed = jax.ShapeDtypeStruct((3, pairs, 8, group * 32), F32)
-    row = jax.ShapeDtypeStruct((3, 1, 32, 128), F32)
     return pl.pallas_call(
         functools.partial(pack_kernel, group),
         in_specs=[pl.BlockSpec(memory_space=pltpu.HBM)],
-        out_specs=[vmem()] * 5,
-        out_shape=[held(velocity.shape), packed, packed, row, row],
+        out_specs=[vmem()] * 4,
+        out_shape=[held(velocity.shape), pltpu.VMEM((3, n * 32, 256), BF16), packed, packed],
         scratch_shapes=[pltpu.SemaphoreType.DMA((pairs,))],
         compiler_params=limit(8),
         cost_estimate=cost(velocity.size, 4 * velocity.size),
@@ -112,80 +185,9 @@
     )(pltpu.with_memory_space_constraint(velocity, pltpu.HBM))
 
 
-def coef_kernel(n, group, lower_ref, upper_ref, out_ref, wide_ref, gap_ref):
-    width = out_ref.shape[1]
-    shape = (8, width)
-    lane = lax.broadcasted_iota(jnp.int32, shape, 1)
-    gap_ref[...] = jnp.ones_like(gap_ref)
-    gap_ref[0:8, 0:n] = jnp.broadcast_to(lower_ref[...].reshape(1, n), (8, n))
-    gap_ref[8:16, 0:n] = jnp.broadcast_to(upper_ref[...].reshape(1, n), (8, n))
-    lower, upper = gap_ref[0:8, :], gap_ref[8:16, :]
-    gap_sum = lower + upper
-    kappa = gap_sum * (0.5 / STIFF)
-    live = lane < n
-
-    def at(values, place):
-        return jnp.sum(jnp.where(lane == place, values, 0.0), axis=1, keepdims=True)
-
-    def sweep(gap, start, backward):
-        one, zero = jnp.ones(shape, F32), jnp.zeros(shape, F32)
-        m = [jnp.where(live, v, w) for v, w in
-             ((1.0 + gap * kappa, one), (gap, zero), (kappa, zero), (one, one))]
-        s = 1
-        while s < n:
-            inside = lane < width - s if backward else lane >= s
-            turn = width - s if backward else s
-            a, b, c, d = (jnp.where(inside, pltpu.roll(v, turn, 1), w)
-                          for v, w in zip(m, (one, zero, zero, one)))
-            m = [m[0] * a + m[1] * c, m[0] * b + m[1] * d, m[2] * a + m[3] * c, m[2] * b + m[3] * d]
-            s *= 2
-        return m[0] * start + m[1]
-
-    first, last = at(lower, 0), at(upper, n - 1)
-    phi_next = sweep(upper, first, False)
-    psi_next = sweep(lower, last, True)
-    phi = jnp.where(lane == 0, first, pltpu.roll(phi_next, 1, 1))
-    psi = jnp.where(lane == n - 1, last, pltpu.roll(psi_next, width - 1, 1))
-    scale = 1.0 / at(phi_next, n - 1)
-    forward, backward = phi * kappa, psi * kappa
-    out_ref[...] = jnp.zeros_like(out_ref)
-    for row, value in ((INV_GAP, 1.0 / gap_sum), (FORWARD, forward), (BACKWARD, backward),
-                       (PSI, psi * scale), (PHI, phi * scale), (OWN, upper / phi_next), (NEXT, phi / phi_next)):
-        out_ref[row : row + 1, :] = value[0:1]
-
-    pairs, rows = wide_ref.shape[1], wide_ref.shape[3]
-    y = lax.broadcasted_iota(jnp.int32, (pairs * 8, width), 1)
-    r = lax.broadcasted_iota(jnp.int32, (pairs * 8, width), 0)
-    mine = y // group == (r // 8) * 2 + (r & 7) // 4
-    fold = (lax.broadcasted_iota(jnp.int32, (width, rows), 0) % group
-            == lax.broadcasted_iota(jnp.int32, (width, rows), 1) // 32)
-    fold = jnp.where(fold, 1.0, 0.0).astype(BF16)
-    for t, value in enumerate((forward, backward)):
-        value = jnp.where(live, value, 0.0)
-        hi, lo = split(jnp.where(mine, jnp.broadcast_to(value[0:1], mine.shape), 0.0))
-        spread = jnp.dot(hi, fold, preferred_element_type=F32) + jnp.dot(lo, fold, preferred_element_type=F32)
-        wide_ref[t] = spread.reshape(pairs, 8, rows)
-
-
-def coefs(lower_gap, upper_gap, group):
-    n = lower_gap.shape[0]
-    width = -(-n // 128) * 128
-    return pl.pallas_call(
-        functools.partial(coef_kernel, n, group),
-        in_specs=[vmem(), vmem()],
-        out_specs=[vmem(), vmem()],
-        out_shape=[jax.ShapeDtypeStruct((8, width), F32), held((2, n // (2 * group), 8, group * 32))],
-        scratch_shapes=[held((16, width))],
-        compiler_params=limit(8),
-        cost_estimate=cost(1e5),
-        name="coefficients",
-    )(lower_gap, upper_gap)
-
-
-def main_kernel(n, block, group, co, vel_ref, old_hbm, dx_ref, dz_ref, adv_ref, sum_ref, b_ref, old_ref, a_ref, sems):
+def main_plain(n, block, group, co, vel_ref, pair_ref, old_hbm, dx_ref, dz_ref, adv_ref, sum_ref, b_ref, old_ref, a_ref, w_ref, sems):
     steps = n // block
     rows = group * 32
-    nothing = jnp.zeros((32, 128), F32)
 
     def copy(step):
         here = pl.ds(step * block, block)
@@ -193,7 +195,6 @@
 
     for step in range(steps):
         copy(step).start()
-    a_ref[...] = jnp.zeros_like(a_ref)
     b_ref[...] = jnp.zeros_like(b_ref)
 
     def part(step, _):
@@ -203,21 +204,22 @@
             vel = [vel_ref[c, pl.ds(i0, group)].reshape(rows, 128) for c in range(3)]
             for c in range(3):
                 f = vel[c]
-                pair = jnp.concatenate(split(f), axis=1)
+                pair = pair_ref[c, pl.ds(i0 * 32, rows), :]
                 along_x = jnp.dot(pair, dx_ref[...], preferred_element_type=F32)
                 both = jnp.dot(dz_ref[...], pair, preferred_element_type=F32)
                 along_z = both[:, :128] + both[:, 128:]
-                below = jnp.where(i0 == 0, nothing, vel_ref[c, jnp.maximum(i0 - 1, 0)])
-                above = jnp.where(i0 == n - group, nothing, vel_ref[c, jnp.minimum(i0 + group, n - 1)])
-                up, down = a_ref[c], b_ref[c]
+                below = jnp.where(i0 == 0, 0.0, vel_ref[c, jnp.maximum(i0 - 1, 0)])
+                above = jnp.where(i0 == n - group, 0.0, vel_ref[c, jnp.minimum(i0 + group, n - 1)])
+                up = jnp.where(jnp.logical_or(i0 == 0, i0 == n // 2), 0.0, a_ref[c])
+                down = b_ref[c]
                 for y in range(group):
                     here = slice(32 * y, 32 * y + 32)
                     i = i0 + y
                     under = below if y == 0 else f[32 * y - 32 : 32 * y]
                     over = above if y == group - 1 else f[32 * y + 32 : 32 * y + 64]
-                    flat = (vel[0][here] * along_x[here] + vel[2][here] * along_z[here]) * (-UNIT)
-                    adv = flat - vel[1][here] * ((over - under) * co[INV_GAP, i])
-                    force = f[here] + GAMMA * adv + ZETA * old_ref[c, i]
+                    flat = vel[0][here] * along_x[here] + vel[2][here] * along_z[here]
+                    adv = flat + vel[1][here] * ((over - under) * co[INV_GAP, i])
+                    force = f[here] + (-UNIT * GAMMA) * adv + ZETA * old_ref[c, i]
                     up = up + co[FORWARD, i] * force
                     down = down + co[BACKWARD, i] * force
                     adv_ref[c, i] = adv
@@ -229,21 +231,115 @@
     lax.fori_loop(0, steps, part, 0)
 
 
-def main_part(vel, old, table, group, block):
+def main_kernel(n, block, group, co, vel_ref, pair_ref, old_hbm, dx_ref, dz_ref, adv_ref, sum_ref, b_ref, old_ref,
+                a_ref, w_ref, sems):
+    pairs = n // (2 * group)
+    half = n // 2
+    rows = group * 32
+    pieces = 4
+    high = rows // pieces
+
+    def copies(p):
+        found = []
+        for h in range(2):
+            here = pl.ds(h * half + p * group, group)
+            found.append(pltpu.make_async_copy(old_hbm.at[:, here], old_ref.at[:, here], sems.at[2 * p + h]))
+        return found
+
+    for p in range(pairs):
+        for copy in copies(p):
+            copy.start()
+    a_ref[...] = jnp.zeros_like(a_ref)
+    b_ref[...] = jnp.zeros_like(b_ref)
+
+    def run(*accs):
+        def issue(p, c, first=False):
+            parts = [pair_ref[c, pl.ds((h * half + p * group) * 32, rows), :] for h in range(2)]
+            for t in range(2):
+                side = jnp.concatenate([part[:, 128 * t : 128 * t + 128] for part in parts], axis=1)
+                pltpu.matmul_push_rhs(side, t, 1)
+                for q in range(pieces):
+                    here = slice(q * high, (q + 1) * high)
+                    fresh = 0 if first and t == 0 and q == 0 else None
+                    pltpu.matmul_acc_lhs(accs[c * 8 + q], side[here], load_staged_rhs=fresh)
+                    pltpu.matmul_acc_lhs(accs[c * 8 + 4 + q], dz_ref[here, :], load_staged_rhs=t if q == 0 else None)
+
+        def scale(p):
+            for h in range(2):
+                for y in range(group):
+                    i = h * half + p * group + y
+                    w_ref[h, y] = vel_ref[1, i] * co[INV_GAP, i]
+
+        def points(p, c):
+            up = [a_ref[h, c] for h in range(2)]
+            down = b_ref[c]
+            for q in range(pieces):
+                along_x = pltpu.matmul_pop(accs[c * 8 + q])
+                along_z = pltpu.matmul_pop(accs[c * 8 + 4 + q])
+                for h in range(2):
+                    lanes = slice(128 * h, 128 * h + 128)
+                    for k in range(group // pieces):
+                        y = q * (group // pieces) + k
+                        i = h * half + p * group + y
+                        here = slice(32 * k, 32 * k + 32)
+                        under = vel_ref[c, jnp.maximum(i - 1, 0)]
+                        over = vel_ref[c, jnp.minimum(i + 1, n - 1)]
+                        if h == 0 and y == 0:
+                            under = jnp.where(p == 0, 0.0, under)
+                        if h == 1 and y == group - 1:
+                            over = jnp.where(p == pairs - 1, 0.0, over)
+                        adv = vel_ref[0, i] * along_x[here, lanes] + vel_ref[2, i] * along_z[here, lanes]
+                        adv = adv + w_ref[h, y] * (over - under)
+                        force = vel_ref[c, i] + (-UNIT * GAMMA) * adv + ZETA * old_ref[c, i]
+                        up[h] = up[h] + co[FORWARD, i] * force
+                        down = down + co[BACKWARD, i] * force
+                        adv_ref[c, i] = adv
+                        sum_ref[c, i] = up[h]
+            for h in range(2):
+                a_ref[h, c] = up[h]
+            b_ref[c] = down
+
+        pltpu.matmul_push_rhs(dx_ref[...], 0, 0)
+        for c in range(3):
+            issue(0, c, c == 0)
+
+        def part(p, _):
+            for copy in copies(p):
+                copy.wait()
+            scale(p)
+            for c in range(3):
+                points(p, c)
+                issue(p + 1, c)
+            return 0
+
+        lax.fori_loop(0, pairs - 1, part, 0)
+        for copy in copies(pairs - 1):
+            copy.wait()
+        scale(pairs - 1)
+        for c in range(3):
+            points(pairs - 1, c)
+
+    pl.run_scoped(run, *(pltpu.ACC(unit)((high, 256), F32) for _ in range(3) for unit in range(2) for _ in range(pieces)))
+
+
+def main_part(vel, pair, old, table, group, block):
     n = vel.shape[1]
+    both_units = group == 8
     dx = shift_matrix(128, False)
-    dx = jnp.asarray(np.concatenate([dx, dx]), BF16)
+    dx = np.kron(np.eye(2), dx) if both_units else np.concatenate([dx, dx])
     dz = jnp.asarray(np.kron(np.eye(group), shift_matrix(32, True).T), BF16)
     return pl.pallas_call(
-        functools.partial(main_kernel, n, block, group),
-        in_specs=[smem(), vmem(), pl.BlockSpec(memory_space=pltpu.HBM), vmem(), vmem()],
+        functools.partial(main_kernel if both_units else main_plain, n, block, group),
+        in_specs=[smem(), vmem(), vmem(), pl.BlockSpec(memory_space=pltpu.HBM), vmem(), vmem()],
         out_specs=[vmem()] * 3,
         out_shape=[held(vel.shape), held(vel.shape), held((3, 32, 128))],
-        scratch_shapes=[held(vel.shape), held((3, 32, 128)), pltpu.SemaphoreType.DMA((n // block,))],
-        compiler_params=limit(12),
+        scratch_shapes=[held(vel.shape), held((2, 3, 32, 128) if both_units else (3, 32, 128)),
+                        held((2, group, 32, 128)),
+                        pltpu.SemaphoreType.DMA((n // group,))],
+        compiler_params=limit(15),
         cost_estimate=cost(25 * old.size, 4 * old.size),
         name="inner_part",
-    )(table, vel, pltpu.with_memory_space_constraint(old, pltpu.HBM), dx, dz)
+    )(table, vel, pair, pltpu.with_memory_space_constraint(old, pltpu.HBM), jnp.asarray(dx, BF16), dz)
 
 
 def place_matrix():
@@ -257,7 +353,8 @@
 
 
 def edge_kernel(pairs, group, co, from_left, from_right, left_ref, right_ref, sum_ref, b_ref, wide_ref,
-                low_ref, high_ref, vel_ref, extra_ref, rim_ref, load_ref):
+                near_ref, far_ref, vel_ref, extra_ref, rim_ref, load_ref):
+    even = (lax.axis_index("gy") & 1) == 0
     n = 2 * pairs * group
     rows = group * 32
     shape = (pairs, 8, rows)
@@ -279,8 +376,10 @@
         return parts
 
     for c in range(3):
-        rims = (vel_ref[1, 0] * low_ref[c, 0] * co[INV_GAP, 0],
-                -vel_ref[1, n - 1] * high_ref[c, 0] * co[INV_GAP, n - 1])
+        below = jnp.where(even, far_ref[c, 0], near_ref[c, 0])
+        above = jnp.where(even, near_ref[c, 0], far_ref[c, 0])
+        rims = (vel_ref[1, 0] * below * (UNIT * co[INV_GAP, 0]),
+                -vel_ref[1, n - 1] * above * (UNIT * co[INV_GAP, n - 1]))
         rim_ref[0, c], rim_ref[1, c] = rims
         adv, totals = [], []
         for side, halo, own in ((0, from_left, left_ref), (1, from_right, right_ref)):
@@ -303,7 +402,7 @@
             for h, value in ((0, jnp.where(low, l, swap(r))), (1, jnp.where(low, swap(l), r))):
                 extra_ref[c, 2 * p + h] = jnp.concatenate(split(value), axis=0)
         for t, (main, weight, row, i) in enumerate(
-            ((b_ref[c], BACKWARD, PHI, 0), (sum_ref[c, n - 1], FORWARD, PSI, n - 1))
+            ((b_ref[c], BACKWARD, PHI, 0), (sum_ref[c, n // 2 - 1] + sum_ref[c, n - 1], FORWARD, PSI, n - 1))
         ):
             main = main + (GAMMA * co[weight, 0]) * rims[0] + (GAMMA * co[weight, n - 1]) * rims[1]
             value = jnp.where(low[:, :32], totals[0][1 - t], totals[1][1 - t])
@@ -315,7 +414,7 @@
     load_ref[192:200, :] = jnp.where(row == 3, co[PHI, n - 1], ends)
 
 
-def edge_part(from_left, from_right, left, right, sums, b_sum, wide, low, high, vel, table, group):
+def edge_part(from_left, from_right, left, right, sums, b_sum, wide, near, far, vel, table, group):
     pairs = left.shape[1]
     return pl.pallas_call(
         functools.partial(edge_kernel, pairs, group),
@@ -326,7 +425,7 @@
         compiler_params=limit(8),
         cost_estimate=cost(40 * left.size),
         name="edge_part",
-    )(table, from_left, from_right, left, right, sums, b_sum, wide, low, high, vel)
+    )(table, from_left, from_right, left, right, sums, b_sum, wide, near, far, vel)
 
 
 def read(ref):
@@ -436,7 +535,7 @@
     n = adv_part.shape[1]
     if start:
         _, before_ref, adv_hbm, sum_ref, end_ref, adv_ref, sems = refs
-        end_ref[...] = before_ref[...]
+        end_ref[...] = before_ref[...] + sum_part[:, start - 1]
     else:
         adv_hbm, sum_ref, end_ref, adv_ref, sems = refs
         end_ref[...] = (GAMMA * co[FORWARD, 0]) * rim_ref[0]
@@ -456,7 +555,7 @@
                 for y in range(group):
                     i = here + y
                     extra = spread[32 * y : 32 * y + 32]
-                    adv_ref[c, i] = adv_part[c, start + i] + extra
+                    adv_ref[c, i] = adv_part[c, start + i] * (-UNIT) + extra
                     acc = acc + (GAMMA * co[FORWARD, start + i]) * extra
                     sum_ref[c, i] = sum_part[c, start + i] + acc
             end_ref[c] = acc
@@ -556,17 +655,18 @@
     block = 2 * group
     nx, ny = lax.axis_size("gx"), lax.axis_size("gy")
     ring = [(i, (i + 1) % nx) for i in range(nx)]
-    line = [(i, i + 1) for i in range(ny - 1)]
-
-    vel, left, right, bottom, top = pack(velocity, group)
+    pairs = [(i, i ^ 1) for i in range(ny)]
+    others = [(i, j) for k in range(1, ny - 1, 2) for i, j in ((k, k + 1), (k + 1, k))]
+
+    vel, pair, left, right = pack(velocity, group)
     from_left = lax.ppermute(right, "gx", ring)
     from_right = lax.ppermute(left, "gx", [(j, i) for i, j in ring])
-    below = lax.ppermute(top, "gy", line)
-    above = lax.ppermute(bottom, "gy", [(j, i) for i, j in line])
-    table, wide = coefs(lower_gap, upper_gap, group)
-    adv_part, sums, b_sum = main_part(vel, old_advection, table, group, block)
+    table, wide, near, far = coefs(lower_gap, upper_gap, vel, group)
+    near = lax.ppermute(near, "gy", pairs)
+    far = lax.ppermute(far, "gy", others)
+    adv_part, sums, b_sum = main_part(vel, pair, old_advection, table, group, block)
     extra, rims, load = edge_part(
-        from_left, from_right, left, right, sums, b_sum, wide, below, above, vel, table, group
+        from_left, from_right, left, right, sums, b_sum, wide, near, far, vel, table, group
     )
     bits = [1 << t for t in range(ny.bit_length() - 1)]
     half = n // 2

time: 48.2 us -> 44.7 us (0.927)
  starting transfers between devices: 14.7 us -> 11.1 us
  waiting for transfers between devices: 0.97 us -> 2.45 us
  Pallas kernels: 31.5 us -> 30.2 us
    ppermute x2, starting transfers between devices: 2.74 us -> 0.73 us  [the longest x1 0.66 us: shards(): far = lax.ppermute(far, 'gy', others)]
    ppermute x3, starting transfers between devices: 7.92 us -> 6.39 us  [shards(): other = lax.ppermute(whole, 'gy', [(i, i ^ bit) for i in range(ny)])]
    pallas_call x1, Pallas kernels: 11.9 us -> 10.5 us  [main_part(): pl.pallas_call(functools.partial(main_kernel if both_units else main_plai...]
    ppermute x1, waiting for transfers between devices: 0.01 us -> 1.33 us  [shards(): from_right = lax.ppermute(left, 'gx', [(j, i) for i, j in ring])]
  transfers between devices with their start and end apart: 7 -> 7, of which waited for: 1 -> 3; matrix products, arithmetic and copies ran while one was open for 0% -> 0% of each run, Pallas kernels for 42% -> 42%
where the time goes in v5:
time: 44.7 us; the launch traced here: 44.6 us
  Pallas kernels  30.2 us (68%)
  starting transfers between devices  11.1 us (25%)
  waiting for transfers between devices  2.45 us (5%)
  between operations  0.77 us (2%)
    pallas_call x1, Pallas kernels, main_part(): pl.pallas_call(functools.partial(main_kernel if both_units else main_plai...  10.5 us
    pallas_call x2, Pallas kernels, sweep_up(): pl.pallas_call(functools.partial(up_kernel, start, count, block, group),...  7.37 us
    ppermute x3, starting transfers between devices, shards(): other = lax.ppermute(whole, 'gy', [(i, i ^ bit) for i in range(ny)])  6.39 us
    pallas_call x1, Pallas kernels, pack(): pl.pallas_call(functools.partial(pack_kernel, group), in_specs=[pl.BlockS...  5.3 us
    pallas_call x1, Pallas kernels, sweep_down(): pl.pallas_call(functools.partial(down_kernel, bit, n, block), in_specs=[s...  4.58 us
    ppermute x1, starting transfers between devices, shards(): from_left = lax.ppermute(right, 'gx', ring)  2.99 us
    pallas_call x1, Pallas kernels, edge_part(): pl.pallas_call(functools.partial(edge_kernel, pairs, group), in_specs=[sm...  1.45 us
    ppermute x1, waiting for transfers between devices, shards(): from_right = lax.ppermute(left, 'gx', [(j, i) for i, j in ring])  1.33 us
  transfers between devices with their start and end apart: 7, of which 3 were waited for; matrix products, arithmetic and copies ran while one was open for 0% of the time, Pallas kernels for 42%

profile of v5, /device:TPU:0, one launch (start us, length us, event | category | flops | bytes accessed | tf_op | source)
XLA Modules:
  0.0 44.6 jit_solution(12939131423905068641)
XLA Ops:
  0.6 0.0 copy-start
  0.6 0.0 copy-start.1
  0.7 0.0 copy-start.3
  0.7 0.0 copy-start.2
  0.7 5.3 %pack_edges.1 = (f32[3,192,32,128]{3,2,1,0:T(8,128)S(1)}, bf16[3,6144,256]{2,1,0:T(8,128)(2,1)S(1)}, f32[3,12,8,256]{3,2,1,0:T(8,128)S(1)}, f32[3,12,8,256]{3,2,1,0:T(8,128)S(1)}) custom-call(f32[3,192,32,128]{3,2,1,0:T(8,128)} %v_hbm.1), custom_call_target="tpu_custom_call" | custom-call | flops 2359296 | bytes 9437184 | tf_op jit(solution)/shard_map/pack_edges/pallas_call | solution.py:176
  6.0 3.0 %collective-permute-start = (f32[3,12,8,256]{3,2,1,0:T(8,128)S(1)}, f32[3,12,8,256]{3,2,1,0:T(8,128)S(1)}, u32[]{:S(2)}, u32[]{:S(2)}) collective-permute-start(f32[3,12,8,256]{3,2,1,0:T(8,128)S(1)} %get-tuple-element.29.right_ref), channel_id=1, source_target_pairs={{0,8},{8,16},{16,24},{24,0},{1,9},{9,17},{17,25},{25,1},{2,10},{10... | collective-permute-start | bytes 884744 | tf_op jit(solution)/shard_map/ppermute | solution.py:662
  9.0 1.0 %collective-permute-start.1 = (f32[3,12,8,256]{3,2,1,0:T(8,128)S(1)}, f32[3,12,8,256]{3,2,1,0:T(8,128)S(1)}, u32[]{:S(2)}, u32[]{:S(2)}) collective-permute-start(f32[3,12,8,256]{3,2,1,0:T(8,128)S(1)} %get-tuple-element.30.left_ref), channel_id=1, source_target_pairs={{8,0},{16,8},{24,16},{0,24},{9,1},{17,9},{25,17},{1,25},{10,2},{18... | collective-permute-start | bytes 884744 | tf_op jit(solution)/shard_map/ppermute | solution.py:663
  10.0 0.0 copy-done.3
  10.0 0.0 copy-done.2
  10.0 0.9 %coefficients.1 = (f32[8,256]{1,0:T(8,128)S(1)}, f32[2,12,8,256]{3,2,1,0:T(8,128)S(1)}, f32[3,1,32,128]{3,2,1,0:T(8,128)S(1)}, f32[3,1,32,128]{3,2,1,0:T(8,128)S(1)}) custom-call(f32[192]{0:T(256)S(1)} %copy-done.2, f32[192]{0:T(256)S(1)} %copy-done.3, f32[3,192,32,128]{3,2,1,0:T(8,128)S(1)} %get-tuple-element.27.vel_ref), custom_call_target="tpu_custom_call" | custom-call | flops 100000 | tf_op jit(solution)/shard_map/coefficients/pallas_call | solution.py:128
  10.9 0.1 collective-permute-start.2
  11.0 0.7 %collective-permute-start.3 = (f32[3,1,32,128]{3,2,1,0:T(8,128)S(1)}, f32[3,1,32,128]{3,2,1,0:T(8,128)S(1)}, u32[]{:S(2)}, u32[]{:S(2)}) collective-permute-start(f32[3,1,32,128]{3,2,1,0:T(8,128)S(1)} %get-tuple-element.36), channel_id=1, source_target_pairs={{1,2},{2,1},{3,4},{4,3},{5,6},{6,5},{9,10},{10,9},{11,12},{12,11},... | collective-permute-start | bytes 147464 | tf_op jit(solution)/shard_map/ppermute | solution.py:666
  11.6 0.0 copy-done
  11.6 0.0 copy-done.1
  11.7 10.5 %inner_part.1 = (f32[3,192,32,128]{3,2,1,0:T(8,128)S(1)}, f32[3,192,32,128]{3,2,1,0:T(8,128)S(1)}, f32[3,32,128]{2,1,0:T(8,128)S(1)}) custom-call(f32[8,256]{1,0:T(8,128)S(1)} %get-tuple-element.28.co, f32[3,192,32,128]{3,2,1,0:T(8,128)S(1)} %get-tuple-element.27.vel_ref, bf16[3,6144,256]{2,1,0:T(8,128)(2,1)S(1)} %get-tuple-element.31.pair_ref, ...), custom_call_target="tpu_custom_call" | custom-call | flops 58982400 | bytes 9437184 | tf_op jit(solution)/shard_map/inner_part/pallas_call | solution.py:331
  22.1 0.0 collective-permute-done.2.near_ref
  22.2 0.0 collective-permute-done.3.far_ref
  22.2 0.0 collective-permute-done.from_left
  22.2 1.3 %collective-permute-done.1.from_right = f32[3,12,8,256]{3,2,1,0:T(8,128)S(1)} collective-permute-done((f32[3,12,8,256]{3,2,1,0:T(8,128)S(1)}, f32[3,12,8,256]{3,2,1,0:T(8,128)S(1)}, u32[]{:S(2)}, u32[]{:S(2)}) %collective-permute-start.1) | collective-permute-done | bytes 294944 | tf_op jit(solution)/shard_map/ppermute | solution.py:663
  23.5 1.5 %edge_part.1 = (bf16[3,24,16,256]{3,2,1,0:T(8,128)(2,1)S(1)}, f32[2,3,32,128]{3,2,1,0:T(8,128)S(1)}, f32[200,128]{1,0:T(8,128)S(1)}) custom-call(f32[8,256]{1,0:T(8,128)S(1)} %get-tuple-element.28.co, f32[3,12,8,256]{3,2,1,0:T(8,128)S(1)} %collective-permute-done.from_left, f32[3,12,8,256]{3,2,1,0:T(8,128)S(1)} %collective-permute-done.1.from_right, ...), custom_call_target="tpu_custom_call" | custom-call | flops 2949120 | tf_op jit(solution)/shard_map/edge_part/pallas_call | solution.py:419
  25.0 2.1 %collective-permute-start.4 = (f32[200,128]{1,0:T(8,128)S(1)}, f32[200,128]{1,0:T(8,128)S(1)}, u32[]{:S(2)}, u32[]{:S(2)}) collective-permute-start(f32[200,128]{1,0:T(8,128)S(1)} %get-tuple-element.37.token.all_ref.load), channel_id=1, source_target_pairs={{0,1},{1,0},{2,3},{3,2},{4,5},{5,4},{6,7},{7,6},{8,9},{9,8},{10,11... | collective-permute-start | bytes 307208 | tf_op jit(solution)/shard_map/ppermute | solution.py:675
  27.0 0.9 %collective-permute-done.4.other_ref = f32[200,128]{1,0:T(8,128)S(1)} collective-permute-done((f32[200,128]{1,0:T(8,128)S(1)}, f32[200,128]{1,0:T(8,128)S(1)}, u32[]{:S(2)}, u32[]{:S(2)}) %collective-permute-start.4) | collective-permute-done | bytes 102432 | tf_op jit(solution)/shard_map/ppermute | solution.py:675
  28.0 1.7 %collective-permute-start.5 = (f32[200,128]{1,0:T(8,128)S(1)}, f32[200,128]{1,0:T(8,128)S(1)}, u32[]{:S(2)}, u32[]{:S(2)}) collective-permute-start(f32[200,128]{1,0:T(8,128)S(1)} %get-tuple-element.38.token.all_ref), channel_id=1, source_target_pairs={{0,2},{1,3},{2,0},{3,1},{4,6},{5,7},{6,4},{7,5},{8,10},{9,11},{10,... | collective-permute-start | bytes 307208 | tf_op jit(solution)/shard_map/ppermute | solution.py:675
  29.7 3.4 %sweep_up.2 = (f32[3,192,32,128]{3,2,1,0:T(8,128)}, f32[3,96,32,128]{3,2,1,0:T(8,128)S(1)}, f32[3,32,128]{2,1,0:T(8,128)S(1)}) custom-call(f32[200,128]{1,0:T(8,128)S(1)} %get-tuple-element.38.token.all_ref, f32[8,256]{1,0:T(8,128)S(1)} %get-tuple-element.28.co, f32[3,192,32,128]{3,2,1,0:T(8,128)S(1)} %get-tuple-element.39.adv_part, ...), custom_call_target="tpu_custom_call" | custom-call | flops 9437184 | bytes 4718592 | tf_op jit(solution)/shard_map/sweep_up/pallas_call | solution.py:591
  33.1 0.2 collective-permute-done.5.other_ref
  33.2 0.1 join_runs.3
  33.3 2.7 %collective-permute-start.6 = (f32[104,128]{1,0:T(8,128)S(1)}, f32[104,128]{1,0:T(8,128)S(1)}, u32[]{:S(2)}, u32[]{:S(2)}) collective-permute-start(f32[104,128]{1,0:T(8,128)S(1)} %get-tuple-element.45.token), channel_id=1, source_target_pairs={{0,4},{1,5},{2,6},{3,7},{4,0},{5,1},{6,2},{7,3},{8,12},{9,13},{10,... | collective-permute-start | bytes 159752 | tf_op jit(solution)/shard_map/ppermute | solution.py:675
  36.0 4.0 %sweep_up.3 = (f32[3,192,32,128]{3,2,1,0:T(8,128)}, f32[3,96,32,128]{3,2,1,0:T(8,128)S(1)}, f32[3,32,128]{2,1,0:T(8,128)}) custom-call(f32[104,128]{1,0:T(8,128)S(1)} %get-tuple-element.45.token, f32[8,256]{1,0:T(8,128)S(1)} %get-tuple-element.28.co, f32[3,192,32,128]{3,2,1,0:T(8,128)S(1)} %get-tuple-element.39.adv_part, ...), custom_call_target="tpu_custom_call", output_to_operand_aliasing={{0}: (6, {})} | custom-call | flops 9437184 | bytes 4718592 | tf_op jit(solution)/shard_map/sweep_up/pallas_call | solution.py:591
  40.0 0.0 collective-permute-done.6.other
  40.0 4.6 %sweep_down.1 = f32[3,192,32,128]{3,2,1,0:T(8,128)} custom-call(f32[8,256]{1,0:T(8,128)S(1)} %get-tuple-element.28.co, f32[200,128]{1,0:T(8,128)S(1)} %get-tuple-element.37.token.all_ref.load, f32[104,128]{1,0:T(8,128)S(1)} %collective-permute-done.6.other, f32[200,128]{1,0:T(8,128)S(1)} %get-tuple-element.46.lower, f32[200,128]{1,0:T(8,128)S(1)} %get-tuple-element.47.upper, ...), custom_call_target="tpu_custom_call" | custom-call | flops 14155776 | bytes 9437184 | tf_op jit(solution)/shard_map/sweep_down/pallas_call | solution.py:640
  (1 shorter events, 0.0 us)
Async XLA Ops:
  0.6 11.0 %copy-start = (bf16[256,256]{1,0:T(8,128)(2,1)S(1)}, bf16[256,256]{1,0:T(8,128)(2,1)}, u32[]{:S(2)}) copy-start(bf16[256,256]{1,0:T(8,128)(2,1)} %constant.5.clone.dx_ref) | copy-start | bytes 393220
  0.6 11.0 %copy-start.1 = (bf16[256,256]{1,0:T(8,128)(2,1)S(1)}, bf16[256,256]{1,0:T(8,128)(2,1)}, u32[]{:S(2)}) copy-start(bf16[256,256]{1,0:T(8,128)(2,1)} %constant.4.clone.dz_ref) | copy-start | bytes 393220
  0.7 9.3 %copy-start.3 = (f32[192]{0:T(256)S(1)}, f32[192]{0:T(256)}, u32[]{:S(2)}) copy-start(f32[192]{0:T(256)} %upper_ref.1) | copy-start | bytes 2308
  0.7 9.3 %copy-start.2 = (f32[192]{0:T(256)S(1)}, f32[192]{0:T(256)}, u32[]{:S(2)}) copy-start(f32[192]{0:T(256)} %lower_ref.1) | copy-start | bytes 2308
  6.0 16.2 %collective-permute-start = (f32[3,12,8,256]{3,2,1,0:T(8,128)S(1)}, f32[3,12,8,256]{3,2,1,0:T(8,128)S(1)}, u32[]{:S(2)}, u32[]{:S(2)}) collective-permute-start(f32[3,12,8,256]{3,2,1,0:T(8,128)S(1)} %get-tuple-element.29.right_ref), channel_id=1, source_target_pairs={{0,8},{8,16},{16,24},{24,0},{1,9},{9,17},{17,25},{25,1},{2,10},{10... | collective-permute-start | bytes 884744 | tf_op jit(solution)/shard_map/ppermute | solution.py:662
  9.0 14.5 %collective-permute-start.1 = (f32[3,12,8,256]{3,2,1,0:T(8,128)S(1)}, f32[3,12,8,256]{3,2,1,0:T(8,128)S(1)}, u32[]{:S(2)}, u32[]{:S(2)}) collective-permute-start(f32[3,12,8,256]{3,2,1,0:T(8,128)S(1)} %get-tuple-element.30.left_ref), channel_id=1, source_target_pairs={{8,0},{16,8},{24,16},{0,24},{9,1},{17,9},{25,17},{1,25},{10,2},{18... | collective-permute-start | bytes 884744 | tf_op jit(solution)/shard_map/ppermute | solution.py:663
  10.9 11.3 %collective-permute-start.2 = (f32[3,1,32,128]{3,2,1,0:T(8,128)S(1)}, f32[3,1,32,128]{3,2,1,0:T(8,128)S(1)}, u32[]{:S(2)}, u32[]{:S(2)}) collective-permute-start(f32[3,1,32,128]{3,2,1,0:T(8,128)S(1)} %get-tuple-element.35), channel_id=1, source_target_pairs={{0,1},{1,0},{2,3},{3,2},{4,5},{5,4},{6,7},{7,6},{8,9},{9,8},{10,11... | collective-permute-start | bytes 147464 | tf_op jit(solution)/shard_map/ppermute | solution.py:665
  11.0 11.2 %collective-permute-start.3 = (f32[3,1,32,128]{3,2,1,0:T(8,128)S(1)}, f32[3,1,32,128]{3,2,1,0:T(8,128)S(1)}, u32[]{:S(2)}, u32[]{:S(2)}) collective-permute-start(f32[3,1,32,128]{3,2,1,0:T(8,128)S(1)} %get-tuple-element.36), channel_id=1, source_target_pairs={{1,2},{2,1},{3,4},{4,3},{5,6},{6,5},{9,10},{10,9},{11,12},{12,11},... | collective-permute-start | bytes 147464 | tf_op jit(solution)/shard_map/ppermute | solution.py:666
  25.0 3.0 %collective-permute-start.4 = (f32[200,128]{1,0:T(8,128)S(1)}, f32[200,128]{1,0:T(8,128)S(1)}, u32[]{:S(2)}, u32[]{:S(2)}) collective-permute-start(f32[200,128]{1,0:T(8,128)S(1)} %get-tuple-element.37.token.all_ref.load), channel_id=1, source_target_pairs={{0,1},{1,0},{2,3},{3,2},{4,5},{5,4},{6,7},{7,6},{8,9},{9,8},{10,11... | collective-permute-start | bytes 307208 | tf_op jit(solution)/shard_map/ppermute | solution.py:675
  28.0 5.2 %collective-permute-start.5 = (f32[200,128]{1,0:T(8,128)S(1)}, f32[200,128]{1,0:T(8,128)S(1)}, u32[]{:S(2)}, u32[]{:S(2)}) collective-permute-start(f32[200,128]{1,0:T(8,128)S(1)} %get-tuple-element.38.token.all_ref), channel_id=1, source_target_pairs={{0,2},{1,3},{2,0},{3,1},{4,6},{5,7},{6,4},{7,5},{8,10},{9,11},{10,... | collective-permute-start | bytes 307208 | tf_op jit(solution)/shard_map/ppermute | solution.py:675
  33.3 6.7 %collective-permute-start.6 = (f32[104,128]{1,0:T(8,128)S(1)}, f32[104,128]{1,0:T(8,128)S(1)}, u32[]{:S(2)}, u32[]{:S(2)}) collective-permute-start(f32[104,128]{1,0:T(8,128)S(1)} %get-tuple-element.45.token), channel_id=1, source_target_pairs={{0,4},{1,5},{2,6},{3,7},{4,0},{5,1},{6,2},{7,3},{8,12},{9,13},{10,... | collective-permute-start | bytes 159752 | tf_op jit(solution)/shard_map/ppermute | solution.py:675

commit v6 on v5

--- a/solution.py
+++ b/solution.py
@@ -231,38 +231,31 @@
     lax.fori_loop(0, steps, part, 0)
 
 
-def main_kernel(n, block, group, co, vel_ref, pair_ref, old_hbm, dx_ref, dz_ref, adv_ref, sum_ref, b_ref, old_ref,
-                a_ref, w_ref, sems):
+def main_kernel(n, block, group, co, vel_ref, pair_ref, old_ref, dx_ref, dz_ref, adv_ref, sum_ref, b_ref,
+                a_ref, w_ref):
     pairs = n // (2 * group)
     half = n // 2
     rows = group * 32
     pieces = 4
     high = rows // pieces
 
-    def copies(p):
-        found = []
-        for h in range(2):
-            here = pl.ds(h * half + p * group, group)
-            found.append(pltpu.make_async_copy(old_hbm.at[:, here], old_ref.at[:, here], sems.at[2 * p + h]))
-        return found
-
-    for p in range(pairs):
-        for copy in copies(p):
-            copy.start()
     a_ref[...] = jnp.zeros_like(a_ref)
     b_ref[...] = jnp.zeros_like(b_ref)
 
     def run(*accs):
         def issue(p, c, first=False):
             parts = [pair_ref[c, pl.ds((h * half + p * group) * 32, rows), :] for h in range(2)]
+            sides = [jnp.concatenate([part[:, 128 * t : 128 * t + 128] for part in parts], axis=1) for t in range(2)]
             for t in range(2):
-                side = jnp.concatenate([part[:, 128 * t : 128 * t + 128] for part in parts], axis=1)
-                pltpu.matmul_push_rhs(side, t, 1)
+                here = slice(t * rows // 2, (t + 1) * rows // 2)
+                pltpu.matmul_push_rhs(jnp.concatenate([side[here] for side in sides], axis=0), t, 1)
+            for t in range(2):
                 for q in range(pieces):
-                    here = slice(q * high, (q + 1) * high)
                     fresh = 0 if first and t == 0 and q == 0 else None
-                    pltpu.matmul_acc_lhs(accs[c * 8 + q], side[here], load_staged_rhs=fresh)
-                    pltpu.matmul_acc_lhs(accs[c * 8 + 4 + q], dz_ref[here, :], load_staged_rhs=t if q == 0 else None)
+                    pltpu.matmul_acc_lhs(accs[c * 8 + q], sides[t][q * high : (q + 1) * high], load_staged_rhs=fresh)
+                for q in range(2 * t, 2 * t + 2):
+                    here = slice((q % 2) * high, (q % 2 + 1) * high)
+                    pltpu.matmul_acc_lhs(accs[c * 8 + 4 + q], dz_ref[here, :], load_staged_rhs=t if q % 2 == 0 else None)
 
         def scale(p):
             for h in range(2):
@@ -304,8 +297,6 @@
             issue(0, c, c == 0)
 
         def part(p, _):
-            for copy in copies(p):
-                copy.wait()
             scale(p)
             for c in range(3):
                 points(p, c)
@@ -313,8 +304,6 @@
             return 0
 
         lax.fori_loop(0, pairs - 1, part, 0)
-        for copy in copies(pairs - 1):
-            copy.wait()
         scale(pairs - 1)
         for c in range(3):
             points(pairs - 1, c)
@@ -327,19 +316,19 @@
     both_units = group == 8
     dx = shift_matrix(128, False)
     dx = np.kron(np.eye(2), dx) if both_units else np.concatenate([dx, dx])
-    dz = jnp.asarray(np.kron(np.eye(group), shift_matrix(32, True).T), BF16)
+    dz = np.kron(np.eye(group // 2 if both_units else group), shift_matrix(32, True).T)
+    dz = jnp.asarray(np.concatenate([dz, dz], axis=1) if both_units else dz, BF16)
     return pl.pallas_call(
         functools.partial(main_kernel if both_units else main_plain, n, block, group),
-        in_specs=[smem(), vmem(), vmem(), pl.BlockSpec(memory_space=pltpu.HBM), vmem(), vmem()],
+        in_specs=[smem(), vmem(), vmem(), vmem() if both_units else pl.BlockSpec(memory_space=pltpu.HBM), vmem(), vmem()],
         out_specs=[vmem()] * 3,
         out_shape=[held(vel.shape), held(vel.shape), held((3, 32, 128))],
-        scratch_shapes=[held(vel.shape), held((2, 3, 32, 128) if both_units else (3, 32, 128)),
-                        held((2, group, 32, 128)),
-                        pltpu.SemaphoreType.DMA((n // group,))],
-        compiler_params=limit(15),
+        scratch_shapes=[held((2, 3, 32, 128)), held((2, group, 32, 128))] if both_units else [
+            held(vel.shape), held((3, 32, 128)), held((2, group, 32, 128)), pltpu.SemaphoreType.DMA((n // group,))],
+        compiler_params=limit(6),
         cost_estimate=cost(25 * old.size, 4 * old.size),
         name="inner_part",
-    )(table, vel, pair, pltpu.with_memory_space_constraint(old, pltpu.HBM), jnp.asarray(dx, BF16), dz)
+    )(table, vel, pair, old if both_units else pltpu.with_memory_space_constraint(old, pltpu.HBM), jnp.asarray(dx, BF16), dz)
 
 
 def place_matrix():

time: 44.7 us -> 43.5 us (0.973)
  Pallas kernels: 30.2 us -> 28.7 us
  starting transfers between devices: 11.1 us -> 9.91 us
  waiting for transfers between devices: 2.45 us -> 3.46 us
    pallas_call x1, Pallas kernels: 10.5 us -> 8.94 us  [main_part(): pl.pallas_call(functools.partial(main_kernel if both_units else main_plai...]
    ppermute x3, starting transfers between devices: 6.39 us -> 5.03 us  [shards(): other = lax.ppermute(whole, 'gy', [(i, i ^ bit) for i in range(ny)])]
    ppermute x1, waiting for transfers between devices: 1.33 us -> 2.34 us  [shards(): from_right = lax.ppermute(left, 'gx', [(j, i) for i, j in ring])]
  transfers between devices with their start and end apart: 7 -> 7, of which waited for: 3 -> 3; matrix products, arithmetic and copies ran while one was open for 0% -> 0% of each run, Pallas kernels for 42% -> 40%
where the time goes in v6:
time: 43.5 us; the launch traced here: 43.3 us
  Pallas kernels  28.7 us (66%)
  starting transfers between devices  9.91 us (23%)
  waiting for transfers between devices  3.46 us (8%)
  between operations  0.81 us (2%)
    pallas_call x1, Pallas kernels, main_part(): pl.pallas_call(functools.partial(main_kernel if both_units else main_plai...  8.94 us
    pallas_call x2, Pallas kernels, sweep_up(): pl.pallas_call(functools.partial(up_kernel, start, count, block, group),...  7.37 us
    pallas_call x1, Pallas kernels, pack(): pl.pallas_call(functools.partial(pack_kernel, group), in_specs=[pl.BlockS...  5.36 us
    ppermute x3, starting transfers between devices, shards(): other = lax.ppermute(whole, 'gy', [(i, i ^ bit) for i in range(ny)])  5.03 us
    pallas_call x1, Pallas kernels, sweep_down(): pl.pallas_call(functools.partial(down_kernel, bit, n, block), in_specs=[s...  4.58 us
    ppermute x1, starting transfers between devices, shards(): from_left = lax.ppermute(right, 'gx', ring)  2.99 us
    ppermute x1, waiting for transfers between devices, shards(): from_right = lax.ppermute(left, 'gx', [(j, i) for i, j in ring])  2.34 us
    pallas_call x1, Pallas kernels, edge_part(): pl.pallas_call(functools.partial(edge_kernel, pairs, group), in_specs=[sm...  1.46 us
  transfers between devices with their start and end apart: 7, of which 3 were waited for; matrix products, arithmetic and copies ran while one was open for 0% of the time, Pallas kernels for 40%

profile of v6, /device:TPU:0, one launch (start us, length us, event | category | flops | bytes accessed | tf_op | source)
XLA Modules:
  0.0 43.3 jit_solution(8606143821642453383)
XLA Ops:
  0.6 0.0 copy-start
  0.6 0.0 copy-start.1
  0.7 0.0 copy-start.3
  0.7 0.0 copy-start.2
  0.7 0.0 slice-start
  0.7 0.0 slice-start.1
  0.7 5.4 %pack_edges.1 = (f32[3,192,32,128]{3,2,1,0:T(8,128)S(1)}, bf16[3,6144,256]{2,1,0:T(8,128)(2,1)S(1)}, f32[3,12,8,256]{3,2,1,0:T(8,128)S(1)}, f32[3,12,8,256]{3,2,1,0:T(8,128)S(1)}) custom-call(f32[3,192,32,128]{3,2,1,0:T(8,128)} %v_hbm.1), custom_call_target="tpu_custom_call" | custom-call | flops 2359296 | bytes 9437184 | tf_op jit(solution)/shard_map/pack_edges/pallas_call | solution.py:176
  6.1 3.0 %collective-permute-start = (f32[3,12,8,256]{3,2,1,0:T(8,128)S(1)}, f32[3,12,8,256]{3,2,1,0:T(8,128)S(1)}, u32[]{:S(2)}, u32[]{:S(2)}) collective-permute-start(f32[3,12,8,256]{3,2,1,0:T(8,128)S(1)} %get-tuple-element.29.right_ref), channel_id=1, source_target_pairs={{0,8},{8,16},{16,24},{24,0},{1,9},{9,17},{17,25},{25,1},{2,10},{10... | collective-permute-start | bytes 884744 | tf_op jit(solution)/shard_map/ppermute | solution.py:651
  9.1 1.0 %collective-permute-start.1 = (f32[3,12,8,256]{3,2,1,0:T(8,128)S(1)}, f32[3,12,8,256]{3,2,1,0:T(8,128)S(1)}, u32[]{:S(2)}, u32[]{:S(2)}) collective-permute-start(f32[3,12,8,256]{3,2,1,0:T(8,128)S(1)} %get-tuple-element.30.left_ref), channel_id=1, source_target_pairs={{8,0},{16,8},{24,16},{0,24},{9,1},{17,9},{25,17},{1,25},{10,2},{18... | collective-permute-start | bytes 884744 | tf_op jit(solution)/shard_map/ppermute | solution.py:652
  10.1 0.0 copy-done.3
  10.1 0.0 copy-done.2
  10.1 0.0 slice-start.2
  10.1 0.9 %coefficients.1 = (f32[8,256]{1,0:T(8,128)S(1)}, f32[2,12,8,256]{3,2,1,0:T(8,128)S(1)}, f32[3,1,32,128]{3,2,1,0:T(8,128)S(1)}, f32[3,1,32,128]{3,2,1,0:T(8,128)S(1)}) custom-call(f32[192]{0:T(256)S(1)} %copy-done.2, f32[192]{0:T(256)S(1)} %copy-done.3, f32[3,192,32,128]{3,2,1,0:T(8,128)S(1)} %get-tuple-element.27.vel_ref), custom_call_target="tpu_custom_call" | custom-call | flops 100000 | tf_op jit(solution)/shard_map/coefficients/pallas_call | solution.py:128
  11.0 0.1 collective-permute-start.2
  11.0 0.8 %collective-permute-start.3 = (f32[3,1,32,128]{3,2,1,0:T(8,128)S(1)}, f32[3,1,32,128]{3,2,1,0:T(8,128)S(1)}, u32[]{:S(2)}, u32[]{:S(2)}) collective-permute-start(f32[3,1,32,128]{3,2,1,0:T(8,128)S(1)} %get-tuple-element.36), channel_id=1, source_target_pairs={{1,2},{2,1},{3,4},{4,3},{5,6},{6,5},{9,10},{10,9},{11,12},{12,11},... | collective-permute-start | bytes 147464 | tf_op jit(solution)/shard_map/ppermute | solution.py:655
  11.9 0.0 copy-done
  11.9 0.0 copy-done.1
  11.9 0.0 slice-done
  11.9 0.0 slice-done.1
  11.9 0.4 slice-done.2
  12.3 8.9 %inner_part.1 = (f32[3,192,32,128]{3,2,1,0:T(8,128)S(1)}, f32[3,192,32,128]{3,2,1,0:T(8,128)S(1)}, f32[3,32,128]{2,1,0:T(8,128)S(1)}) custom-call(f32[8,256]{1,0:T(8,128)S(1)} %get-tuple-element.28.co, f32[3,192,32,128]{3,2,1,0:T(8,128)S(1)} %get-tuple-element.27.vel_ref, bf16[3,6144,256]{2,1,0:T(8,128)(2,1)S(1)} %get-tuple-element.31.pair_ref, ...), custom_call_target="tpu_custom_call" | custom-call | flops 58982400 | bytes 9437184 | tf_op jit(solution)/shard_map/inner_part/pallas_call | solution.py:321
  21.2 0.0 collective-permute-done.2.near_ref
  21.2 0.0 collective-permute-done.3.far_ref
  21.2 0.0 collective-permute-done.from_left
  21.3 2.3 %collective-permute-done.1.from_right = f32[3,12,8,256]{3,2,1,0:T(8,128)S(1)} collective-permute-done((f32[3,12,8,256]{3,2,1,0:T(8,128)S(1)}, f32[3,12,8,256]{3,2,1,0:T(8,128)S(1)}, u32[]{:S(2)}, u32[]{:S(2)}) %collective-permute-start.1) | collective-permute-done | bytes 294944 | tf_op jit(solution)/shard_map/ppermute | solution.py:652
  23.6 1.5 %edge_part.1 = (bf16[3,24,16,256]{3,2,1,0:T(8,128)(2,1)S(1)}, f32[2,3,32,128]{3,2,1,0:T(8,128)S(1)}, f32[200,128]{1,0:T(8,128)S(1)}) custom-call(f32[8,256]{1,0:T(8,128)S(1)} %get-tuple-element.28.co, f32[3,12,8,256]{3,2,1,0:T(8,128)S(1)} %collective-permute-done.from_left, f32[3,12,8,256]{3,2,1,0:T(8,128)S(1)} %collective-permute-done.1.from_right, ...), custom_call_target="tpu_custom_call" | custom-call | flops 2949120 | tf_op jit(solution)/shard_map/edge_part/pallas_call | solution.py:408
  25.0 0.7 %collective-permute-start.4 = (f32[200,128]{1,0:T(8,128)S(1)}, f32[200,128]{1,0:T(8,128)S(1)}, u32[]{:S(2)}, u32[]{:S(2)}) collective-permute-start(f32[200,128]{1,0:T(8,128)S(1)} %get-tuple-element.37.token.all_ref.load), channel_id=1, source_target_pairs={{0,1},{1,0},{2,3},{3,2},{4,5},{5,4},{6,7},{7,6},{8,9},{9,8},{10,11... | collective-permute-start | bytes 307208 | tf_op jit(solution)/shard_map/ppermute | solution.py:664
  25.8 0.9 %collective-permute-done.4.other_ref = f32[200,128]{1,0:T(8,128)S(1)} collective-permute-done((f32[200,128]{1,0:T(8,128)S(1)}, f32[200,128]{1,0:T(8,128)S(1)}, u32[]{:S(2)}, u32[]{:S(2)}) %collective-permute-start.4) | collective-permute-done | bytes 102432 | tf_op jit(solution)/shard_map/ppermute | solution.py:664
  26.8 1.7 %collective-permute-start.5 = (f32[200,128]{1,0:T(8,128)S(1)}, f32[200,128]{1,0:T(8,128)S(1)}, u32[]{:S(2)}, u32[]{:S(2)}) collective-permute-start(f32[200,128]{1,0:T(8,128)S(1)} %get-tuple-element.38.token.all_ref), channel_id=1, source_target_pairs={{0,2},{1,3},{2,0},{3,1},{4,6},{5,7},{6,4},{7,5},{8,10},{9,11},{10,... | collective-permute-start | bytes 307208 | tf_op jit(solution)/shard_map/ppermute | solution.py:664
  28.4 3.4 %sweep_up.2 = (f32[3,192,32,128]{3,2,1,0:T(8,128)}, f32[3,96,32,128]{3,2,1,0:T(8,128)S(1)}, f32[3,32,128]{2,1,0:T(8,128)S(1)}) custom-call(f32[200,128]{1,0:T(8,128)S(1)} %get-tuple-element.38.token.all_ref, f32[8,256]{1,0:T(8,128)S(1)} %get-tuple-element.28.co, f32[3,192,32,128]{3,2,1,0:T(8,128)S(1)} %get-tuple-element.39.adv_part, ...), custom_call_target="tpu_custom_call" | custom-call | flops 9437184 | bytes 4718592 | tf_op jit(solution)/shard_map/sweep_up/pallas_call | solution.py:580
  31.8 0.2 collective-permute-done.5.other_ref
  32.0 0.1 join_runs.3
  32.1 2.7 %collective-permute-start.6 = (f32[104,128]{1,0:T(8,128)S(1)}, f32[104,128]{1,0:T(8,128)S(1)}, u32[]{:S(2)}, u32[]{:S(2)}) collective-permute-start(f32[104,128]{1,0:T(8,128)S(1)} %get-tuple-element.45.token), channel_id=1, source_target_pairs={{0,4},{1,5},{2,6},{3,7},{4,0},{5,1},{6,2},{7,3},{8,12},{9,13},{10,... | collective-permute-start | bytes 159752 | tf_op jit(solution)/shard_map/ppermute | solution.py:664
  34.7 4.0 %sweep_up.3 = (f32[3,192,32,128]{3,2,1,0:T(8,128)}, f32[3,96,32,128]{3,2,1,0:T(8,128)S(1)}, f32[3,32,128]{2,1,0:T(8,128)}) custom-call(f32[104,128]{1,0:T(8,128)S(1)} %get-tuple-element.45.token, f32[8,256]{1,0:T(8,128)S(1)} %get-tuple-element.28.co, f32[3,192,32,128]{3,2,1,0:T(8,128)S(1)} %get-tuple-element.39.adv_part, ...), custom_call_target="tpu_custom_call", output_to_operand_aliasing={{0}: (6, {})} | custom-call | flops 9437184 | bytes 4718592 | tf_op jit(solution)/shard_map/sweep_up/pallas_call | solution.py:580
  38.7 0.0 collective-permute-done.6.other
  38.7 4.6 %sweep_down.1 = f32[3,192,32,128]{3,2,1,0:T(8,128)} custom-call(f32[8,256]{1,0:T(8,128)S(1)} %get-tuple-element.28.co, f32[200,128]{1,0:T(8,128)S(1)} %get-tuple-element.37.token.all_ref.load, f32[104,128]{1,0:T(8,128)S(1)} %collective-permute-done.6.other, f32[200,128]{1,0:T(8,128)S(1)} %get-tuple-element.46.lower, f32[200,128]{1,0:T(8,128)S(1)} %get-tuple-element.47.upper, ...), custom_call_target="tpu_custom_call" | custom-call | flops 14155776 | bytes 9437184 | tf_op jit(solution)/shard_map/sweep_down/pallas_call | solution.py:629
  (2 shorter events, 0.0 us)
Async XLA Ops:
  0.6 11.2 %copy-start = (bf16[256,256]{1,0:T(8,128)(2,1)S(1)}, bf16[256,256]{1,0:T(8,128)(2,1)}, u32[]{:S(2)}) copy-start(bf16[256,256]{1,0:T(8,128)(2,1)} %constant.5.clone.dx_ref) | copy-start | bytes 393220
  0.6 11.2 %copy-start.1 = (bf16[128,256]{1,0:T(8,128)(2,1)S(1)}, bf16[128,256]{1,0:T(8,128)(2,1)}, u32[]{:S(2)}) copy-start(bf16[128,256]{1,0:T(8,128)(2,1)} %constant.4.clone.dz_ref) | copy-start | bytes 196612
  0.7 9.4 %copy-start.3 = (f32[192]{0:T(256)S(1)}, f32[192]{0:T(256)}, u32[]{:S(2)}) copy-start(f32[192]{0:T(256)} %upper_ref.1) | copy-start | bytes 2308
  0.7 9.4 %copy-start.2 = (f32[192]{0:T(256)S(1)}, f32[192]{0:T(256)}, u32[]{:S(2)}) copy-start(f32[192]{0:T(256)} %lower_ref.1) | copy-start | bytes 2308
  0.7 11.2 %slice-start = ((s8[9437184]{0:T(1024)(128)(4,1)}), s8[1048576]{0:T(1024)(128)(4,1)S(1)}, s32[]{:S(2)}) async-start(s8[9437184]{0:T(1024)(128)(4,1)} %bitcast), calls=%async_computation | async-start | bytes 2097152
  0.7 11.2 %slice-start.1 = ((s8[9437184]{0:T(1024)(128)(4,1)}), s8[4194304]{0:T(1024)(128)(4,1)S(1)}, s32[]{:S(2)}) async-start(s8[9437184]{0:T(1024)(128)(4,1)} %bitcast), calls=%async_computation.1 | async-start | bytes 8388608
  6.1 15.2 %collective-permute-start = (f32[3,12,8,256]{3,2,1,0:T(8,128)S(1)}, f32[3,12,8,256]{3,2,1,0:T(8,128)S(1)}, u32[]{:S(2)}, u32[]{:S(2)}) collective-permute-start(f32[3,12,8,256]{3,2,1,0:T(8,128)S(1)} %get-tuple-element.29.right_ref), channel_id=1, source_target_pairs={{0,8},{8,16},{16,24},{24,0},{1,9},{9,17},{17,25},{25,1},{2,10},{10... | collective-permute-start | bytes 884744 | tf_op jit(solution)/shard_map/ppermute | solution.py:651
  9.1 14.5 %collective-permute-start.1 = (f32[3,12,8,256]{3,2,1,0:T(8,128)S(1)}, f32[3,12,8,256]{3,2,1,0:T(8,128)S(1)}, u32[]{:S(2)}, u32[]{:S(2)}) collective-permute-start(f32[3,12,8,256]{3,2,1,0:T(8,128)S(1)} %get-tuple-element.30.left_ref), channel_id=1, source_target_pairs={{8,0},{16,8},{24,16},{0,24},{9,1},{17,9},{25,17},{1,25},{10,2},{18... | collective-permute-start | bytes 884744 | tf_op jit(solution)/shard_map/ppermute | solution.py:652
  10.1 2.2 %slice-start.2 = ((s8[9437184]{0:T(1024)(128)(4,1)}), s8[4194304]{0:T(1024)(128)(4,1)S(1)}, s32[]{:S(2)}) async-start(s8[9437184]{0:T(1024)(128)(4,1)} %bitcast), calls=%async_computation.2 | async-start | bytes 8388608
  11.0 10.3 %collective-permute-start.2 = (f32[3,1,32,128]{3,2,1,0:T(8,128)S(1)}, f32[3,1,32,128]{3,2,1,0:T(8,128)S(1)}, u32[]{:S(2)}, u32[]{:S(2)}) collective-permute-start(f32[3,1,32,128]{3,2,1,0:T(8,128)S(1)} %get-tuple-element.35), channel_id=1, source_target_pairs={{0,1},{1,0},{2,3},{3,2},{4,5},{5,4},{6,7},{7,6},{8,9},{9,8},{10,11... | collective-permute-start | bytes 147464 | tf_op jit(solution)/shard_map/ppermute | solution.py:654
  11.0 10.2 %collective-permute-start.3 = (f32[3,1,32,128]{3,2,1,0:T(8,128)S(1)}, f32[3,1,32,128]{3,2,1,0:T(8,128)S(1)}, u32[]{:S(2)}, u32[]{:S(2)}) collective-permute-start(f32[3,1,32,128]{3,2,1,0:T(8,128)S(1)} %get-tuple-element.36), channel_id=1, source_target_pairs={{1,2},{2,1},{3,4},{4,3},{5,6},{6,5},{9,10},{10,9},{11,12},{12,11},... | collective-permute-start | bytes 147464 | tf_op jit(solution)/shard_map/ppermute | solution.py:655
  25.0 1.7 %collective-permute-start.4 = (f32[200,128]{1,0:T(8,128)S(1)}, f32[200,128]{1,0:T(8,128)S(1)}, u32[]{:S(2)}, u32[]{:S(2)}) collective-permute-start(f32[200,128]{1,0:T(8,128)S(1)} %get-tuple-element.37.token.all_ref.load), channel_id=1, source_target_pairs={{0,1},{1,0},{2,3},{3,2},{4,5},{5,4},{6,7},{7,6},{8,9},{9,8},{10,11... | collective-permute-start | bytes 307208 | tf_op jit(solution)/shard_map/ppermute | solution.py:664
  26.8 5.2 %collective-permute-start.5 = (f32[200,128]{1,0:T(8,128)S(1)}, f32[200,128]{1,0:T(8,128)S(1)}, u32[]{:S(2)}, u32[]{:S(2)}) collective-permute-start(f32[200,128]{1,0:T(8,128)S(1)} %get-tuple-element.38.token.all_ref), channel_id=1, source_target_pairs={{0,2},{1,3},{2,0},{3,1},{4,6},{5,7},{6,4},{7,5},{8,10},{9,11},{10,... | collective-permute-start | bytes 307208 | tf_op jit(solution)/shard_map/ppermute | solution.py:664
  32.1 6.7 %collective-permute-start.6 = (f32[104,128]{1,0:T(8,128)S(1)}, f32[104,128]{1,0:T(8,128)S(1)}, u32[]{:S(2)}, u32[]{:S(2)}) collective-permute-start(f32[104,128]{1,0:T(8,128)S(1)} %get-tuple-element.45.token), channel_id=1, source_target_pairs={{0,4},{1,5},{2,6},{3,7},{4,0},{5,1},{6,2},{7,3},{8,12},{9,13},{10,... | collective-permute-start | bytes 159752 | tf_op jit(solution)/shard_map/ppermute | solution.py:664

commit v7 on v6

--- a/solution.py
+++ b/solution.py
@@ -41,10 +41,6 @@
     return lax.broadcasted_iota(jnp.int32, shape, len(shape) - 2)
 
 
-def smem():
-    return pl.BlockSpec(memory_space=pltpu.SMEM)
-
-
 def vmem():
     return pl.BlockSpec(memory_space=pltpu.VMEM)
 
@@ -62,7 +58,7 @@
 
 
 def coef_kernel(n, group, lower_ref, upper_ref, vel_ref, out_ref, wide_ref, near_ref, far_ref, gap_ref):
-    width = out_ref.shape[1]
+    width = gap_ref.shape[1]
     shape = (8, width)
     lane = lax.broadcasted_iota(jnp.int32, shape, 1)
     gap_ref[...] = jnp.ones_like(gap_ref)
@@ -97,10 +93,21 @@
     psi = jnp.where(lane == n - 1, last, pltpu.roll(psi_next, width - 1, 1))
     scale = 1.0 / at(phi_next, n - 1)
     forward, backward = phi * kappa, psi * kappa
-    out_ref[...] = jnp.zeros_like(out_ref)
+    sub = sublanes(shape)
+    table = jnp.zeros(shape, F32)
     for row, value in ((INV_GAP, (1.0 / UNIT) / gap_sum), (FORWARD, forward), (BACKWARD, backward),
                        (PSI, psi * scale), (PHI, phi * scale), (OWN, upper / phi_next), (NEXT, phi / phi_next)):
-        out_ref[row : row + 1, :] = value[0:1]
+        table = jnp.where(jnp.logical_and(sub == row, live), value, table)
+    high = split(table)[0]
+    middle, low = split(table - high.astype(F32))
+    parts = jnp.concatenate([high, middle, low, jnp.zeros_like(low)], axis=0)
+    count = out_ref.shape[0]
+    k = lax.broadcasted_iota(jnp.int32, (32, count * 128), 0)
+    t = lax.broadcasted_iota(jnp.int32, (32, count * 128), 1) // 128
+    pick = jnp.where(jnp.logical_and((k & 7) == t, k < 24), 1.0, 0.0).astype(BF16)
+    rows = lax.dot_general(parts, pick, (((0,), (0,)), ((), ())), preferred_element_type=F32)
+    for row in range(count):
+        out_ref[row] = rows[:n, 128 * row : 128 * row + 128]
 
     pairs, rows = wide_ref.shape[1], wide_ref.shape[3]
     y = lax.broadcasted_iota(jnp.int32, (pairs * 8, width), 1)
@@ -129,7 +136,7 @@
         functools.partial(coef_kernel, n, group),
         in_specs=[vmem()] * 3,
         out_specs=[vmem()] * 4,
-        out_shape=[jax.ShapeDtypeStruct((8, width), F32), held((2, n // (2 * group), 8, group * 32)), row, row],
+        out_shape=[held((NEXT + 1, n, 128)), held((2, n // (2 * group), 8, group * 32)), row, row],
         scratch_shapes=[held((16, width))],
         compiler_params=limit(4),
         cost_estimate=cost(1e5),
@@ -141,12 +148,15 @@
     n = vel.shape[1]
     pairs = n // (2 * group)
 
-    def copy(p):
-        rows = pl.ds(p * 2 * group, 2 * group)
-        return pltpu.make_async_copy(v_hbm.at[:, rows], vel.at[:, rows], sems.at[p])
-
-    for p in range(pairs):
-        copy(p).start()
+    cuts = [2, 2, 2, 2, 2, 2] if pairs == 12 else [1] * pairs
+    starts = [sum(cuts[:k]) for k in range(len(cuts))]
+
+    def copy(k):
+        rows = pl.ds(starts[k] * 2 * group, cuts[k] * 2 * group)
+        return pltpu.make_async_copy(v_hbm.at[:, rows], vel.at[:, rows], sems.at[k])
+
+    for k in range(len(cuts)):
+        copy(k).start()
     rows = group * 32
     low = sublanes((8, rows)) < 4
     r = lax.broadcasted_iota(jnp.int32, (16, 256), 0)
@@ -154,7 +164,8 @@
     inside = jnp.logical_or(r < 4, r >= 12)
     pick = jnp.where(lane == jnp.where(inside, 124, 0) + (r & 3), 1.0, 0.0).astype(BF16)
     for p in range(pairs):
-        copy(p).wait()
+        if p in starts:
+            copy(starts.index(p)).wait()
         for c in range(3):
             picked = []
             for h in range(2):
@@ -218,10 +229,10 @@
                     under = below if y == 0 else f[32 * y - 32 : 32 * y]
                     over = above if y == group - 1 else f[32 * y + 32 : 32 * y + 64]
                     flat = vel[0][here] * along_x[here] + vel[2][here] * along_z[here]
-                    adv = flat + vel[1][here] * ((over - under) * co[INV_GAP, i])
+                    adv = flat + vel[1][here] * ((over - under) * co[INV_GAP, pl.ds(i, 1), :])
                     force = f[here] + (-UNIT * GAMMA) * adv + ZETA * old_ref[c, i]
-                    up = up + co[FORWARD, i] * force
-                    down = down + co[BACKWARD, i] * force
+                    up = up + co[FORWARD, pl.ds(i, 1), :] * force
+                    down = down + co[BACKWARD, pl.ds(i, 1), :] * force
                     adv_ref[c, i] = adv
                     sum_ref[c, i] = up
                 a_ref[c] = up
@@ -261,7 +272,7 @@
             for h in range(2):
                 for y in range(group):
                     i = h * half + p * group + y
-                    w_ref[h, y] = vel_ref[1, i] * co[INV_GAP, i]
+                    w_ref[h, y] = vel_ref[1, i] * co[INV_GAP, pl.ds(i, 1), :]
 
         def points(p, c):
             up = [a_ref[h, c] for h in range(2)]
@@ -284,8 +295,8 @@
                         adv = vel_ref[0, i] * along_x[here, lanes] + vel_ref[2, i] * along_z[here, lanes]
                         adv = adv + w_ref[h, y] * (over - under)
                         force = vel_ref[c, i] + (-UNIT * GAMMA) * adv + ZETA * old_ref[c, i]
-                        up[h] = up[h] + co[FORWARD, i] * force
-                        down = down + co[BACKWARD, i] * force
+                        up[h] = up[h] + co[FORWARD, pl.ds(i, 1), :] * force
+                        down = down + co[BACKWARD, pl.ds(i, 1), :] * force
                         adv_ref[c, i] = adv
                         sum_ref[c, i] = up[h]
             for h in range(2):
@@ -320,7 +331,7 @@
     dz = jnp.asarray(np.concatenate([dz, dz], axis=1) if both_units else dz, BF16)
     return pl.pallas_call(
         functools.partial(main_kernel if both_units else main_plain, n, block, group),
-        in_specs=[smem(), vmem(), vmem(), vmem() if both_units else pl.BlockSpec(memory_space=pltpu.HBM), vmem(), vmem()],
+        in_specs=[vmem(), vmem(), vmem(), vmem() if both_units else pl.BlockSpec(memory_space=pltpu.HBM), vmem(), vmem()],
         out_specs=[vmem()] * 3,
         out_shape=[held(vel.shape), held(vel.shape), held((3, 32, 128))],
         scratch_shapes=[held((2, 3, 32, 128)), held((2, group, 32, 128))] if both_units else [
@@ -367,8 +378,8 @@
     for c in range(3):
         below = jnp.where(even, far_ref[c, 0], near_ref[c, 0])
         above = jnp.where(even, near_ref[c, 0], far_ref[c, 0])
-        rims = (vel_ref[1, 0] * below * (UNIT * co[INV_GAP, 0]),
-                -vel_ref[1, n - 1] * above * (UNIT * co[INV_GAP, n - 1]))
+        rims = (vel_ref[1, 0] * below * (UNIT * co[INV_GAP, pl.ds(0, 1), :]),
+                -vel_ref[1, n - 1] * above * (UNIT * co[INV_GAP, pl.ds(n - 1, 1), :]))
         rim_ref[0, c], rim_ref[1, c] = rims
         adv, totals = [], []
         for side, halo, own in ((0, from_left, left_ref), (1, from_right, right_ref)):
@@ -393,21 +404,21 @@
         for t, (main, weight, row, i) in enumerate(
             ((b_ref[c], BACKWARD, PHI, 0), (sum_ref[c, n // 2 - 1] + sum_ref[c, n - 1], FORWARD, PSI, n - 1))
         ):
-            main = main + (GAMMA * co[weight, 0]) * rims[0] + (GAMMA * co[weight, n - 1]) * rims[1]
+            main = main + (GAMMA * co[weight, pl.ds(0, 1), :]) * rims[0] + (GAMMA * co[weight, pl.ds(n - 1, 1), :]) * rims[1]
             value = jnp.where(low[:, :32], totals[0][1 - t], totals[1][1 - t])
             spread = spread_planes(jnp.concatenate(split(value), axis=0))
-            load_ref[pl.ds(t * 96 + c * 32, 32), :] = (main + spread) * co[row, i]
+            load_ref[pl.ds(t * 96 + c * 32, 32), :] = (main + spread) * co[row, pl.ds(i, 1), :]
     row = sublanes((8, 128))
-    ends = jnp.where(row == 0, co[PSI, 0], co[PSI, n - 1])
-    ends = jnp.where(row == 2, co[PHI, 0], ends)
-    load_ref[192:200, :] = jnp.where(row == 3, co[PHI, n - 1], ends)
+    ends = jnp.where(row == 0, co[PSI, pl.ds(0, 1), :], co[PSI, pl.ds(n - 1, 1), :])
+    ends = jnp.where(row == 2, co[PHI, pl.ds(0, 1), :], ends)
+    load_ref[192:200, :] = jnp.where(row == 3, co[PHI, pl.ds(n - 1, 1), :], ends)
 
 
 def edge_part(from_left, from_right, left, right, sums, b_sum, wide, near, far, vel, table, group):
     pairs = left.shape[1]
     return pl.pallas_call(
         functools.partial(edge_kernel, pairs, group),
-        in_specs=[smem()] + [vmem()] * 10,
+        in_specs=[vmem()] + [vmem()] * 10,
         out_specs=[vmem()] * 3,
         out_shape=[pltpu.VMEM((3, 2 * pairs, 16, group * 32), BF16), held((2, 3, 32, 128)),
                    jax.ShapeDtypeStruct((200, 128), F32)],
@@ -527,7 +538,7 @@
         end_ref[...] = before_ref[...] + sum_part[:, start - 1]
     else:
         adv_hbm, sum_ref, end_ref, adv_ref, sems = refs
-        end_ref[...] = (GAMMA * co[FORWARD, 0]) * rim_ref[0]
+        end_ref[...] = (GAMMA * co[FORWARD, pl.ds(0, 1), :]) * rim_ref[0]
     steps = count // block
 
     def copy(step):
@@ -545,7 +556,7 @@
                     i = here + y
                     extra = spread[32 * y : 32 * y + 32]
                     adv_ref[c, i] = adv_part[c, start + i] * (-UNIT) + extra
-                    acc = acc + (GAMMA * co[FORWARD, start + i]) * extra
+                    acc = acc + (GAMMA * co[FORWARD, pl.ds(start + i, 1), :]) * extra
                     sum_ref[c, i] = sum_part[c, start + i] + acc
             end_ref[c] = acc
 
@@ -558,7 +569,7 @@
             @pl.when(step == steps - 1)
             def _():
                 adv_ref[:, count - 1] = adv_ref[:, count - 1] + rim_ref[1]
-                sum_ref[:, count - 1] = sum_ref[:, count - 1] + (GAMMA * co[FORWARD, n - 1]) * rim_ref[1]
+                sum_ref[:, count - 1] = sum_ref[:, count - 1] + (GAMMA * co[FORWARD, pl.ds(n - 1, 1), :]) * rim_ref[1]
 
         copy(step).start()
         return 0
@@ -579,7 +590,7 @@
     part = (3, count, 32, 128)
     return pl.pallas_call(
         functools.partial(up_kernel, start, count, block, group),
-        in_specs=[pl.BlockSpec(memory_space=pl.ANY), smem()] + [vmem()] * 4 + ([hbm, vmem()] if before else []),
+        in_specs=[pl.BlockSpec(memory_space=pl.ANY), vmem()] + [vmem()] * 4 + ([hbm, vmem()] if before else []),
         out_specs=[hbm, vmem(), vmem()],
         out_shape=[jax.ShapeDtypeStruct(shape, F32), held(part), held((3, 32, 128))],
         scratch_shapes=[held(part), pltpu.SemaphoreType.DMA((count // block,))],
@@ -605,7 +616,7 @@
             step = steps // 2 - 1 - k
             for y in reversed(range(block)):
                 i = step * block + y
-                value = co[OWN, first + i] * (sum_ref[:, i] + below) + co[NEXT, first + i] * value
+                value = co[OWN, pl.ds(first + i, 1), :] * (sum_ref[:, i] + below) + co[NEXT, pl.ds(first + i, 1), :] * value
                 u_ref[:, first + i] = value
             copy(first // block + step).start()
             return value
@@ -628,7 +639,7 @@
     shape = (3, n, 32, 128)
     return pl.pallas_call(
         functools.partial(down_kernel, bit, n, block),
-        in_specs=[smem()] + [vmem()] * 6,
+        in_specs=[vmem()] + [vmem()] * 6,
         out_specs=pl.BlockSpec(memory_space=pltpu.HBM),
         out_shape=jax.ShapeDtypeStruct(shape, F32),
         scratch_shapes=[held(shape), held((96, 128)), held((96, 128)), pltpu.SemaphoreType.DMA((n // block,))],

time: 43.5 us -> 40.4 us (0.929)
  Pallas kernels: 28.7 us -> 24.9 us
  waiting for transfers between devices: 3.46 us -> 5.08 us
  starting transfers between devices: 9.91 us -> 9.22 us
    pallas_call x2, Pallas kernels: 6.04 us -> 4.71 us  [the longest x1 3.91 us: sweep_down(): pl.pallas_call(functools.partial(down_kernel, bit, n, block), in_specs=[v...]
    pallas_call x2, Pallas kernels: 7.37 us -> 6.04 us  [sweep_up(): pl.pallas_call(functools.partial(up_kernel, start, count, block, group),...]
    ppermute x3, waiting for transfers between devices: 1.12 us -> 1.94 us  [shards(): other = lax.ppermute(whole, 'gy', [(i, i ^ bit) for i in range(ny)])]
    ppermute x1, waiting for transfers between devices: 2.34 us -> 3.13 us  [shards(): from_right = lax.ppermute(left, 'gx', [(j, i) for i, j in ring])]
    pallas_call x1, Pallas kernels: 8.94 us -> 8.15 us  [main_part(): pl.pallas_call(functools.partial(main_kernel if both_units else main_plai...]
    ppermute x3, starting transfers between devices: 5.03 us -> 4.34 us  [shards(): other = lax.ppermute(whole, 'gy', [(i, i ^ bit) for i in range(ny)])]
    pallas_call x1, Pallas kernels: 5.36 us -> 4.86 us  [pack(): pl.pallas_call(functools.partial(pack_kernel, group), in_specs=[pl.BlockS...]
  transfers between devices with their start and end apart: 7 -> 7, of which waited for: 3 -> 3; matrix products, arithmetic and copies ran while one was open for 0% -> 0% of each run, Pallas kernels for 40% -> 38%
where the time goes in v7:
time: 40.4 us; the launch traced here: 40.3 us
  Pallas kernels  24.9 us (62%)
  starting transfers between devices  9.22 us (23%)
  waiting for transfers between devices  5.08 us (13%)
  between operations  0.81 us (2%)
    pallas_call x1, Pallas kernels, main_part(): pl.pallas_call(functools.partial(main_kernel if both_units else main_plai...  8.15 us
    pallas_call x2, Pallas kernels, sweep_up(): pl.pallas_call(functools.partial(up_kernel, start, count, block, group),...  6.04 us
    pallas_call x1, Pallas kernels, pack(): pl.pallas_call(functools.partial(pack_kernel, group), in_specs=[pl.BlockS...  4.86 us
    ppermute x3, starting transfers between devices, shards(): other = lax.ppermute(whole, 'gy', [(i, i ^ bit) for i in range(ny)])  4.34 us
    pallas_call x1, Pallas kernels, sweep_down(): pl.pallas_call(functools.partial(down_kernel, bit, n, block), in_specs=[v...  3.91 us
    ppermute x1, waiting for transfers between devices, shards(): from_right = lax.ppermute(left, 'gx', [(j, i) for i, j in ring])  3.13 us
    ppermute x1, starting transfers between devices, shards(): from_left = lax.ppermute(right, 'gx', ring)  2.99 us
    ppermute x3, waiting for transfers between devices, shards(): other = lax.ppermute(whole, 'gy', [(i, i ^ bit) for i in range(ny)])  1.94 us
  transfers between devices with their start and end apart: 7, of which 3 were waited for; matrix products, arithmetic and copies ran while one was open for 0% of the time, Pallas kernels for 38%

profile of v7, /device:TPU:0, one launch (start us, length us, event | category | flops | bytes accessed | tf_op | source)
XLA Modules:
  0.0 40.3 jit_solution(8115860058156872149)
XLA Ops:
  0.6 0.0 copy-start
  0.6 0.0 copy-start.1
  0.7 0.0 copy-start.3
  0.7 0.0 copy-start.2
  0.7 0.0 slice-start
  0.7 0.0 slice-start.1
  0.7 4.9 %pack_edges.1 = (f32[3,192,32,128]{3,2,1,0:T(8,128)S(1)}, bf16[3,6144,256]{2,1,0:T(8,128)(2,1)S(1)}, f32[3,12,8,256]{3,2,1,0:T(8,128)S(1)}, f32[3,12,8,256]{3,2,1,0:T(8,128)S(1)}) custom-call(f32[3,192,32,128]{3,2,1,0:T(8,128)} %v_hbm.1), custom_call_target="tpu_custom_call" | custom-call | flops 2359296 | bytes 9437184 | tf_op jit(solution)/shard_map/pack_edges/pallas_call | solution.py:187
  5.6 3.0 %collective-permute-start = (f32[3,12,8,256]{3,2,1,0:T(8,128)S(1)}, f32[3,12,8,256]{3,2,1,0:T(8,128)S(1)}, u32[]{:S(2)}, u32[]{:S(2)}) collective-permute-start(f32[3,12,8,256]{3,2,1,0:T(8,128)S(1)} %get-tuple-element.29.right_ref), channel_id=1, source_target_pairs={{0,8},{8,16},{16,24},{24,0},{1,9},{9,17},{17,25},{25,1},{2,10},{10... | collective-permute-start | bytes 884744 | tf_op jit(solution)/shard_map/ppermute | solution.py:662
  8.6 1.0 %collective-permute-start.1 = (f32[3,12,8,256]{3,2,1,0:T(8,128)S(1)}, f32[3,12,8,256]{3,2,1,0:T(8,128)S(1)}, u32[]{:S(2)}, u32[]{:S(2)}) collective-permute-start(f32[3,12,8,256]{3,2,1,0:T(8,128)S(1)} %get-tuple-element.30.left_ref), channel_id=1, source_target_pairs={{8,0},{16,8},{24,16},{0,24},{9,1},{17,9},{25,17},{1,25},{10,2},{18... | collective-permute-start | bytes 884744 | tf_op jit(solution)/shard_map/ppermute | solution.py:663
  9.6 0.0 copy-done.3
  9.6 0.0 copy-done.2
  9.6 0.0 slice-start.2
  9.6 1.0 %coefficients.1 = (f32[7,192,128]{2,1,0:T(8,128)S(1)}, f32[2,12,8,256]{3,2,1,0:T(8,128)S(1)}, f32[3,1,32,128]{3,2,1,0:T(8,128)S(1)}, f32[3,1,32,128]{3,2,1,0:T(8,128)S(1)}) custom-call(f32[192]{0:T(256)S(1)} %copy-done.2, f32[192]{0:T(256)S(1)} %copy-done.3, f32[3,192,32,128]{3,2,1,0:T(8,128)S(1)} %get-tuple-element.27.vel_ref), custom_call_target="tpu_custom_call" | custom-call | flops 100000 | tf_op jit(solution)/shard_map/coefficients/pallas_call | solution.py:135
  10.6 0.1 collective-permute-start.2
  10.7 0.8 %collective-permute-start.3 = (f32[3,1,32,128]{3,2,1,0:T(8,128)S(1)}, f32[3,1,32,128]{3,2,1,0:T(8,128)S(1)}, u32[]{:S(2)}, u32[]{:S(2)}) collective-permute-start(f32[3,1,32,128]{3,2,1,0:T(8,128)S(1)} %get-tuple-element.36), channel_id=1, source_target_pairs={{1,2},{2,1},{3,4},{4,3},{5,6},{6,5},{9,10},{10,9},{11,12},{12,11},... | collective-permute-start | bytes 147464 | tf_op jit(solution)/shard_map/ppermute | solution.py:666
  11.5 0.0 copy-done
  11.5 0.0 copy-done.1
  11.5 0.0 slice-done
  11.5 0.0 slice-done.1
  11.5 0.2 slice-done.2
  11.8 8.1 %inner_part.1 = (f32[3,192,32,128]{3,2,1,0:T(8,128)S(1)}, f32[3,192,32,128]{3,2,1,0:T(8,128)S(1)}, f32[3,32,128]{2,1,0:T(8,128)S(1)}) custom-call(f32[7,192,128]{2,1,0:T(8,128)S(1)} %get-tuple-element.28.co, f32[3,192,32,128]{3,2,1,0:T(8,128)S(1)} %get-tuple-element.27.vel_ref, bf16[3,6144,256]{2,1,0:T(8,128)(2,1)S(1)} %get-tuple-element.31.pair_ref, ...), custom_call_target="tpu_custom_call" | custom-call | flops 58982400 | bytes 9437184 | tf_op jit(solution)/shard_map/inner_part/pallas_call | solution.py:332
  19.9 0.0 collective-permute-done.2.near_ref
  19.9 0.0 collective-permute-done.3.far_ref
  19.9 0.0 collective-permute-done.from_left
  20.0 3.1 %collective-permute-done.1.from_right = f32[3,12,8,256]{3,2,1,0:T(8,128)S(1)} collective-permute-done((f32[3,12,8,256]{3,2,1,0:T(8,128)S(1)}, f32[3,12,8,256]{3,2,1,0:T(8,128)S(1)}, u32[]{:S(2)}, u32[]{:S(2)}) %collective-permute-start.1) | collective-permute-done | bytes 294944 | tf_op jit(solution)/shard_map/ppermute | solution.py:663
  23.1 0.8 %edge_part.1 = (bf16[3,24,16,256]{3,2,1,0:T(8,128)(2,1)S(1)}, f32[2,3,32,128]{3,2,1,0:T(8,128)S(1)}, f32[200,128]{1,0:T(8,128)S(1)}) custom-call(f32[7,192,128]{2,1,0:T(8,128)S(1)} %get-tuple-element.28.co, f32[3,12,8,256]{3,2,1,0:T(8,128)S(1)} %collective-permute-done.from_left, f32[3,12,8,256]{3,2,1,0:T(8,128)S(1)} %collective-permute-done.1.from_right, ...), custom_call_target="tpu_custom_call" | custom-call | flops 2949120 | tf_op jit(solution)/shard_map/edge_part/pallas_call | solution.py:419
  23.9 0.0 collective-permute-start.4
  23.9 1.3 %collective-permute-done.4.other_ref = f32[200,128]{1,0:T(8,128)S(1)} collective-permute-done((f32[200,128]{1,0:T(8,128)S(1)}, f32[200,128]{1,0:T(8,128)S(1)}, u32[]{:S(2)}, u32[]{:S(2)}) %collective-permute-start.4) | collective-permute-done | bytes 102432 | tf_op jit(solution)/shard_map/ppermute | solution.py:675
  25.3 1.6 %collective-permute-start.5 = (f32[200,128]{1,0:T(8,128)S(1)}, f32[200,128]{1,0:T(8,128)S(1)}, u32[]{:S(2)}, u32[]{:S(2)}) collective-permute-start(f32[200,128]{1,0:T(8,128)S(1)} %get-tuple-element.38.token.all_ref), channel_id=1, source_target_pairs={{0,2},{1,3},{2,0},{3,1},{4,6},{5,7},{6,4},{7,5},{8,10},{9,11},{10,... | collective-permute-start | bytes 307208 | tf_op jit(solution)/shard_map/ppermute | solution.py:675
  26.9 2.7 %sweep_up.2 = (f32[3,192,32,128]{3,2,1,0:T(8,128)}, f32[3,96,32,128]{3,2,1,0:T(8,128)S(1)}, f32[3,32,128]{2,1,0:T(8,128)S(1)}) custom-call(f32[200,128]{1,0:T(8,128)S(1)} %get-tuple-element.38.token.all_ref, f32[7,192,128]{2,1,0:T(8,128)S(1)} %get-tuple-element.28.co, f32[3,192,32,128]{3,2,1,0:T(8,128)S(1)} %get-tuple-element.39.adv_part, ...), custom_call_target="tpu_custom_call" | custom-call | flops 9437184 | bytes 4718592 | tf_op jit(solution)/shard_map/sweep_up/pallas_call | solution.py:591
  29.6 0.6 %collective-permute-done.5.other_ref = f32[200,128]{1,0:T(8,128)S(1)} collective-permute-done((f32[200,128]{1,0:T(8,128)S(1)}, f32[200,128]{1,0:T(8,128)S(1)}, u32[]{:S(2)}, u32[]{:S(2)}) %collective-permute-start.5) | collective-permute-done | bytes 102432 | tf_op jit(solution)/shard_map/ppermute | solution.py:675
  30.3 0.1 join_runs.3
  30.4 2.7 %collective-permute-start.6 = (f32[104,128]{1,0:T(8,128)S(1)}, f32[104,128]{1,0:T(8,128)S(1)}, u32[]{:S(2)}, u32[]{:S(2)}) collective-permute-start(f32[104,128]{1,0:T(8,128)S(1)} %get-tuple-element.45.token), channel_id=1, source_target_pairs={{0,4},{1,5},{2,6},{3,7},{4,0},{5,1},{6,2},{7,3},{8,12},{9,13},{10,... | collective-permute-start | bytes 159752 | tf_op jit(solution)/shard_map/ppermute | solution.py:675
  33.0 3.3 %sweep_up.3 = (f32[3,192,32,128]{3,2,1,0:T(8,128)}, f32[3,96,32,128]{3,2,1,0:T(8,128)S(1)}, f32[3,32,128]{2,1,0:T(8,128)}) custom-call(f32[104,128]{1,0:T(8,128)S(1)} %get-tuple-element.45.token, f32[7,192,128]{2,1,0:T(8,128)S(1)} %get-tuple-element.28.co, f32[3,192,32,128]{3,2,1,0:T(8,128)S(1)} %get-tuple-element.39.adv_part, ...), custom_call_target="tpu_custom_call", output_to_operand_aliasing={{0}: (6, {})} | custom-call | flops 9437184 | bytes 4718592 | tf_op jit(solution)/shard_map/sweep_up/pallas_call | solution.py:591
  36.4 0.0 collective-permute-done.6.other
  36.4 3.9 %sweep_down.1 = f32[3,192,32,128]{3,2,1,0:T(8,128)} custom-call(f32[7,192,128]{2,1,0:T(8,128)S(1)} %get-tuple-element.28.co, f32[200,128]{1,0:T(8,128)S(1)} %get-tuple-element.37.token.all_ref.load, f32[104,128]{1,0:T(8,128)S(1)} %collective-permute-done.6.other, f32[200,128]{1,0:T(8,128)S(1)} %get-tuple-element.46.lower, ...), custom_call_target="tpu_custom_call" | custom-call | flops 14155776 | bytes 9437184 | tf_op jit(solution)/shard_map/sweep_down/pallas_call | solution.py:640
  (2 shorter events, 0.0 us)
Async XLA Ops:
  0.6 10.9 %copy-start = (bf16[256,256]{1,0:T(8,128)(2,1)S(1)}, bf16[256,256]{1,0:T(8,128)(2,1)}, u32[]{:S(2)}) copy-start(bf16[256,256]{1,0:T(8,128)(2,1)} %constant.5.clone.dx_ref) | copy-start | bytes 393220
  0.6 10.9 %copy-start.1 = (bf16[128,256]{1,0:T(8,128)(2,1)S(1)}, bf16[128,256]{1,0:T(8,128)(2,1)}, u32[]{:S(2)}) copy-start(bf16[128,256]{1,0:T(8,128)(2,1)} %constant.4.clone.dz_ref) | copy-start | bytes 196612
  0.7 8.9 %copy-start.3 = (f32[192]{0:T(256)S(1)}, f32[192]{0:T(256)}, u32[]{:S(2)}) copy-start(f32[192]{0:T(256)} %upper_ref.1) | copy-start | bytes 2308
  0.7 8.9 %copy-start.2 = (f32[192]{0:T(256)S(1)}, f32[192]{0:T(256)}, u32[]{:S(2)}) copy-start(f32[192]{0:T(256)} %lower_ref.1) | copy-start | bytes 2308
  0.7 10.8 %slice-start = ((s8[9437184]{0:T(1024)(128)(4,1)}), s8[1048576]{0:T(1024)(128)(4,1)S(1)}, s32[]{:S(2)}) async-start(s8[9437184]{0:T(1024)(128)(4,1)} %bitcast), calls=%async_computation | async-start | bytes 2097152
  0.7 10.8 %slice-start.1 = ((s8[9437184]{0:T(1024)(128)(4,1)}), s8[4194304]{0:T(1024)(128)(4,1)S(1)}, s32[]{:S(2)}) async-start(s8[9437184]{0:T(1024)(128)(4,1)} %bitcast), calls=%async_computation.1 | async-start | bytes 8388608
  5.6 14.4 %collective-permute-start = (f32[3,12,8,256]{3,2,1,0:T(8,128)S(1)}, f32[3,12,8,256]{3,2,1,0:T(8,128)S(1)}, u32[]{:S(2)}, u32[]{:S(2)}) collective-permute-start(f32[3,12,8,256]{3,2,1,0:T(8,128)S(1)} %get-tuple-element.29.right_ref), channel_id=1, source_target_pairs={{0,8},{8,16},{16,24},{24,0},{1,9},{9,17},{17,25},{25,1},{2,10},{10... | collective-permute-start | bytes 884744 | tf_op jit(solution)/shard_map/ppermute | solution.py:662
  8.6 14.5 %collective-permute-start.1 = (f32[3,12,8,256]{3,2,1,0:T(8,128)S(1)}, f32[3,12,8,256]{3,2,1,0:T(8,128)S(1)}, u32[]{:S(2)}, u32[]{:S(2)}) collective-permute-start(f32[3,12,8,256]{3,2,1,0:T(8,128)S(1)} %get-tuple-element.30.left_ref), channel_id=1, source_target_pairs={{8,0},{16,8},{24,16},{0,24},{9,1},{17,9},{25,17},{1,25},{10,2},{18... | collective-permute-start | bytes 884744 | tf_op jit(solution)/shard_map/ppermute | solution.py:663
  9.6 2.2 %slice-start.2 = ((s8[9437184]{0:T(1024)(128)(4,1)}), s8[4194304]{0:T(1024)(128)(4,1)S(1)}, s32[]{:S(2)}) async-start(s8[9437184]{0:T(1024)(128)(4,1)} %bitcast), calls=%async_computation.2 | async-start | bytes 8388608
  10.6 9.3 %collective-permute-start.2 = (f32[3,1,32,128]{3,2,1,0:T(8,128)S(1)}, f32[3,1,32,128]{3,2,1,0:T(8,128)S(1)}, u32[]{:S(2)}, u32[]{:S(2)}) collective-permute-start(f32[3,1,32,128]{3,2,1,0:T(8,128)S(1)} %get-tuple-element.35), channel_id=1, source_target_pairs={{0,1},{1,0},{2,3},{3,2},{4,5},{5,4},{6,7},{7,6},{8,9},{9,8},{10,11... | collective-permute-start | bytes 147464 | tf_op jit(solution)/shard_map/ppermute | solution.py:665
  10.7 9.3 %collective-permute-start.3 = (f32[3,1,32,128]{3,2,1,0:T(8,128)S(1)}, f32[3,1,32,128]{3,2,1,0:T(8,128)S(1)}, u32[]{:S(2)}, u32[]{:S(2)}) collective-permute-start(f32[3,1,32,128]{3,2,1,0:T(8,128)S(1)} %get-tuple-element.36), channel_id=1, source_target_pairs={{1,2},{2,1},{3,4},{4,3},{5,6},{6,5},{9,10},{10,9},{11,12},{12,11},... | collective-permute-start | bytes 147464 | tf_op jit(solution)/shard_map/ppermute | solution.py:666
  23.9 1.3 %collective-permute-start.4 = (f32[200,128]{1,0:T(8,128)S(1)}, f32[200,128]{1,0:T(8,128)S(1)}, u32[]{:S(2)}, u32[]{:S(2)}) collective-permute-start(f32[200,128]{1,0:T(8,128)S(1)} %get-tuple-element.37.token.all_ref.load), channel_id=1, source_target_pairs={{0,1},{1,0},{2,3},{3,2},{4,5},{5,4},{6,7},{7,6},{8,9},{9,8},{10,11... | collective-permute-start | bytes 307208 | tf_op jit(solution)/shard_map/ppermute | solution.py:675
  25.3 5.0 %collective-permute-start.5 = (f32[200,128]{1,0:T(8,128)S(1)}, f32[200,128]{1,0:T(8,128)S(1)}, u32[]{:S(2)}, u32[]{:S(2)}) collective-permute-start(f32[200,128]{1,0:T(8,128)S(1)} %get-tuple-element.38.token.all_ref), channel_id=1, source_target_pairs={{0,2},{1,3},{2,0},{3,1},{4,6},{5,7},{6,4},{7,5},{8,10},{9,11},{10,... | collective-permute-start | bytes 307208 | tf_op jit(solution)/shard_map/ppermute | solution.py:675
  30.4 6.0 %collective-permute-start.6 = (f32[104,128]{1,0:T(8,128)S(1)}, f32[104,128]{1,0:T(8,128)S(1)}, u32[]{:S(2)}, u32[]{:S(2)}) collective-permute-start(f32[104,128]{1,0:T(8,128)S(1)} %get-tuple-element.45.token), channel_id=1, source_target_pairs={{0,4},{1,5},{2,6},{3,7},{4,0},{5,1},{6,2},{7,3},{8,12},{9,13},{10,... | collective-permute-start | bytes 159752 | tf_op jit(solution)/shard_map/ppermute | solution.py:675

commit v8 on v7

--- a/solution.py
+++ b/solution.py
@@ -16,6 +16,7 @@
 F32 = jnp.float32
 BF16 = jnp.bfloat16
 MIB = 1 << 20
+CUT = 16
 
 INV_GAP, FORWARD, BACKWARD, PSI, PHI, OWN, NEXT = range(7)
 
@@ -535,7 +536,7 @@
     n = adv_part.shape[1]
     if start:
         _, before_ref, adv_hbm, sum_ref, end_ref, adv_ref, sems = refs
-        end_ref[...] = before_ref[...] + sum_part[:, start - 1]
+        end_ref[...] = before_ref[...]
     else:
         adv_hbm, sum_ref, end_ref, adv_ref, sems = refs
         end_ref[...] = (GAMMA * co[FORWARD, pl.ds(0, 1), :]) * rim_ref[0]
@@ -551,7 +552,9 @@
             acc = end_ref[c]
             for k in range(block // group):
                 here = step * block + k * group
-                spread = spread_planes(extra_ref[c, start // group + step * (block // group) + k])
+                chunk = start // group + step * (block // group) + k
+                acc = jnp.where(chunk == n // (2 * group), acc + sum_part[c, n // 2 - 1], acc)
+                spread = spread_planes(extra_ref[c, chunk])
                 for y in range(group):
                     i = here + y
                     extra = spread[32 * y : 32 * y + 32]
@@ -574,18 +577,18 @@
         copy(step).start()
         return 0
 
-    lax.fori_loop(0, steps, part, 0)
+    lax.fori_loop(0, steps, part, 0, unroll=True)
 
     def finish(step, _):
         copy(step).wait()
         return 0
 
-    lax.fori_loop(0, steps, finish, 0)
+    lax.fori_loop(0, steps, finish, 0, unroll=True)
 
 
 def sweep_up(start, count, token, table, adv_part, sums, extra, rims, group, before=()):
     shape = adv_part.shape
-    block = max(d for d in range(group, 33, group) if count % d == 0)
+    block = max(d for d in range(group, 17, group) if count % d == 0)
     hbm = pl.BlockSpec(memory_space=pltpu.HBM)
     part = (3, count, 32, 128)
     return pl.pallas_call(
@@ -612,8 +615,10 @@
         return pltpu.make_async_copy(u_ref.at[:, here], u_hbm.at[:, here], sems.at[step])
 
     def part(sum_ref, first):
+        count = sum_ref.shape[1] // block
+
         def run(k, value):
-            step = steps // 2 - 1 - k
+            step = count - 1 - k
             for y in reversed(range(block)):
                 i = step * block + y
                 value = co[OWN, pl.ds(first + i, 1), :] * (sum_ref[:, i] + below) + co[NEXT, pl.ds(first + i, 1), :] * value
@@ -624,8 +629,9 @@
         return run
 
     value = above_ref[...].reshape(3, 32, 128)
-    value = lax.fori_loop(0, steps // 2, part(high_ref, n // 2), value)
-    lax.fori_loop(0, steps // 2, part(low_ref, 0), value)
+    cut = low_ref.shape[1]
+    value = lax.fori_loop(0, (n - cut) // block, part(high_ref, cut), value)
+    lax.fori_loop(0, cut // block, part(low_ref, 0), value)
 
     def finish(step, _):
         copy(step).wait()
@@ -635,7 +641,7 @@
 
 
 def sweep_down(bit, table, load, other, around, sums, block):
-    n = 2 * sums[0].shape[1]
+    n = sums[0].shape[1] + sums[1].shape[1]
     shape = (3, n, 32, 128)
     return pl.pallas_call(
         functools.partial(down_kernel, bit, n, block),
@@ -669,17 +675,17 @@
         from_left, from_right, left, right, sums, b_sum, wide, near, far, vel, table, group
     )
     bits = [1 << t for t in range(ny.bit_length() - 1)]
-    half = n // 2
+    cut = group * (CUT * (n // group) // 24)
     whole, around, token = load, [], load
     for bit in bits:
         other = lax.ppermute(whole, "gy", [(i, i ^ bit) for i in range(ny)])
         if bit != bits[-1]:
             whole, *around = join_runs(bit, 2 * bit == bits[-1], token, whole, other, around)
         if bit == bits[0]:
-            adv, low, end = sweep_up(0, half, whole, table, adv_part, sums, extra, rims, group)
+            adv, low, end = sweep_up(0, cut, whole, table, adv_part, sums, extra, rims, group)
             token = end
-    adv, high, _ = sweep_up(half, half, whole, table, adv_part, sums, extra, rims, group, (adv, end))
-    down_block = block if half % block == 0 else group
+    adv, high, _ = sweep_up(cut, n - cut, whole, table, adv_part, sums, extra, rims, group, (adv, end))
+    down_block = max(d for d in range(group, 17, group) if cut % d == 0 and n % d == 0)
     return sweep_down(bits[-1], table, load, other, around, (low, high), down_block), adv
 
 

time: 40.4 us -> 39.8 us (0.985)
  no operation moved by 1% of the time
where the time goes in v8:
time: 39.8 us; the launch traced here: 39.6 us
  Pallas kernels  24.6 us (62%)
  starting transfers between devices  9.22 us (23%)
  waiting for transfers between devices  4.69 us (12%)
  between operations  0.81 us (2%)
    pallas_call x1, Pallas kernels, main_part(): pl.pallas_call(functools.partial(main_kernel if both_units else main_plai...  8.15 us
    pallas_call x2, Pallas kernels, sweep_up(): pl.pallas_call(functools.partial(up_kernel, start, count, block, group),...  5.76 us
    pallas_call x1, Pallas kernels, pack(): pl.pallas_call(functools.partial(pack_kernel, group), in_specs=[pl.BlockS...  4.86 us
    ppermute x3, starting transfers between devices, shards(): other = lax.ppermute(whole, 'gy', [(i, i ^ bit) for i in range(ny)])  4.34 us
    pallas_call x1, Pallas kernels, sweep_down(): pl.pallas_call(functools.partial(down_kernel, bit, n, block), in_specs=[v...  3.92 us
    ppermute x1, waiting for transfers between devices, shards(): from_right = lax.ppermute(left, 'gx', [(j, i) for i, j in ring])  3.13 us
    ppermute x1, starting transfers between devices, shards(): from_left = lax.ppermute(right, 'gx', ring)  2.99 us
    ppermute x3, waiting for transfers between devices, shards(): other = lax.ppermute(whole, 'gy', [(i, i ^ bit) for i in range(ny)])  1.56 us
  transfers between devices with their start and end apart: 7, of which 3 were waited for; matrix products, arithmetic and copies ran while one was open for 0% of the time, Pallas kernels for 38%

profile of v8, /device:TPU:0, one launch (start us, length us, event | category | flops | bytes accessed | tf_op | source)
XLA Modules:
  0.0 39.6 jit_solution(11869489986806419813)
XLA Ops:
  0.6 0.0 copy-start
  0.6 0.0 copy-start.1
  0.7 0.0 copy-start.3
  0.7 0.0 copy-start.2
  0.7 0.0 slice-start
  0.7 0.0 slice-start.1
  0.7 4.9 %pack_edges.1 = (f32[3,192,32,128]{3,2,1,0:T(8,128)S(1)}, bf16[3,6144,256]{2,1,0:T(8,128)(2,1)S(1)}, f32[3,12,8,256]{3,2,1,0:T(8,128)S(1)}, f32[3,12,8,256]{3,2,1,0:T(8,128)S(1)}) custom-call(f32[3,192,32,128]{3,2,1,0:T(8,128)} %v_hbm.1), custom_call_target="tpu_custom_call" | custom-call | flops 2359296 | bytes 9437184 | tf_op jit(solution)/shard_map/pack_edges/pallas_call | solution.py:188
  5.6 3.0 %collective-permute-start = (f32[3,12,8,256]{3,2,1,0:T(8,128)S(1)}, f32[3,12,8,256]{3,2,1,0:T(8,128)S(1)}, u32[]{:S(2)}, u32[]{:S(2)}) collective-permute-start(f32[3,12,8,256]{3,2,1,0:T(8,128)S(1)} %get-tuple-element.29.right_ref), channel_id=1, source_target_pairs={{0,8},{8,16},{16,24},{24,0},{1,9},{9,17},{17,25},{25,1},{2,10},{10... | collective-permute-start | bytes 884744 | tf_op jit(solution)/shard_map/ppermute | solution.py:668
  8.6 1.0 %collective-permute-start.1 = (f32[3,12,8,256]{3,2,1,0:T(8,128)S(1)}, f32[3,12,8,256]{3,2,1,0:T(8,128)S(1)}, u32[]{:S(2)}, u32[]{:S(2)}) collective-permute-start(f32[3,12,8,256]{3,2,1,0:T(8,128)S(1)} %get-tuple-element.30.left_ref), channel_id=1, source_target_pairs={{8,0},{16,8},{24,16},{0,24},{9,1},{17,9},{25,17},{1,25},{10,2},{18... | collective-permute-start | bytes 884744 | tf_op jit(solution)/shard_map/ppermute | solution.py:669
  9.6 0.0 copy-done.3
  9.6 0.0 copy-done.2
  9.6 0.0 slice-start.2
  9.6 1.0 %coefficients.1 = (f32[7,192,128]{2,1,0:T(8,128)S(1)}, f32[2,12,8,256]{3,2,1,0:T(8,128)S(1)}, f32[3,1,32,128]{3,2,1,0:T(8,128)S(1)}, f32[3,1,32,128]{3,2,1,0:T(8,128)S(1)}) custom-call(f32[192]{0:T(256)S(1)} %copy-done.2, f32[192]{0:T(256)S(1)} %copy-done.3, f32[3,192,32,128]{3,2,1,0:T(8,128)S(1)} %get-tuple-element.27.vel_ref), custom_call_target="tpu_custom_call" | custom-call | flops 100000 | tf_op jit(solution)/shard_map/coefficients/pallas_call | solution.py:136
  10.6 0.1 collective-permute-start.2
  10.7 0.8 %collective-permute-start.3 = (f32[3,1,32,128]{3,2,1,0:T(8,128)S(1)}, f32[3,1,32,128]{3,2,1,0:T(8,128)S(1)}, u32[]{:S(2)}, u32[]{:S(2)}) collective-permute-start(f32[3,1,32,128]{3,2,1,0:T(8,128)S(1)} %get-tuple-element.36), channel_id=1, source_target_pairs={{1,2},{2,1},{3,4},{4,3},{5,6},{6,5},{9,10},{10,9},{11,12},{12,11},... | collective-permute-start | bytes 147464 | tf_op jit(solution)/shard_map/ppermute | solution.py:672
  11.5 0.0 copy-done
  11.5 0.0 copy-done.1
  11.5 0.0 slice-done
  11.5 0.0 slice-done.1
  11.5 0.2 slice-done.2
  11.8 8.1 %inner_part.1 = (f32[3,192,32,128]{3,2,1,0:T(8,128)S(1)}, f32[3,192,32,128]{3,2,1,0:T(8,128)S(1)}, f32[3,32,128]{2,1,0:T(8,128)S(1)}) custom-call(f32[7,192,128]{2,1,0:T(8,128)S(1)} %get-tuple-element.28.co, f32[3,192,32,128]{3,2,1,0:T(8,128)S(1)} %get-tuple-element.27.vel_ref, bf16[3,6144,256]{2,1,0:T(8,128)(2,1)S(1)} %get-tuple-element.31.pair_ref, ...), custom_call_target="tpu_custom_call" | custom-call | flops 58982400 | bytes 9437184 | tf_op jit(solution)/shard_map/inner_part/pallas_call | solution.py:333
  19.9 0.0 collective-permute-done.2.near_ref
  19.9 0.0 collective-permute-done.3.far_ref
  19.9 0.0 collective-permute-done.from_left
  20.0 3.1 %collective-permute-done.1.from_right = f32[3,12,8,256]{3,2,1,0:T(8,128)S(1)} collective-permute-done((f32[3,12,8,256]{3,2,1,0:T(8,128)S(1)}, f32[3,12,8,256]{3,2,1,0:T(8,128)S(1)}, u32[]{:S(2)}, u32[]{:S(2)}) %collective-permute-start.1) | collective-permute-done | bytes 294944 | tf_op jit(solution)/shard_map/ppermute | solution.py:669
  23.1 0.8 %edge_part.1 = (bf16[3,24,16,256]{3,2,1,0:T(8,128)(2,1)S(1)}, f32[2,3,32,128]{3,2,1,0:T(8,128)S(1)}, f32[200,128]{1,0:T(8,128)S(1)}) custom-call(f32[7,192,128]{2,1,0:T(8,128)S(1)} %get-tuple-element.28.co, f32[3,12,8,256]{3,2,1,0:T(8,128)S(1)} %collective-permute-done.from_left, f32[3,12,8,256]{3,2,1,0:T(8,128)S(1)} %collective-permute-done.1.from_right, ...), custom_call_target="tpu_custom_call" | custom-call | flops 2949120 | tf_op jit(solution)/shard_map/edge_part/pallas_call | solution.py:420
  23.9 0.0 collective-permute-start.4
  23.9 1.3 %collective-permute-done.4.other_ref = f32[200,128]{1,0:T(8,128)S(1)} collective-permute-done((f32[200,128]{1,0:T(8,128)S(1)}, f32[200,128]{1,0:T(8,128)S(1)}, u32[]{:S(2)}, u32[]{:S(2)}) %collective-permute-start.4) | collective-permute-done | bytes 102432 | tf_op jit(solution)/shard_map/ppermute | solution.py:681
  25.3 1.6 %collective-permute-start.5 = (f32[200,128]{1,0:T(8,128)S(1)}, f32[200,128]{1,0:T(8,128)S(1)}, u32[]{:S(2)}, u32[]{:S(2)}) collective-permute-start(f32[200,128]{1,0:T(8,128)S(1)} %get-tuple-element.38.token.all_ref), channel_id=1, source_target_pairs={{0,2},{1,3},{2,0},{3,1},{4,6},{5,7},{6,4},{7,5},{8,10},{9,11},{10,... | collective-permute-start | bytes 307208 | tf_op jit(solution)/shard_map/ppermute | solution.py:681
  26.9 3.1 %sweep_up.2 = (f32[3,192,32,128]{3,2,1,0:T(8,128)}, f32[3,128,32,128]{3,2,1,0:T(8,128)S(1)}, f32[3,32,128]{2,1,0:T(8,128)S(1)}) custom-call(f32[200,128]{1,0:T(8,128)S(1)} %get-tuple-element.38.token.all_ref, f32[7,192,128]{2,1,0:T(8,128)S(1)} %get-tuple-element.28.co, f32[3,192,32,128]{3,2,1,0:T(8,128)S(1)} %get-tuple-element.39.adv_part, ...), custom_call_target="tpu_custom_call" | custom-call | flops 9437184 | bytes 4718592 | tf_op jit(solution)/shard_map/sweep_up/pallas_call | solution.py:594
  30.0 0.3 collective-permute-done.5.other_ref
  30.3 0.1 join_runs.3
  30.4 2.7 %collective-permute-start.6 = (f32[104,128]{1,0:T(8,128)S(1)}, f32[104,128]{1,0:T(8,128)S(1)}, u32[]{:S(2)}, u32[]{:S(2)}) collective-permute-start(f32[104,128]{1,0:T(8,128)S(1)} %get-tuple-element.45.token), channel_id=1, source_target_pairs={{0,4},{1,5},{2,6},{3,7},{4,0},{5,1},{6,2},{7,3},{8,12},{9,13},{10,... | collective-permute-start | bytes 159752 | tf_op jit(solution)/shard_map/ppermute | solution.py:681
  33.0 2.7 %sweep_up.3 = (f32[3,192,32,128]{3,2,1,0:T(8,128)}, f32[3,64,32,128]{3,2,1,0:T(8,128)S(1)}, f32[3,32,128]{2,1,0:T(8,128)}) custom-call(f32[104,128]{1,0:T(8,128)S(1)} %get-tuple-element.45.token, f32[7,192,128]{2,1,0:T(8,128)S(1)} %get-tuple-element.28.co, f32[3,192,32,128]{3,2,1,0:T(8,128)S(1)} %get-tuple-element.39.adv_part, ...), custom_call_target="tpu_custom_call", output_to_operand_aliasing={{0}: (6, {})} | custom-call | flops 9437184 | bytes 4718592 | tf_op jit(solution)/shard_map/sweep_up/pallas_call | solution.py:594
  35.7 0.0 collective-permute-done.6.other
  35.7 3.9 %sweep_down.1 = f32[3,192,32,128]{3,2,1,0:T(8,128)} custom-call(f32[7,192,128]{2,1,0:T(8,128)S(1)} %get-tuple-element.28.co, f32[200,128]{1,0:T(8,128)S(1)} %get-tuple-element.37.token.all_ref.load, f32[104,128]{1,0:T(8,128)S(1)} %collective-permute-done.6.other, f32[200,128]{1,0:T(8,128)S(1)} %get-tuple-element.46.lower, ...), custom_call_target="tpu_custom_call" | custom-call | flops 18874368 | bytes 12582912 | tf_op jit(solution)/shard_map/sweep_down/pallas_call | solution.py:646
  (2 shorter events, 0.1 us)
Async XLA Ops:
  0.6 10.9 %copy-start = (bf16[256,256]{1,0:T(8,128)(2,1)S(1)}, bf16[256,256]{1,0:T(8,128)(2,1)}, u32[]{:S(2)}) copy-start(bf16[256,256]{1,0:T(8,128)(2,1)} %constant.5.clone.dx_ref) | copy-start | bytes 393220
  0.6 10.9 %copy-start.1 = (bf16[128,256]{1,0:T(8,128)(2,1)S(1)}, bf16[128,256]{1,0:T(8,128)(2,1)}, u32[]{:S(2)}) copy-start(bf16[128,256]{1,0:T(8,128)(2,1)} %constant.4.clone.dz_ref) | copy-start | bytes 196612
  0.7 8.9 %copy-start.3 = (f32[192]{0:T(256)S(1)}, f32[192]{0:T(256)}, u32[]{:S(2)}) copy-start(f32[192]{0:T(256)} %upper_ref.1) | copy-start | bytes 2308
  0.7 8.9 %copy-start.2 = (f32[192]{0:T(256)S(1)}, f32[192]{0:T(256)}, u32[]{:S(2)}) copy-start(f32[192]{0:T(256)} %lower_ref.1) | copy-start | bytes 2308
  0.7 10.8 %slice-start = ((s8[9437184]{0:T(1024)(128)(4,1)}), s8[1048576]{0:T(1024)(128)(4,1)S(1)}, s32[]{:S(2)}) async-start(s8[9437184]{0:T(1024)(128)(4,1)} %bitcast), calls=%async_computation | async-start | bytes 2097152
  0.7 10.8 %slice-start.1 = ((s8[9437184]{0:T(1024)(128)(4,1)}), s8[4194304]{0:T(1024)(128)(4,1)S(1)}, s32[]{:S(2)}) async-start(s8[9437184]{0:T(1024)(128)(4,1)} %bitcast), calls=%async_computation.1 | async-start | bytes 8388608
  5.6 14.4 %collective-permute-start = (f32[3,12,8,256]{3,2,1,0:T(8,128)S(1)}, f32[3,12,8,256]{3,2,1,0:T(8,128)S(1)}, u32[]{:S(2)}, u32[]{:S(2)}) collective-permute-start(f32[3,12,8,256]{3,2,1,0:T(8,128)S(1)} %get-tuple-element.29.right_ref), channel_id=1, source_target_pairs={{0,8},{8,16},{16,24},{24,0},{1,9},{9,17},{17,25},{25,1},{2,10},{10... | collective-permute-start | bytes 884744 | tf_op jit(solution)/shard_map/ppermute | solution.py:668
  8.6 14.5 %collective-permute-start.1 = (f32[3,12,8,256]{3,2,1,0:T(8,128)S(1)}, f32[3,12,8,256]{3,2,1,0:T(8,128)S(1)}, u32[]{:S(2)}, u32[]{:S(2)}) collective-permute-start(f32[3,12,8,256]{3,2,1,0:T(8,128)S(1)} %get-tuple-element.30.left_ref), channel_id=1, source_target_pairs={{8,0},{16,8},{24,16},{0,24},{9,1},{17,9},{25,17},{1,25},{10,2},{18... | collective-permute-start | bytes 884744 | tf_op jit(solution)/shard_map/ppermute | solution.py:669
  9.6 2.2 %slice-start.2 = ((s8[9437184]{0:T(1024)(128)(4,1)}), s8[4194304]{0:T(1024)(128)(4,1)S(1)}, s32[]{:S(2)}) async-start(s8[9437184]{0:T(1024)(128)(4,1)} %bitcast), calls=%async_computation.2 | async-start | bytes 8388608
  10.6 9.3 %collective-permute-start.2 = (f32[3,1,32,128]{3,2,1,0:T(8,128)S(1)}, f32[3,1,32,128]{3,2,1,0:T(8,128)S(1)}, u32[]{:S(2)}, u32[]{:S(2)}) collective-permute-start(f32[3,1,32,128]{3,2,1,0:T(8,128)S(1)} %get-tuple-element.35), channel_id=1, source_target_pairs={{0,1},{1,0},{2,3},{3,2},{4,5},{5,4},{6,7},{7,6},{8,9},{9,8},{10,11... | collective-permute-start | bytes 147464 | tf_op jit(solution)/shard_map/ppermute | solution.py:671
  10.7 9.3 %collective-permute-start.3 = (f32[3,1,32,128]{3,2,1,0:T(8,128)S(1)}, f32[3,1,32,128]{3,2,1,0:T(8,128)S(1)}, u32[]{:S(2)}, u32[]{:S(2)}) collective-permute-start(f32[3,1,32,128]{3,2,1,0:T(8,128)S(1)} %get-tuple-element.36), channel_id=1, source_target_pairs={{1,2},{2,1},{3,4},{4,3},{5,6},{6,5},{9,10},{10,9},{11,12},{12,11},... | collective-permute-start | bytes 147464 | tf_op jit(solution)/shard_map/ppermute | solution.py:672
  23.9 1.3 %collective-permute-start.4 = (f32[200,128]{1,0:T(8,128)S(1)}, f32[200,128]{1,0:T(8,128)S(1)}, u32[]{:S(2)}, u32[]{:S(2)}) collective-permute-start(f32[200,128]{1,0:T(8,128)S(1)} %get-tuple-element.37.token.all_ref.load), channel_id=1, source_target_pairs={{0,1},{1,0},{2,3},{3,2},{4,5},{5,4},{6,7},{7,6},{8,9},{9,8},{10,11... | collective-permute-start | bytes 307208 | tf_op jit(solution)/shard_map/ppermute | solution.py:681
  25.3 5.0 %collective-permute-start.5 = (f32[200,128]{1,0:T(8,128)S(1)}, f32[200,128]{1,0:T(8,128)S(1)}, u32[]{:S(2)}, u32[]{:S(2)}) collective-permute-start(f32[200,128]{1,0:T(8,128)S(1)} %get-tuple-element.38.token.all_ref), channel_id=1, source_target_pairs={{0,2},{1,3},{2,0},{3,1},{4,6},{5,7},{6,4},{7,5},{8,10},{9,11},{10,... | collective-permute-start | bytes 307208 | tf_op jit(solution)/shard_map/ppermute | solution.py:681
  30.4 5.3 %collective-permute-start.6 = (f32[104,128]{1,0:T(8,128)S(1)}, f32[104,128]{1,0:T(8,128)S(1)}, u32[]{:S(2)}, u32[]{:S(2)}) collective-permute-start(f32[104,128]{1,0:T(8,128)S(1)} %get-tuple-element.45.token), channel_id=1, source_target_pairs={{0,4},{1,5},{2,6},{3,7},{4,0},{5,1},{6,2},{7,3},{8,12},{9,13},{10,... | collective-permute-start | bytes 159752 | tf_op jit(solution)/shard_map/ppermute | solution.py:681

commit v9 on v8

--- a/solution.py
+++ b/solution.py
@@ -354,7 +354,7 @@
 
 
 def edge_kernel(pairs, group, co, from_left, from_right, left_ref, right_ref, sum_ref, b_ref, wide_ref,
-                near_ref, far_ref, vel_ref, extra_ref, rim_ref, load_ref):
+                near_ref, far_ref, vel_ref, adv_l, adv_r, rim_ref, load_ref):
     even = (lax.axis_index("gy") & 1) == 0
     n = 2 * pairs * group
     rows = group * 32
@@ -398,10 +398,7 @@
             adv.append(-own[0] * slope)
             force = GAMMA * adv[side]
             totals.append([total(wide_ref[t] * force) for t in range(2)])
-        for p in range(pairs):
-            l, r = adv[0][p], adv[1][p]
-            for h, value in ((0, jnp.where(low, l, swap(r))), (1, jnp.where(low, swap(l), r))):
-                extra_ref[c, 2 * p + h] = jnp.concatenate(split(value), axis=0)
+        adv_l[c], adv_r[c] = adv
         for t, (main, weight, row, i) in enumerate(
             ((b_ref[c], BACKWARD, PHI, 0), (sum_ref[c, n // 2 - 1] + sum_ref[c, n - 1], FORWARD, PSI, n - 1))
         ):
@@ -420,13 +417,37 @@
     return pl.pallas_call(
         functools.partial(edge_kernel, pairs, group),
         in_specs=[vmem()] + [vmem()] * 10,
-        out_specs=[vmem()] * 3,
-        out_shape=[pltpu.VMEM((3, 2 * pairs, 16, group * 32), BF16), held((2, 3, 32, 128)),
+        out_specs=[vmem()] * 4,
+        out_shape=[held(left.shape), held(left.shape), held((2, 3, 32, 128)),
                    jax.ShapeDtypeStruct((200, 128), F32)],
         compiler_params=limit(8),
         cost_estimate=cost(40 * left.size),
         name="edge_part",
     )(table, from_left, from_right, left, right, sums, b_sum, wide, near, far, vel)
+
+
+def extra_kernel(pairs, adv_l, adv_r, extra_ref):
+    low = sublanes(adv_l.shape[2:]) < 4
+    for c in range(3):
+        for p in range(pairs):
+            l, r = adv_l[c, p], adv_r[c, p]
+            first = jnp.where(low, l, pltpu.roll(r, 4, 0))
+            second = jnp.where(low, pltpu.roll(l, 4, 0), r)
+            for h, value in ((0, first), (1, second)):
+                extra_ref[c, 2 * p + h] = jnp.concatenate(split(value), axis=0)
+
+
+def extra_part(adv_l, adv_r):
+    _, pairs, _, rows = adv_l.shape
+    return pl.pallas_call(
+        functools.partial(extra_kernel, pairs),
+        in_specs=[vmem()] * 2,
+        out_specs=vmem(),
+        out_shape=pltpu.VMEM((3, 2 * pairs, 16, rows), BF16),
+        compiler_params=limit(4),
+        cost_estimate=cost(10 * adv_l.size),
+        name="extra_part",
+    )(adv_l, adv_r)
 
 
 def read(ref):
@@ -671,12 +692,13 @@
     near = lax.ppermute(near, "gy", pairs)
     far = lax.ppermute(far, "gy", others)
     adv_part, sums, b_sum = main_part(vel, pair, old_advection, table, group, block)
-    extra, rims, load = edge_part(
+    *adv_edges, rims, load = edge_part(
         from_left, from_right, left, right, sums, b_sum, wide, near, far, vel, table, group
     )
     bits = [1 << t for t in range(ny.bit_length() - 1)]
     cut = group * (CUT * (n // group) // 24)
-    whole, around, token = load, [], load
+    extra = extra_part(*adv_edges)
+    whole, around, token = load, [], extra
     for bit in bits:
         other = lax.ppermute(whole, "gy", [(i, i ^ bit) for i in range(ny)])
         if bit != bits[-1]:

time: 39.8 us -> 39.6 us (level)
  no operation moved by 1% of the time
where the time goes in v9:
time: 39.6 us; the launch traced here: 39.4 us
  Pallas kernels  24.6 us (62%)
  starting transfers between devices  9.22 us (23%)
  waiting for transfers between devices  4.51 us (11%)
  between operations  0.81 us (2%)
    pallas_call x1, Pallas kernels, main_part(): pl.pallas_call(functools.partial(main_kernel if both_units else main_plai...  8.15 us
    pallas_call x2, Pallas kernels, sweep_up(): pl.pallas_call(functools.partial(up_kernel, start, count, block, group),...  5.76 us
    pallas_call x1, Pallas kernels, pack(): pl.pallas_call(functools.partial(pack_kernel, group), in_specs=[pl.BlockS...  4.86 us
    ppermute x3, starting transfers between devices, shards(): other = lax.ppermute(whole, 'gy', [(i, i ^ bit) for i in range(ny)])  4.34 us
    pallas_call x1, Pallas kernels, sweep_down(): pl.pallas_call(functools.partial(down_kernel, bit, n, block), in_specs=[v...  3.92 us
    ppermute x1, waiting for transfers between devices, shards(): from_right = lax.ppermute(left, 'gx', [(j, i) for i, j in ring])  3.13 us
    ppermute x1, starting transfers between devices, shards(): from_left = lax.ppermute(right, 'gx', ring)  2.99 us
    ppermute x3, waiting for transfers between devices, shards(): other = lax.ppermute(whole, 'gy', [(i, i ^ bit) for i in range(ny)])  1.37 us
  transfers between devices with their start and end apart: 7, of which 3 were waited for; matrix products, arithmetic and copies ran while one was open for 0% of the time, Pallas kernels for 38%

profile of v9, /device:TPU:0, one launch (start us, length us, event | category | flops | bytes accessed | tf_op | source)
XLA Modules:
  0.0 39.4 jit_solution(16992442877737687228)
XLA Ops:
  0.6 0.0 copy-start
  0.6 0.0 copy-start.1
  0.7 0.0 copy-start.3
  0.7 0.0 copy-start.2
  0.7 0.0 slice-start
  0.7 0.0 slice-start.1
  0.7 4.9 %pack_edges.1 = (f32[3,192,32,128]{3,2,1,0:T(8,128)S(1)}, bf16[3,6144,256]{2,1,0:T(8,128)(2,1)S(1)}, f32[3,12,8,256]{3,2,1,0:T(8,128)S(1)}, f32[3,12,8,256]{3,2,1,0:T(8,128)S(1)}) custom-call(f32[3,192,32,128]{3,2,1,0:T(8,128)} %v_hbm.1), custom_call_target="tpu_custom_call" | custom-call | flops 2359296 | bytes 9437184 | tf_op jit(solution)/shard_map/pack_edges/pallas_call | solution.py:188
  5.6 3.0 %collective-permute-start = (f32[3,12,8,256]{3,2,1,0:T(8,128)S(1)}, f32[3,12,8,256]{3,2,1,0:T(8,128)S(1)}, u32[]{:S(2)}, u32[]{:S(2)}) collective-permute-start(f32[3,12,8,256]{3,2,1,0:T(8,128)S(1)} %get-tuple-element.30.right_ref), channel_id=1, source_target_pairs={{0,8},{8,16},{16,24},{24,0},{1,9},{9,17},{17,25},{25,1},{2,10},{10... | collective-permute-start | bytes 884744 | tf_op jit(solution)/shard_map/ppermute | solution.py:689
  8.6 1.0 %collective-permute-start.1 = (f32[3,12,8,256]{3,2,1,0:T(8,128)S(1)}, f32[3,12,8,256]{3,2,1,0:T(8,128)S(1)}, u32[]{:S(2)}, u32[]{:S(2)}) collective-permute-start(f32[3,12,8,256]{3,2,1,0:T(8,128)S(1)} %get-tuple-element.31.left_ref), channel_id=1, source_target_pairs={{8,0},{16,8},{24,16},{0,24},{9,1},{17,9},{25,17},{1,25},{10,2},{18... | collective-permute-start | bytes 884744 | tf_op jit(solution)/shard_map/ppermute | solution.py:690
  9.6 0.0 copy-done.3
  9.6 0.0 copy-done.2
  9.6 0.0 slice-start.2
  9.6 1.0 %coefficients.1 = (f32[7,192,128]{2,1,0:T(8,128)S(1)}, f32[2,12,8,256]{3,2,1,0:T(8,128)S(1)}, f32[3,1,32,128]{3,2,1,0:T(8,128)S(1)}, f32[3,1,32,128]{3,2,1,0:T(8,128)S(1)}) custom-call(f32[192]{0:T(256)S(1)} %copy-done.2, f32[192]{0:T(256)S(1)} %copy-done.3, f32[3,192,32,128]{3,2,1,0:T(8,128)S(1)} %get-tuple-element.28.vel_ref), custom_call_target="tpu_custom_call" | custom-call | flops 100000 | tf_op jit(solution)/shard_map/coefficients/pallas_call | solution.py:136
  10.6 0.1 collective-permute-start.2
  10.7 0.8 %collective-permute-start.3 = (f32[3,1,32,128]{3,2,1,0:T(8,128)S(1)}, f32[3,1,32,128]{3,2,1,0:T(8,128)S(1)}, u32[]{:S(2)}, u32[]{:S(2)}) collective-permute-start(f32[3,1,32,128]{3,2,1,0:T(8,128)S(1)} %get-tuple-element.37), channel_id=1, source_target_pairs={{1,2},{2,1},{3,4},{4,3},{5,6},{6,5},{9,10},{10,9},{11,12},{12,11},... | collective-permute-start | bytes 147464 | tf_op jit(solution)/shard_map/ppermute | solution.py:693
  11.5 0.0 copy-done
  11.5 0.0 copy-done.1
  11.5 0.0 slice-done
  11.5 0.0 slice-done.1
  11.5 0.2 slice-done.2
  11.8 8.1 %inner_part.1 = (f32[3,192,32,128]{3,2,1,0:T(8,128)S(1)}, f32[3,192,32,128]{3,2,1,0:T(8,128)S(1)}, f32[3,32,128]{2,1,0:T(8,128)S(1)}) custom-call(f32[7,192,128]{2,1,0:T(8,128)S(1)} %get-tuple-element.29.co, f32[3,192,32,128]{3,2,1,0:T(8,128)S(1)} %get-tuple-element.28.vel_ref, bf16[3,6144,256]{2,1,0:T(8,128)(2,1)S(1)} %get-tuple-element.32.pair_ref, ...), custom_call_target="tpu_custom_call" | custom-call | flops 58982400 | bytes 9437184 | tf_op jit(solution)/shard_map/inner_part/pallas_call | solution.py:333
  19.9 0.0 collective-permute-done.2.near_ref
  19.9 0.0 collective-permute-done.3.far_ref
  19.9 0.0 collective-permute-done.from_left
  20.0 3.1 %collective-permute-done.1.from_right = f32[3,12,8,256]{3,2,1,0:T(8,128)S(1)} collective-permute-done((f32[3,12,8,256]{3,2,1,0:T(8,128)S(1)}, f32[3,12,8,256]{3,2,1,0:T(8,128)S(1)}, u32[]{:S(2)}, u32[]{:S(2)}) %collective-permute-start.1) | collective-permute-done | bytes 294944 | tf_op jit(solution)/shard_map/ppermute | solution.py:690
  23.1 0.6 %edge_part.1 = (f32[3,12,8,256]{3,2,1,0:T(8,128)S(1)}, f32[3,12,8,256]{3,2,1,0:T(8,128)S(1)}, f32[2,3,32,128]{3,2,1,0:T(8,128)S(1)}, f32[200,128]{1,0:T(8,128)S(1)}) custom-call(f32[7,192,128]{2,1,0:T(8,128)S(1)} %get-tuple-element.29.co, f32[3,12,8,256]{3,2,1,0:T(8,128)S(1)} %collective-permute-done.from_left, ...), custom_call_target="tpu_custom_call" | custom-call | flops 2949120 | tf_op jit(solution)/shard_map/edge_part/pallas_call | solution.py:417
  23.7 0.0 collective-permute-start.4
  23.8 0.2 extra_part.1.token.extra_ref
  23.9 1.1 %collective-permute-done.4.other_ref = f32[200,128]{1,0:T(8,128)S(1)} collective-permute-done((f32[200,128]{1,0:T(8,128)S(1)}, f32[200,128]{1,0:T(8,128)S(1)}, u32[]{:S(2)}, u32[]{:S(2)}) %collective-permute-start.4) | collective-permute-done | bytes 102432 | tf_op jit(solution)/shard_map/ppermute | solution.py:703
  25.1 1.6 %collective-permute-start.5 = (f32[200,128]{1,0:T(8,128)S(1)}, f32[200,128]{1,0:T(8,128)S(1)}, u32[]{:S(2)}, u32[]{:S(2)}) collective-permute-start(f32[200,128]{1,0:T(8,128)S(1)} %get-tuple-element.41.token.all_ref), channel_id=1, source_target_pairs={{0,2},{1,3},{2,0},{3,1},{4,6},{5,7},{6,4},{7,5},{8,10},{9,11},{10,... | collective-permute-start | bytes 307208 | tf_op jit(solution)/shard_map/ppermute | solution.py:703
  26.7 3.1 %sweep_up.2 = (f32[3,192,32,128]{3,2,1,0:T(8,128)}, f32[3,128,32,128]{3,2,1,0:T(8,128)S(1)}, f32[3,32,128]{2,1,0:T(8,128)S(1)}) custom-call(f32[200,128]{1,0:T(8,128)S(1)} %get-tuple-element.41.token.all_ref, f32[7,192,128]{2,1,0:T(8,128)S(1)} %get-tuple-element.29.co, f32[3,192,32,128]{3,2,1,0:T(8,128)S(1)} %get-tuple-element.42.adv_part, ...), custom_call_target="tpu_custom_call" | custom-call | flops 9437184 | bytes 4718592 | tf_op jit(solution)/shard_map/sweep_up/pallas_call | solution.py:615
  29.8 0.3 collective-permute-done.5.other_ref
  30.1 0.1 join_runs.3
  30.2 2.7 %collective-permute-start.6 = (f32[104,128]{1,0:T(8,128)S(1)}, f32[104,128]{1,0:T(8,128)S(1)}, u32[]{:S(2)}, u32[]{:S(2)}) collective-permute-start(f32[104,128]{1,0:T(8,128)S(1)} %get-tuple-element.47.token), channel_id=1, source_target_pairs={{0,4},{1,5},{2,6},{3,7},{4,0},{5,1},{6,2},{7,3},{8,12},{9,13},{10,... | collective-permute-start | bytes 159752 | tf_op jit(solution)/shard_map/ppermute | solution.py:703
  32.8 2.7 %sweep_up.3 = (f32[3,192,32,128]{3,2,1,0:T(8,128)}, f32[3,64,32,128]{3,2,1,0:T(8,128)S(1)}, f32[3,32,128]{2,1,0:T(8,128)}) custom-call(f32[104,128]{1,0:T(8,128)S(1)} %get-tuple-element.47.token, f32[7,192,128]{2,1,0:T(8,128)S(1)} %get-tuple-element.29.co, f32[3,192,32,128]{3,2,1,0:T(8,128)S(1)} %get-tuple-element.42.adv_part, ...), custom_call_target="tpu_custom_call", output_to_operand_aliasing={{0}: (6, {})} | custom-call | flops 9437184 | bytes 4718592 | tf_op jit(solution)/shard_map/sweep_up/pallas_call | solution.py:615
  35.5 0.0 collective-permute-done.6.other
  35.5 3.9 %sweep_down.1 = f32[3,192,32,128]{3,2,1,0:T(8,128)} custom-call(f32[7,192,128]{2,1,0:T(8,128)S(1)} %get-tuple-element.29.co, f32[200,128]{1,0:T(8,128)S(1)} %get-tuple-element.38.all_ref.load, f32[104,128]{1,0:T(8,128)S(1)} %collective-permute-done.6.other, f32[200,128]{1,0:T(8,128)S(1)} %get-tuple-element.48.lower, f32[200,128]{1,0:T(8,128)S(1)} %get-tuple-element.49.upper, ...), custom_call_target="tpu_custom_call" | custom-call | flops 18874368 | bytes 12582912 | tf_op jit(solution)/shard_map/sweep_down/pallas_call | solution.py:667
  (2 shorter events, 0.1 us)
Async XLA Ops:
  0.6 10.9 %copy-start = (bf16[256,256]{1,0:T(8,128)(2,1)S(1)}, bf16[256,256]{1,0:T(8,128)(2,1)}, u32[]{:S(2)}) copy-start(bf16[256,256]{1,0:T(8,128)(2,1)} %constant.5.clone.dx_ref) | copy-start | bytes 393220
  0.6 10.9 %copy-start.1 = (bf16[128,256]{1,0:T(8,128)(2,1)S(1)}, bf16[128,256]{1,0:T(8,128)(2,1)}, u32[]{:S(2)}) copy-start(bf16[128,256]{1,0:T(8,128)(2,1)} %constant.4.clone.dz_ref) | copy-start | bytes 196612
  0.7 8.9 %copy-start.3 = (f32[192]{0:T(256)S(1)}, f32[192]{0:T(256)}, u32[]{:S(2)}) copy-start(f32[192]{0:T(256)} %upper_ref.1) | copy-start | bytes 2308
  0.7 8.9 %copy-start.2 = (f32[192]{0:T(256)S(1)}, f32[192]{0:T(256)}, u32[]{:S(2)}) copy-start(f32[192]{0:T(256)} %lower_ref.1) | copy-start | bytes 2308
  0.7 10.8 %slice-start = ((s8[9437184]{0:T(1024)(128)(4,1)}), s8[1048576]{0:T(1024)(128)(4,1)S(1)}, s32[]{:S(2)}) async-start(s8[9437184]{0:T(1024)(128)(4,1)} %bitcast), calls=%async_computation | async-start | bytes 2097152
  0.7 10.8 %slice-start.1 = ((s8[9437184]{0:T(1024)(128)(4,1)}), s8[4194304]{0:T(1024)(128)(4,1)S(1)}, s32[]{:S(2)}) async-start(s8[9437184]{0:T(1024)(128)(4,1)} %bitcast), calls=%async_computation.1 | async-start | bytes 8388608
  5.6 14.4 %collective-permute-start = (f32[3,12,8,256]{3,2,1,0:T(8,128)S(1)}, f32[3,12,8,256]{3,2,1,0:T(8,128)S(1)}, u32[]{:S(2)}, u32[]{:S(2)}) collective-permute-start(f32[3,12,8,256]{3,2,1,0:T(8,128)S(1)} %get-tuple-element.30.right_ref), channel_id=1, source_target_pairs={{0,8},{8,16},{16,24},{24,0},{1,9},{9,17},{17,25},{25,1},{2,10},{10... | collective-permute-start | bytes 884744 | tf_op jit(solution)/shard_map/ppermute | solution.py:689
  8.6 14.5 %collective-permute-start.1 = (f32[3,12,8,256]{3,2,1,0:T(8,128)S(1)}, f32[3,12,8,256]{3,2,1,0:T(8,128)S(1)}, u32[]{:S(2)}, u32[]{:S(2)}) collective-permute-start(f32[3,12,8,256]{3,2,1,0:T(8,128)S(1)} %get-tuple-element.31.left_ref), channel_id=1, source_target_pairs={{8,0},{16,8},{24,16},{0,24},{9,1},{17,9},{25,17},{1,25},{10,2},{18... | collective-permute-start | bytes 884744 | tf_op jit(solution)/shard_map/ppermute | solution.py:690
  9.6 2.2 %slice-start.2 = ((s8[9437184]{0:T(1024)(128)(4,1)}), s8[4194304]{0:T(1024)(128)(4,1)S(1)}, s32[]{:S(2)}) async-start(s8[9437184]{0:T(1024)(128)(4,1)} %bitcast), calls=%async_computation.2 | async-start | bytes 8388608
  10.6 9.3 %collective-permute-start.2 = (f32[3,1,32,128]{3,2,1,0:T(8,128)S(1)}, f32[3,1,32,128]{3,2,1,0:T(8,128)S(1)}, u32[]{:S(2)}, u32[]{:S(2)}) collective-permute-start(f32[3,1,32,128]{3,2,1,0:T(8,128)S(1)} %get-tuple-element.36), channel_id=1, source_target_pairs={{0,1},{1,0},{2,3},{3,2},{4,5},{5,4},{6,7},{7,6},{8,9},{9,8},{10,11... | collective-permute-start | bytes 147464 | tf_op jit(solution)/shard_map/ppermute | solution.py:692
  10.7 9.3 %collective-permute-start.3 = (f32[3,1,32,128]{3,2,1,0:T(8,128)S(1)}, f32[3,1,32,128]{3,2,1,0:T(8,128)S(1)}, u32[]{:S(2)}, u32[]{:S(2)}) collective-permute-start(f32[3,1,32,128]{3,2,1,0:T(8,128)S(1)} %get-tuple-element.37), channel_id=1, source_target_pairs={{1,2},{2,1},{3,4},{4,3},{5,6},{6,5},{9,10},{10,9},{11,12},{12,11},... | collective-permute-start | bytes 147464 | tf_op jit(solution)/shard_map/ppermute | solution.py:693
  23.7 1.3 %collective-permute-start.4 = (f32[200,128]{1,0:T(8,128)S(1)}, f32[200,128]{1,0:T(8,128)S(1)}, u32[]{:S(2)}, u32[]{:S(2)}) collective-permute-start(f32[200,128]{1,0:T(8,128)S(1)} %get-tuple-element.38.all_ref.load), channel_id=1, source_target_pairs={{0,1},{1,0},{2,3},{3,2},{4,5},{5,4},{6,7},{7,6},{8,9},{9,8},{10,11... | collective-permute-start | bytes 307208 | tf_op jit(solution)/shard_map/ppermute | solution.py:703
  25.1 5.0 %collective-permute-start.5 = (f32[200,128]{1,0:T(8,128)S(1)}, f32[200,128]{1,0:T(8,128)S(1)}, u32[]{:S(2)}, u32[]{:S(2)}) collective-permute-start(f32[200,128]{1,0:T(8,128)S(1)} %get-tuple-element.41.token.all_ref), channel_id=1, source_target_pairs={{0,2},{1,3},{2,0},{3,1},{4,6},{5,7},{6,4},{7,5},{8,10},{9,11},{10,... | collective-permute-start | bytes 307208 | tf_op jit(solution)/shard_map/ppermute | solution.py:703
  30.2 5.3 %collective-permute-start.6 = (f32[104,128]{1,0:T(8,128)S(1)}, f32[104,128]{1,0:T(8,128)S(1)}, u32[]{:S(2)}, u32[]{:S(2)}) collective-permute-start(f32[104,128]{1,0:T(8,128)S(1)} %get-tuple-element.47.token), channel_id=1, source_target_pairs={{0,4},{1,5},{2,6},{3,7},{4,0},{5,1},{6,2},{7,3},{8,12},{9,13},{10,... | collective-permute-start | bytes 159752 | tf_op jit(solution)/shard_map/ppermute | solution.py:703

commit v10 on v9

--- a/solution.py
+++ b/solution.py
@@ -118,7 +118,7 @@
             == lax.broadcasted_iota(jnp.int32, (width, rows), 1) // 32)
     fold = jnp.where(fold, 1.0, 0.0).astype(BF16)
     for t, value in enumerate((forward, backward)):
-        value = jnp.where(live, value, 0.0)
+        value = jnp.where(live, value * -GAMMA, 0.0)
         hi, lo = split(jnp.where(mine, jnp.broadcast_to(value[0:1], mine.shape), 0.0))
         spread = jnp.dot(hi, fold, preferred_element_type=F32) + jnp.dot(lo, fold, preferred_element_type=F32)
         wide_ref[t] = spread.reshape(pairs, 8, rows)
@@ -315,7 +315,8 @@
                 issue(p + 1, c)
             return 0
 
-        lax.fori_loop(0, pairs - 1, part, 0)
+        lax.fori_loop(0, pairs - 2, part, 0, unroll=2)
+        part(pairs - 2, 0)
         scale(pairs - 1)
         for c in range(3):
             points(pairs - 1, c)
@@ -385,7 +386,7 @@
         adv, totals = [], []
         for side, halo, own in ((0, from_left, left_ref), (1, from_right, right_ref)):
             h = halo[c]
-            slope = jnp.zeros(shape, F32)
+            slope = None
             for d in range(4):
                 w = WEIGHTS[3 - d] * UNIT
                 if side == 0:
@@ -394,10 +395,9 @@
                 else:
                     weight = jnp.where(quarter >= d, w, 0.0)
                     turned = pltpu.roll(h, d, 1) if d else h
-                slope = slope + weight * turned
-            adv.append(-own[0] * slope)
-            force = GAMMA * adv[side]
-            totals.append([total(wide_ref[t] * force) for t in range(2)])
+                slope = weight * turned if slope is None else slope + weight * turned
+            adv.append(own[0] * slope)
+            totals.append([total(wide_ref[t] * adv[side]) for t in range(2)])
         adv_l[c], adv_r[c] = adv
         for t, (main, weight, row, i) in enumerate(
             ((b_ref[c], BACKWARD, PHI, 0), (sum_ref[c, n // 2 - 1] + sum_ref[c, n - 1], FORWARD, PSI, n - 1))
@@ -430,7 +430,7 @@
     low = sublanes(adv_l.shape[2:]) < 4
     for c in range(3):
         for p in range(pairs):
-            l, r = adv_l[c, p], adv_r[c, p]
+            l, r = -adv_l[c, p], -adv_r[c, p]
             first = jnp.where(low, l, pltpu.roll(r, 4, 0))
             second = jnp.where(low, pltpu.roll(l, 4, 0), r)
             for h, value in ((0, first), (1, second)):

time: 39.6 us -> 39.6 us (level)
  no operation moved by 1% of the time
where the time goes in v10:
time: 39.6 us; the launch traced here: 39.4 us
  Pallas kernels  24.4 us (62%)
  starting transfers between devices  9.22 us (23%)
  waiting for transfers between devices  4.69 us (12%)
  between operations  0.82 us (2%)
    pallas_call x1, Pallas kernels, main_part(): pl.pallas_call(functools.partial(main_kernel if both_units else main_plai...  7.95 us
    pallas_call x2, Pallas kernels, sweep_up(): pl.pallas_call(functools.partial(up_kernel, start, count, block, group),...  5.76 us
    pallas_call x1, Pallas kernels, pack(): pl.pallas_call(functools.partial(pack_kernel, group), in_specs=[pl.BlockS...  4.86 us
    ppermute x3, starting transfers between devices, shards(): other = lax.ppermute(whole, 'gy', [(i, i ^ bit) for i in range(ny)])  4.34 us
    pallas_call x1, Pallas kernels, sweep_down(): pl.pallas_call(functools.partial(down_kernel, bit, n, block), in_specs=[v...  3.92 us
    ppermute x1, waiting for transfers between devices, shards(): from_right = lax.ppermute(left, 'gx', [(j, i) for i, j in ring])  3.33 us
    ppermute x1, starting transfers between devices, shards(): from_left = lax.ppermute(right, 'gx', ring)  2.99 us
    ppermute x3, waiting for transfers between devices, shards(): other = lax.ppermute(whole, 'gy', [(i, i ^ bit) for i in range(ny)])  1.35 us
  transfers between devices with their start and end apart: 7, of which 3 were waited for; matrix products, arithmetic and copies ran while one was open for 0% of the time, Pallas kernels for 38%

profile of v10, /device:TPU:0, one launch (start us, length us, event | category | flops | bytes accessed | tf_op | source)
XLA Modules:
  0.0 39.4 jit_solution(17132210549222009355)
XLA Ops:
  0.6 0.0 copy-start
  0.6 0.0 copy-start.1
  0.7 0.0 copy-start.3
  0.7 0.0 copy-start.2
  0.7 0.0 slice-start
  0.7 0.0 slice-start.1
  0.7 4.9 %pack_edges.1 = (f32[3,192,32,128]{3,2,1,0:T(8,128)S(1)}, bf16[3,6144,256]{2,1,0:T(8,128)(2,1)S(1)}, f32[3,12,8,256]{3,2,1,0:T(8,128)S(1)}, f32[3,12,8,256]{3,2,1,0:T(8,128)S(1)}) custom-call(f32[3,192,32,128]{3,2,1,0:T(8,128)} %v_hbm.1), custom_call_target="tpu_custom_call" | custom-call | flops 2359296 | bytes 9437184 | tf_op jit(solution)/shard_map/pack_edges/pallas_call | solution.py:188
  5.6 3.0 %collective-permute-start = (f32[3,12,8,256]{3,2,1,0:T(8,128)S(1)}, f32[3,12,8,256]{3,2,1,0:T(8,128)S(1)}, u32[]{:S(2)}, u32[]{:S(2)}) collective-permute-start(f32[3,12,8,256]{3,2,1,0:T(8,128)S(1)} %get-tuple-element.30.right_ref), channel_id=1, source_target_pairs={{0,8},{8,16},{16,24},{24,0},{1,9},{9,17},{17,25},{25,1},{2,10},{10... | collective-permute-start | bytes 884744 | tf_op jit(solution)/shard_map/ppermute | solution.py:689
  8.6 1.0 %collective-permute-start.1 = (f32[3,12,8,256]{3,2,1,0:T(8,128)S(1)}, f32[3,12,8,256]{3,2,1,0:T(8,128)S(1)}, u32[]{:S(2)}, u32[]{:S(2)}) collective-permute-start(f32[3,12,8,256]{3,2,1,0:T(8,128)S(1)} %get-tuple-element.31.left_ref), channel_id=1, source_target_pairs={{8,0},{16,8},{24,16},{0,24},{9,1},{17,9},{25,17},{1,25},{10,2},{18... | collective-permute-start | bytes 884744 | tf_op jit(solution)/shard_map/ppermute | solution.py:690
  9.6 0.0 copy-done.3
  9.6 0.0 copy-done.2
  9.6 0.0 slice-start.2
  9.6 1.0 %coefficients.1 = (f32[7,192,128]{2,1,0:T(8,128)S(1)}, f32[2,12,8,256]{3,2,1,0:T(8,128)S(1)}, f32[3,1,32,128]{3,2,1,0:T(8,128)S(1)}, f32[3,1,32,128]{3,2,1,0:T(8,128)S(1)}) custom-call(f32[192]{0:T(256)S(1)} %copy-done.2, f32[192]{0:T(256)S(1)} %copy-done.3, f32[3,192,32,128]{3,2,1,0:T(8,128)S(1)} %get-tuple-element.28.vel_ref), custom_call_target="tpu_custom_call" | custom-call | flops 100000 | tf_op jit(solution)/shard_map/coefficients/pallas_call | solution.py:136
  10.6 0.1 collective-permute-start.2
  10.7 0.8 %collective-permute-start.3 = (f32[3,1,32,128]{3,2,1,0:T(8,128)S(1)}, f32[3,1,32,128]{3,2,1,0:T(8,128)S(1)}, u32[]{:S(2)}, u32[]{:S(2)}) collective-permute-start(f32[3,1,32,128]{3,2,1,0:T(8,128)S(1)} %get-tuple-element.37), channel_id=1, source_target_pairs={{1,2},{2,1},{3,4},{4,3},{5,6},{6,5},{9,10},{10,9},{11,12},{12,11},... | collective-permute-start | bytes 147464 | tf_op jit(solution)/shard_map/ppermute | solution.py:693
  11.5 0.0 copy-done
  11.5 0.0 copy-done.1
  11.5 0.0 slice-done
  11.5 0.0 slice-done.1
  11.5 0.2 slice-done.2
  11.8 7.9 %inner_part.1 = (f32[3,192,32,128]{3,2,1,0:T(8,128)S(1)}, f32[3,192,32,128]{3,2,1,0:T(8,128)S(1)}, f32[3,32,128]{2,1,0:T(8,128)S(1)}) custom-call(f32[7,192,128]{2,1,0:T(8,128)S(1)} %get-tuple-element.29.co, f32[3,192,32,128]{3,2,1,0:T(8,128)S(1)} %get-tuple-element.28.vel_ref, bf16[3,6144,256]{2,1,0:T(8,128)(2,1)S(1)} %get-tuple-element.32.pair_ref, ...), custom_call_target="tpu_custom_call" | custom-call | flops 58982400 | bytes 9437184 | tf_op jit(solution)/shard_map/inner_part/pallas_call | solution.py:334
  19.7 0.0 collective-permute-done.2.near_ref
  19.7 0.0 collective-permute-done.3.far_ref
  19.7 0.0 collective-permute-done.from_left
  19.8 3.3 %collective-permute-done.1.from_right = f32[3,12,8,256]{3,2,1,0:T(8,128)S(1)} collective-permute-done((f32[3,12,8,256]{3,2,1,0:T(8,128)S(1)}, f32[3,12,8,256]{3,2,1,0:T(8,128)S(1)}, u32[]{:S(2)}, u32[]{:S(2)}) %collective-permute-start.1) | collective-permute-done | bytes 294944 | tf_op jit(solution)/shard_map/ppermute | solution.py:690
  23.1 0.6 %edge_part.1 = (f32[3,12,8,256]{3,2,1,0:T(8,128)S(1)}, f32[3,12,8,256]{3,2,1,0:T(8,128)S(1)}, f32[2,3,32,128]{3,2,1,0:T(8,128)S(1)}, f32[200,128]{1,0:T(8,128)S(1)}) custom-call(f32[7,192,128]{2,1,0:T(8,128)S(1)} %get-tuple-element.29.co, f32[3,12,8,256]{3,2,1,0:T(8,128)S(1)} %collective-permute-done.from_left, ...), custom_call_target="tpu_custom_call" | custom-call | flops 2949120 | tf_op jit(solution)/shard_map/edge_part/pallas_call | solution.py:417
  23.7 0.0 collective-permute-start.4
  23.7 0.2 extra_part.1.token.extra_ref
  23.9 1.1 %collective-permute-done.4.other_ref = f32[200,128]{1,0:T(8,128)S(1)} collective-permute-done((f32[200,128]{1,0:T(8,128)S(1)}, f32[200,128]{1,0:T(8,128)S(1)}, u32[]{:S(2)}, u32[]{:S(2)}) %collective-permute-start.4) | collective-permute-done | bytes 102432 | tf_op jit(solution)/shard_map/ppermute | solution.py:703
  25.1 1.6 %collective-permute-start.5 = (f32[200,128]{1,0:T(8,128)S(1)}, f32[200,128]{1,0:T(8,128)S(1)}, u32[]{:S(2)}, u32[]{:S(2)}) collective-permute-start(f32[200,128]{1,0:T(8,128)S(1)} %get-tuple-element.41.token.all_ref), channel_id=1, source_target_pairs={{0,2},{1,3},{2,0},{3,1},{4,6},{5,7},{6,4},{7,5},{8,10},{9,11},{10,... | collective-permute-start | bytes 307208 | tf_op jit(solution)/shard_map/ppermute | solution.py:703
  26.7 3.1 %sweep_up.2 = (f32[3,192,32,128]{3,2,1,0:T(8,128)}, f32[3,128,32,128]{3,2,1,0:T(8,128)S(1)}, f32[3,32,128]{2,1,0:T(8,128)S(1)}) custom-call(f32[200,128]{1,0:T(8,128)S(1)} %get-tuple-element.41.token.all_ref, f32[7,192,128]{2,1,0:T(8,128)S(1)} %get-tuple-element.29.co, f32[3,192,32,128]{3,2,1,0:T(8,128)S(1)} %get-tuple-element.42.adv_part, ...), custom_call_target="tpu_custom_call" | custom-call | flops 9437184 | bytes 4718592 | tf_op jit(solution)/shard_map/sweep_up/pallas_call | solution.py:615
  29.8 0.3 collective-permute-done.5.other_ref
  30.1 0.1 join_runs.3
  30.2 2.7 %collective-permute-start.6 = (f32[104,128]{1,0:T(8,128)S(1)}, f32[104,128]{1,0:T(8,128)S(1)}, u32[]{:S(2)}, u32[]{:S(2)}) collective-permute-start(f32[104,128]{1,0:T(8,128)S(1)} %get-tuple-element.47.token), channel_id=1, source_target_pairs={{0,4},{1,5},{2,6},{3,7},{4,0},{5,1},{6,2},{7,3},{8,12},{9,13},{10,... | collective-permute-start | bytes 159752 | tf_op jit(solution)/shard_map/ppermute | solution.py:703
  32.8 2.7 %sweep_up.3 = (f32[3,192,32,128]{3,2,1,0:T(8,128)}, f32[3,64,32,128]{3,2,1,0:T(8,128)S(1)}, f32[3,32,128]{2,1,0:T(8,128)}) custom-call(f32[104,128]{1,0:T(8,128)S(1)} %get-tuple-element.47.token, f32[7,192,128]{2,1,0:T(8,128)S(1)} %get-tuple-element.29.co, f32[3,192,32,128]{3,2,1,0:T(8,128)S(1)} %get-tuple-element.42.adv_part, ...), custom_call_target="tpu_custom_call", output_to_operand_aliasing={{0}: (6, {})} | custom-call | flops 9437184 | bytes 4718592 | tf_op jit(solution)/shard_map/sweep_up/pallas_call | solution.py:615
  35.5 0.0 collective-permute-done.6.other
  35.5 3.9 %sweep_down.1 = f32[3,192,32,128]{3,2,1,0:T(8,128)} custom-call(f32[7,192,128]{2,1,0:T(8,128)S(1)} %get-tuple-element.29.co, f32[200,128]{1,0:T(8,128)S(1)} %get-tuple-element.38.all_ref.load, f32[104,128]{1,0:T(8,128)S(1)} %collective-permute-done.6.other, f32[200,128]{1,0:T(8,128)S(1)} %get-tuple-element.48.lower, f32[200,128]{1,0:T(8,128)S(1)} %get-tuple-element.49.upper, ...), custom_call_target="tpu_custom_call" | custom-call | flops 18874368 | bytes 12582912 | tf_op jit(solution)/shard_map/sweep_down/pallas_call | solution.py:667
  (2 shorter events, 0.1 us)
Async XLA Ops:
  0.6 10.9 %copy-start = (bf16[256,256]{1,0:T(8,128)(2,1)S(1)}, bf16[256,256]{1,0:T(8,128)(2,1)}, u32[]{:S(2)}) copy-start(bf16[256,256]{1,0:T(8,128)(2,1)} %constant.5.clone.dx_ref) | copy-start | bytes 393220
  0.6 10.9 %copy-start.1 = (bf16[128,256]{1,0:T(8,128)(2,1)S(1)}, bf16[128,256]{1,0:T(8,128)(2,1)}, u32[]{:S(2)}) copy-start(bf16[128,256]{1,0:T(8,128)(2,1)} %constant.4.clone.dz_ref) | copy-start | bytes 196612
  0.7 8.9 %copy-start.3 = (f32[192]{0:T(256)S(1)}, f32[192]{0:T(256)}, u32[]{:S(2)}) copy-start(f32[192]{0:T(256)} %upper_ref.1) | copy-start | bytes 2308
  0.7 8.9 %copy-start.2 = (f32[192]{0:T(256)S(1)}, f32[192]{0:T(256)}, u32[]{:S(2)}) copy-start(f32[192]{0:T(256)} %lower_ref.1) | copy-start | bytes 2308
  0.7 10.8 %slice-start = ((s8[9437184]{0:T(1024)(128)(4,1)}), s8[1048576]{0:T(1024)(128)(4,1)S(1)}, s32[]{:S(2)}) async-start(s8[9437184]{0:T(1024)(128)(4,1)} %bitcast), calls=%async_computation | async-start | bytes 2097152
  0.7 10.8 %slice-start.1 = ((s8[9437184]{0:T(1024)(128)(4,1)}), s8[4194304]{0:T(1024)(128)(4,1)S(1)}, s32[]{:S(2)}) async-start(s8[9437184]{0:T(1024)(128)(4,1)} %bitcast), calls=%async_computation.1 | async-start | bytes 8388608
  5.6 14.2 %collective-permute-start = (f32[3,12,8,256]{3,2,1,0:T(8,128)S(1)}, f32[3,12,8,256]{3,2,1,0:T(8,128)S(1)}, u32[]{:S(2)}, u32[]{:S(2)}) collective-permute-start(f32[3,12,8,256]{3,2,1,0:T(8,128)S(1)} %get-tuple-element.30.right_ref), channel_id=1, source_target_pairs={{0,8},{8,16},{16,24},{24,0},{1,9},{9,17},{17,25},{25,1},{2,10},{10... | collective-permute-start | bytes 884744 | tf_op jit(solution)/shard_map/ppermute | solution.py:689
  8.6 14.5 %collective-permute-start.1 = (f32[3,12,8,256]{3,2,1,0:T(8,128)S(1)}, f32[3,12,8,256]{3,2,1,0:T(8,128)S(1)}, u32[]{:S(2)}, u32[]{:S(2)}) collective-permute-start(f32[3,12,8,256]{3,2,1,0:T(8,128)S(1)} %get-tuple-element.31.left_ref), channel_id=1, source_target_pairs={{8,0},{16,8},{24,16},{0,24},{9,1},{17,9},{25,17},{1,25},{10,2},{18... | collective-permute-start | bytes 884744 | tf_op jit(solution)/shard_map/ppermute | solution.py:690
  9.6 2.2 %slice-start.2 = ((s8[9437184]{0:T(1024)(128)(4,1)}), s8[4194304]{0:T(1024)(128)(4,1)S(1)}, s32[]{:S(2)}) async-start(s8[9437184]{0:T(1024)(128)(4,1)} %bitcast), calls=%async_computation.2 | async-start | bytes 8388608
  10.6 9.1 %collective-permute-start.2 = (f32[3,1,32,128]{3,2,1,0:T(8,128)S(1)}, f32[3,1,32,128]{3,2,1,0:T(8,128)S(1)}, u32[]{:S(2)}, u32[]{:S(2)}) collective-permute-start(f32[3,1,32,128]{3,2,1,0:T(8,128)S(1)} %get-tuple-element.36), channel_id=1, source_target_pairs={{0,1},{1,0},{2,3},{3,2},{4,5},{5,4},{6,7},{7,6},{8,9},{9,8},{10,11... | collective-permute-start | bytes 147464 | tf_op jit(solution)/shard_map/ppermute | solution.py:692
  10.7 9.1 %collective-permute-start.3 = (f32[3,1,32,128]{3,2,1,0:T(8,128)S(1)}, f32[3,1,32,128]{3,2,1,0:T(8,128)S(1)}, u32[]{:S(2)}, u32[]{:S(2)}) collective-permute-start(f32[3,1,32,128]{3,2,1,0:T(8,128)S(1)} %get-tuple-element.37), channel_id=1, source_target_pairs={{1,2},{2,1},{3,4},{4,3},{5,6},{6,5},{9,10},{10,9},{11,12},{12,11},... | collective-permute-start | bytes 147464 | tf_op jit(solution)/shard_map/ppermute | solution.py:693
  23.7 1.3 %collective-permute-start.4 = (f32[200,128]{1,0:T(8,128)S(1)}, f32[200,128]{1,0:T(8,128)S(1)}, u32[]{:S(2)}, u32[]{:S(2)}) collective-permute-start(f32[200,128]{1,0:T(8,128)S(1)} %get-tuple-element.38.all_ref.load), channel_id=1, source_target_pairs={{0,1},{1,0},{2,3},{3,2},{4,5},{5,4},{6,7},{7,6},{8,9},{9,8},{10,11... | collective-permute-start | bytes 307208 | tf_op jit(solution)/shard_map/ppermute | solution.py:703
  25.1 5.0 %collective-permute-start.5 = (f32[200,128]{1,0:T(8,128)S(1)}, f32[200,128]{1,0:T(8,128)S(1)}, u32[]{:S(2)}, u32[]{:S(2)}) collective-permute-start(f32[200,128]{1,0:T(8,128)S(1)} %get-tuple-element.41.token.all_ref), channel_id=1, source_target_pairs={{0,2},{1,3},{2,0},{3,1},{4,6},{5,7},{6,4},{7,5},{8,10},{9,11},{10,... | collective-permute-start | bytes 307208 | tf_op jit(solution)/shard_map/ppermute | solution.py:703
  30.2 5.3 %collective-permute-start.6 = (f32[104,128]{1,0:T(8,128)S(1)}, f32[104,128]{1,0:T(8,128)S(1)}, u32[]{:S(2)}, u32[]{:S(2)}) collective-permute-start(f32[104,128]{1,0:T(8,128)S(1)} %get-tuple-element.47.token), channel_id=1, source_target_pairs={{0,4},{1,5},{2,6},{3,7},{4,0},{5,1},{6,2},{7,3},{8,12},{9,13},{10,... | collective-permute-start | bytes 159752 | tf_op jit(solution)/shard_map/ppermute | solution.py:703
